TPU v7x, 32 devices: a whole 2x2x4 slice. The times are simulated.
32 devices in a mesh: src: 4 (over y, x), vox: 8 (over z, core).
Axes of the slice: x: 2, y: 2, z: 4, core: 2. Of those that a mesh axis runs over, the one named last changes fastest.
Arguments:
- kappa: float32 [64, 64, 256], P('vox'), may hold values from 0.3 to 3
- mua: float32 [64, 64, 256], P('vox'), may hold values from 0.1 to 2
- prior_forward_fields: float32 [8, 64, 64, 256], P('src', 'vox'), may hold values from -10 to 10
- prior_adjoint_fields: float32 [8, 64, 64, 256], P('src', 'vox'), may hold values from -10 to 10
- source_position: int32 [8], replicated, may hold values from 0 to 1048575
- detector_voxel: int32 [1024], P('vox'), may hold values from 0 to 1048575, as said below
- measured_source: int32 [32768], P(('src', 'vox')), may hold values from 0 to 7, as said below
- measured_detector: int32 [32768], P(('src', 'vox')), may hold values from 0 to 1023, as said below
- measured_data: float32 [32768], P(('src', 'vox')), may hold values from -6 to 6
- measured_weight: float32 [32768], P(('src', 'vox')), may hold values from 0.25 to 4
Outputs:
- grad_mua: float32 [64, 64, 256], P('vox', 'src')
- grad_kappa: float32 [64, 64, 256], P('vox', 'src')
Inputs may be any that keep to these rules, and one draw needn't show every extreme that they name: `measured_source`: in each aligned block of 1024 rows (the rows of one device), at most 512 rows name a source of one group, a group being the 2 sources s with the same s // 2. `measured_detector`: row r names a detector of detector block (r // 1024) % 8, that is one from that block times 128 up to the next block's first. `detector_voxel`: detector d lies in the voxel planes x from (d // 128) * 8 to that plus 8 - 1.
All inputs are finite; a program needn't handle non-finite values.
Results may differ from a plain program's by a relative error of at most 0.0003.
Values sent between devices are 32-bit elements; how exact they have to be, the bound alone decides.
No kernel may reach another device: no remote copies, remote signals or barrier semaphores. Data moves between devices by JAX's collectives and lax.ppermute only.
A program may use at most 256 MiB of HBM per device.

v0:
```python
import jax
import jax.numpy as jnp
from jax import lax
from jax.sharding import PartitionSpec as P

SWEEPS = 6


source_gain = 10.0


def extended(block, sides, width):
    for axis, dim in sides:
        count = lax.axis_size(axis)
        forward = [(i, i + 1) for i in range(count - 1)]
        backward = [(target, source) for source, target in forward]
        low = lax.ppermute(
            lax.slice_in_dim(block, block.shape[dim] - width, None, axis=dim), axis, forward
        )
        high = lax.ppermute(lax.slice_in_dim(block, 0, width, axis=dim), axis, backward)
        block = jnp.concatenate([low, block, high], axis=dim)
    return block


def from_behind(block, axis, distance):
    devices = range(lax.axis_size(axis))
    route = [(i - distance, i) for i in devices if i - distance in devices]
    return lax.ppermute(block, axis, route)


def conductances(wide_kappa, mid_mua):
    face_x = 0.5 * (wide_kappa[1:] + wide_kappa[:-1])
    middle = wide_kappa[1:-1]
    padded_y = jnp.pad(middle, ((0, 0), (1, 1), (0, 0)))
    face_y = 0.5 * (padded_y[:, 1:] + padded_y[:, :-1])
    padded_z = jnp.pad(middle, ((0, 0), (0, 0), (1, 1)))
    face_z = 0.5 * (padded_z[:, :, 1:] + padded_z[:, :, :-1])
    diagonal = (
        mid_mua
        + face_x[1:]
        + face_x[:-1]
        + face_y[:, 1:]
        + face_y[:, :-1]
        + face_z[:, :, 1:]
        + face_z[:, :, :-1]
    )
    return (face_x, face_y, face_z, diagonal)


def jacobi_sweep(widened, source, face_x, face_y, face_z, diagonal):
    middle = widened[:, 1:-1]
    padded_y = jnp.pad(middle, ((0, 0), (0, 0), (1, 1), (0, 0)))
    padded_z = jnp.pad(middle, ((0, 0), (0, 0), (0, 0), (1, 1)))
    inflow = face_x[1:] * widened[:, 2:] + face_x[:-1] * widened[:, :-2]
    inflow = inflow + face_y[:, 1:] * padded_y[:, :, 2:] + face_y[:, :-1] * padded_y[:, :, :-2]
    inflow = (
        inflow
        + face_z[:, :, 1:] * padded_z[:, :, :, 2:]
        + face_z[:, :, :-1] * padded_z[:, :, :, :-2]
    )
    return (source + inflow) / diagonal


def along(values, axis):
    upper = lax.slice_in_dim(values, 1, values.shape[axis], axis=axis)
    edge = jnp.zeros_like(lax.slice_in_dim(values, 0, 1, axis=axis))
    return jnp.concatenate([upper, edge], axis=axis) - values


def rim_exchange(current):
    return extended(current, (("vox", 1),), 1)


def body(
    kappa,
    mua,
    prior_forward_fields,
    prior_adjoint_fields,
    source_position,
    detector_voxel,
    measured_source,
    measured_detector,
    measured_data,
    measured_weight,
):
    source_count = prior_forward_fields.shape[0]
    depth_x, width_y, width_z = kappa.shape
    plane_size = width_y * width_z
    slab_position_index = lax.axis_index("vox")
    src_index = lax.axis_index("src")
    groups = lax.axis_size("src")
    detector_count = detector_voxel.shape[0]
    det_local = detector_voxel - slab_position_index * depth_x * plane_size
    row_detector = measured_detector - slab_position_index * detector_count
    my_sources = lax.dynamic_slice_in_dim(source_position, src_index * source_count, source_count)
    slot_capacity = measured_source.shape[0] // 2
    owning_group = measured_source // source_count
    onehot = (owning_group[:, None] == jnp.arange(groups)[None, :]).astype(jnp.int32)
    position = jnp.sum(onehot * (jnp.cumsum(onehot, axis=0) - 1), axis=1)
    row_identifier = measured_source % source_count * detector_count + row_detector
    floats = jnp.zeros((groups, 2, slot_capacity), jnp.float32)
    floats = (
        floats.at[owning_group, 0, position]
        .set(measured_weight)
        .at[owning_group, 1, position]
        .set(measured_data)
    )
    row_codes = (
        jnp.full((groups, slot_capacity), -1, jnp.int32)
        .at[owning_group, position]
        .set(row_identifier)
    )
    got_floats, got_codes = (
        lax.all_to_all(floats, "src", split_axis=0, concat_axis=0, tiled=True),
        lax.all_to_all(row_codes, "src", split_axis=0, concat_axis=0, tiled=True),
    )
    wide_kappa, fwd_wide, adj_wide = (
        extended(kappa[None], (("vox", 1),), 1),
        extended(prior_forward_fields, (("vox", 1),), 1),
        extended(prior_adjoint_fields, (("vox", 1),), 1),
    )
    face_x, face_y, face_z, diagonal = conductances(wide_kappa[0], mua)
    column = my_sources // plane_size
    remainder = my_sources % plane_size
    offset = column - slab_position_index * depth_x
    spot_index = jnp.where((offset >= 0) & (offset < depth_x), offset * plane_size + remainder, -1)
    cell_ids = jnp.arange(depth_x * plane_size, dtype=jnp.int32)
    placed = jnp.where(cell_ids[None, :] == spot_index[:, None], source_gain, 0.0).astype(
        jnp.float32
    )
    fwd_source = placed.reshape(source_count, depth_x, width_y, width_z)
    forward = jacobi_sweep(fwd_wide, fwd_source, face_x, face_y, face_z, diagonal)
    for sweep in range(SWEEPS - 1):
        forward = jacobi_sweep(rim_exchange(forward), fwd_source, face_x, face_y, face_z, diagonal)
    predicted_value = jnp.take(forward.reshape(source_count, -1), det_local, axis=1)
    filled = got_codes >= 0
    safe_code = jnp.where(filled, got_codes, 0)
    flat_pred = predicted_value.reshape(-1)
    residual_value = jnp.where(
        filled, got_floats[:, 0] * (flat_pred[safe_code] - got_floats[:, 1]), 0.0
    )
    detector_totals = (
        jnp.zeros((source_count * detector_count,), jnp.float32)
        .at[safe_code.reshape(-1)]
        .add(residual_value.reshape(-1))
    )
    place_detector_totals = detector_totals.reshape(source_count, detector_count)
    offset = detector_voxel // plane_size - slab_position_index * depth_x
    valid = (offset >= 0) & (offset < depth_x)
    flat = jnp.where(valid, offset * plane_size + detector_voxel % plane_size, depth_x * plane_size)
    placed = (
        jnp.zeros((source_count, depth_x * plane_size), jnp.float32)
        .at[:, flat]
        .add(place_detector_totals, mode="drop")
    )
    back_source = placed.reshape(source_count, depth_x, width_y, width_z)
    adjoint = jacobi_sweep(adj_wide, back_source, face_x, face_y, face_z, diagonal)
    for sweep in range(SWEEPS - 1):
        adjoint = jacobi_sweep(rim_exchange(adjoint), back_source, face_x, face_y, face_z, diagonal)
    boundary = from_behind(jnp.stack([forward[:, 0], adjoint[:, 0]]), "vox", -1)
    forward_next = jnp.concatenate([forward[:, 1:], boundary[0][:, None]], axis=1)
    adjoint_next = jnp.concatenate([adjoint[:, 1:], boundary[1][:, None]], axis=1)
    grad_mua = -jnp.sum(forward * adjoint, axis=0)
    product = (forward_next - forward) * (adjoint_next - adjoint)
    product = (
        product + along(forward, 2) * along(adjoint, 2) + along(forward, 3) * along(adjoint, 3)
    )
    grad_kappa = -jnp.sum(product, axis=0)
    tiles = lax.psum_scatter(
        jnp.stack([grad_mua, grad_kappa]), "src", scatter_dimension=2, tiled=True
    )
    return (tiles[0], tiles[1])


def solution(mesh):
    in_specs = (
        P("vox", None, None),
        P("vox", None, None),
        P("src", "vox", None, None),
        P("src", "vox", None, None),
        P(),
        P("vox"),
        P(("src", "vox")),
        P(("src", "vox")),
        P(("src", "vox")),
        P(("src", "vox")),
    )
    out_specs = (P("vox", "src", None), P("vox", "src", None))
    return jax.shard_map(body, mesh=mesh, in_specs=in_specs, out_specs=out_specs, check_vma=False)
```

profile of v0, /device:TPU:10, one launch (start us, length us, event | category | flops | bytes accessed | tf_op | source)
XLA Modules:
  0.0 367.3 jit_solution(17043801174375346992)
XLA Ops:
  13.5 3.2 collective-permute-start.2
  22.5 4.9 %scatter_custom_fusion.2 = s32[2048]{0:T(1024)} fusion(s32[1024]{0:T(1024)S(1)} %broadcast_select_fusion.2, s32[1024]{0:T(1024)S(1)} %get-tuple-element.53, s32[]{:T(128)} %constant.131.clone.1), kind=kCustom, calls=%fused_computation.307 | custom fusion | bytes 8196
  27.3 4.2 %all-to-all-start = ((s32[4,1,512]{2,1,0:T(1,128)}), s32[4,1,512]{2,1,0:T(1,128)S(1)}, u32[]{:S(2)}, u32[]{:S(2)}) async-start(s32[4,1,512]{2,1,0:T(1,128)} %bitcast.7), calls=%async_computation | async-start | bytes 16384 | tf_op jit(solution)/shard_map/all_to_all | solution.py:115
  33.3 3.2 collective-permute-start.14
  46.8 3.6 collective-permute-start.4
  53.0 4.5 %scatter_custom_fusion.3 = f32[4096]{0:T(1024)S(1)} fusion(s32[1024]{0:T(1024)S(1)} %get-tuple-element.55, f32[1024]{0:T(1024)} %param.19, f32[]{:T(128)} %constant.134.clone.1), kind=kCustom, calls=%fused_computation.293 | custom fusion | bytes 16896
  57.5 4.3 %scatter_fusion = f32[4096]{0:T(1024)S(1)} fusion(f32[4096]{0:T(1024)S(1)} %scatter_custom_fusion.3, s32[1024]{0:T(1024)S(1)} %get-tuple-element.54, f32[1024]{0:T(1024)S(1)} %copy-done.17), kind=kCustom, calls=%fused_computation.6 | custom fusion | bytes 16384
  62.4 2.6 sort
  65.6 4.9 %fusion.152 = f32[2,8,64,256]{3,2,1,0:T(8,128)S(1)} fusion(f32[2,8,64,256]{3,2,1,0:T(8,128)} %copy-done.11, f32[2,1,64,256]{3,2,1,0:T(8,128)} %collective-permute-done.5, f32[2,1,64,256]{3,2,1,0:T(8,128)} %collective-permute-done.4, f32[8,64,256]{2,1,0:T(8,128)S(1)} %get-tuple-element.39, f32[8,64,256]{2,1,0:T(8,128)S(1)} %get-tuple-element.40, ...), kind=kLoop, calls=%fused_computation.241 | loop fusion | flops 4456448 | bytes 6553608 | tf_op jit(solution)/shard_map/div | solution.py:61
  71.5 3.6 collective-permute-start.6
  77.1 4.2 %all-to-all-start.1 = ((f32[4,2,512]{2,1,0:T(2,128)}), f32[4,2,512]{2,1,0:T(2,128)}, u32[]{:S(2)}, u32[]{:S(2)}) async-start(f32[4,2,512]{2,1,0:T(2,128)} %reshape.188), calls=%async_computation.1 | async-start | bytes 32768 | tf_op jit(solution)/shard_map/all_to_all | solution.py:114
  82.6 4.9 %fusion.153 = f32[2,8,64,256]{3,2,1,0:T(8,128)S(1)} fusion(f32[2,8,64,256]{3,2,1,0:T(8,128)} %copy-done.12, f32[2,1,64,256]{3,2,1,0:T(8,128)} %collective-permute-done.7, f32[2,1,64,256]{3,2,1,0:T(8,128)} %collective-permute-done.6, f32[8,64,256]{2,1,0:T(8,128)S(1)} %get-tuple-element.39, f32[8,64,256]{2,1,0:T(8,128)S(1)} %get-tuple-element.40, ...), kind=kLoop, calls=%fused_computation.242 | loop fusion | flops 4456448 | bytes 6553608 | tf_op jit(solution)/shard_map/div | solution.py:61
  87.5 3.3 collective-permute-start.8
  93.4 3.8 %collective-permute-done.9 = f32[2,1,64,256]{3,2,1,0:T(8,128)S(1)} collective-permute-done((f32[2,1,64,256]{3,2,1,0:T(8,128)S(1)}, f32[2,1,64,256]{3,2,1,0:T(8,128)S(1)}, u32[]{:S(2)}, u32[]{:S(2)}) %collective-permute-start.9) | collective-permute-done | bytes 131104 | tf_op jit(solution)/shard_map/ppermute | solution.py:17
  100.2 2.7 collective-permute-start.11
  103.4 3.0 collective-permute-done.11
  117.4 5.8 %fusion.156 = f32[2,8,64,256]{3,2,1,0:T(8,128)} fusion(f32[2,8,64,256]{3,2,1,0:T(8,128)} %copy-done.8, f32[2,1,64,256]{3,2,1,0:T(8,128)S(1)} %collective-permute-done.13, f32[2,1,64,256]{3,2,1,0:T(8,128)S(1)} %collective-permute-done.12, f32[8,64,256]{2,1,0:T(8,128)S(1)} %get-tuple-element.39, f32[8,64,256]{2,1,0:T(8,128)S(1)} %get-tuple-element.40, ...), kind=kLoop, calls=%fused_computation.245 | loop fusion | flops 4456448 | bytes 6553608 | tf_op jit(solution)/shard_map/div | solution.py:61
  123.2 33.3 %copy.34 = f32[2,8,64,256]{0,3,2,1:T(8,128)} copy(f32[2,8,64,256]{3,2,1,0:T(8,128)} %fusion.156) | data formatting | bytes 2097152 | tf_op jit(solution)/shard_map/div | solution.py:61
  158.5 13.4 %gather_fusion.1 = f32[2048]{0:T(1024)S(1)} fusion(f32[256]{0:T(256)S(1)} %bitcast.68, s32[2048]{0:T(1024)} %broadcast_clamp_fusion), kind=kCustom, calls=%fused_computation.1 | custom fusion | bytes 24576 | tf_op jit(solution)/shard_map/gather | solution.py:140
  171.9 14.8 %scatter_custom_fusion = f32[256]{0:T(256)S(1)} fusion(s32[2048]{0:T(1024)} %bitcast.84, f32[2048]{0:T(1024)S(1)} %multiply_select_fusion, f32[]{:T(128)} %constant.134.clone.1), kind=kCustom, calls=%fused_computation.332 | custom fusion | flops 2048 | bytes 1536 | tf_op jit(solution)/shard_map/scatter-add | solution.py:145
  186.9 42.4 %scatter_custom_fusion.1 = f32[2,131072]{0,1:T(8,128)} fusion(s32[128]{0:T(128)} %get-tuple-element.2, f32[]{:T(128)} %constant.134.clone.1, f32[128,2]{1,0:T(8,128)S(1)} %copy.36, s32[1024]{0:T(1024)} %pad_clamp_fusion), kind=kCustom, calls=%fused_computation.8 | custom fusion | flops 256 | bytes 1049088 | tf_op jit(solution)/shard_map/scatter-add | solution.py:154
  229.3 39.1 %copy.42 = f32[2,8,64,256]{3,2,1,0:T(8,128)} copy(f32[2,8,64,256]{0,3,2,1:T(8,128)} %bitcast.19) | data formatting | bytes 2097152 | tf_op jit(solution)/shard_map/reshape | solution.py:156
  268.4 5.0 %fusion.45 = f32[2,8,64,256]{3,2,1,0:T(8,128)S(1)} fusion(f32[2,8,64,256]{3,2,1,0:T(8,128)} %copy.42, f32[2,8,64,256]{3,2,1,0:T(8,128)} %param.13, f32[2,1,64,256]{3,2,1,0:T(8,128)} %collective-permute-done.15, f32[2,1,64,256]{3,2,1,0:T(8,128)} %collective-permute-done.14, f32[8,64,256]{2,1,0:T(8,128)S(1)} %get-tuple-element.39, ...), kind=kLoop, calls=%fused_computation.106 | loop fusion | flops 3932160 | bytes 7077888 | tf_op jit(solution)/shard_map/div | solution.py:61
  277.8 3.8 %collective-permute-done.17 = f32[2,1,64,256]{3,2,1,0:T(8,128)S(1)} collective-permute-done((f32[2,1,64,256]{3,2,1,0:T(8,128)S(1)}, f32[2,1,64,256]{3,2,1,0:T(8,128)S(1)}, u32[]{:S(2)}, u32[]{:S(2)}) %collective-permute-start.17) | collective-permute-done | bytes 131104 | tf_op jit(solution)/shard_map/ppermute | solution.py:17
  287.0 3.8 %collective-permute-done.19 = f32[2,1,64,256]{3,2,1,0:T(8,128)S(1)} collective-permute-done((f32[2,1,64,256]{3,2,1,0:T(8,128)S(1)}, f32[2,1,64,256]{3,2,1,0:T(8,128)S(1)}, u32[]{:S(2)}, u32[]{:S(2)}) %collective-permute-start.19) | collective-permute-done | bytes 131104 | tf_op jit(solution)/shard_map/ppermute | solution.py:17
  296.2 3.8 %collective-permute-done.21 = f32[2,1,64,256]{3,2,1,0:T(8,128)S(1)} collective-permute-done((f32[2,1,64,256]{3,2,1,0:T(8,128)S(1)}, f32[2,1,64,256]{3,2,1,0:T(8,128)S(1)}, u32[]{:S(2)}, u32[]{:S(2)}) %collective-permute-start.21) | collective-permute-done | bytes 131104 | tf_op jit(solution)/shard_map/ppermute | solution.py:17
  302.9 2.5 collective-permute-start.23
  305.5 3.9 %collective-permute-done.23 = f32[2,1,64,256]{3,2,1,0:T(8,128)S(1)} collective-permute-done((f32[2,1,64,256]{3,2,1,0:T(8,128)S(1)}, f32[2,1,64,256]{3,2,1,0:T(8,128)S(1)}, u32[]{:S(2)}, u32[]{:S(2)}) %collective-permute-start.23) | collective-permute-done | bytes 131104 | tf_op jit(solution)/shard_map/ppermute | solution.py:17
  314.8 3.8 %collective-permute-done.25 = f32[2,1,64,256]{3,2,1,0:T(8,128)S(1)} collective-permute-done((f32[2,1,64,256]{3,2,1,0:T(8,128)S(1)}, f32[2,1,64,256]{3,2,1,0:T(8,128)S(1)}, u32[]{:S(2)}, u32[]{:S(2)}) %collective-permute-start.25) | collective-permute-done | bytes 131104 | tf_op jit(solution)/shard_map/ppermute | solution.py:17
  322.5 2.9 collective-permute-done.26
  325.4 2.5 multiply_reduce_fusion
  329.2 29.4 %reduce-scatter.2.cloned.1.call-done = f32[2,8,16,256]{3,2,1,0:T(8,128)} async-done(((f32[2,8,64,256]{3,2,1,0:T(8,128)}), f32[2,8,16,256]{3,2,1,0:T(8,128)}) %reduce-scatter.2.cloned.1.call-update) | async-done | bytes 262160 | tf_op jit(solution)/shard_map/reduce_scatter | solution.py:169
  (165 shorter events, 81.1 us)
Async XLA Ops:
  7.2 29.4 %copy-start.10 = (f32[8,64,256]{2,1,0:T(8,128)S(1)}, f32[8,64,256]{2,1,0:T(8,128)}, u32[]{:S(2)}) copy-start(f32[8,64,256]{2,1,0:T(8,128)} %param.10) | copy-start | bytes 1572868
  8.1 31.5 %collective-permute-start = (f32[1,1,64,256]{3,2,1,0:T(8,128)S(1)}, f32[1,1,64,256]{3,2,1,0:T(8,128)S(1)}, u32[]{:S(2)}, u32[]{:S(2)}) collective-permute-start(f32[1,1,64,256]{3,2,1,0:T(8,128)S(1)} %get-tuple-element.46), channel_id=1, source_target_pairs={{1,0},{2,1},{3,2},{4,3},{5,4},{6,5},{7,6},{9,8},{10,9},{11,10},{12... | collective-permute-start | bytes 196616 | tf_op jit(solution)/shard_map/ppermute | solution.py:20
  10.0 31.7 %collective-permute-start.1 = (f32[1,1,64,256]{3,2,1,0:T(8,128)S(1)}, f32[1,1,64,256]{3,2,1,0:T(8,128)S(1)}, u32[]{:S(2)}, u32[]{:S(2)}) collective-permute-start(f32[1,1,64,256]{3,2,1,0:T(8,128)S(1)} %get-tuple-element.45), channel_id=1, source_target_pairs={{0,1},{1,2},{2,3},{3,4},{4,5},{5,6},{6,7},{8,9},{9,10},{10,11},{11... | collective-permute-start | bytes 196616 | tf_op jit(solution)/shard_map/ppermute | solution.py:17
  13.5 29.9 %collective-permute-start.2 = (f32[2,1,64,256]{3,2,1,0:T(8,128)S(1)}, f32[2,1,64,256]{3,2,1,0:T(8,128)}, u32[]{:S(2)}, u32[]{:S(2)}) collective-permute-start(f32[2,1,64,256]{3,2,1,0:T(8,128)S(1)} %get-tuple-element.36), channel_id=1, source_target_pairs={{1,0},{2,1},{3,2},{4,3},{5,4},{6,5},{7,6},{9,8},{10,9},{11,10},{12... | collective-permute-start | bytes 393224 | tf_op jit(solution)/shard_map/ppermute | solution.py:20
  16.6 26.7 %collective-permute-start.3 = (f32[2,1,64,256]{3,2,1,0:T(8,128)S(1)}, f32[2,1,64,256]{3,2,1,0:T(8,128)}, u32[]{:S(2)}, u32[]{:S(2)}) collective-permute-start(f32[2,1,64,256]{3,2,1,0:T(8,128)S(1)} %get-tuple-element.37), channel_id=1, source_target_pairs={{0,1},{1,2},{2,3},{3,4},{4,5},{5,6},{6,7},{8,9},{9,10},{10,11},{11... | collective-permute-start | bytes 393224 | tf_op jit(solution)/shard_map/ppermute | solution.py:17
  27.3 49.8 %all-to-all-start = ((s32[4,1,512]{2,1,0:T(1,128)}), s32[4,1,512]{2,1,0:T(1,128)S(1)}, u32[]{:S(2)}, u32[]{:S(2)}) async-start(s32[4,1,512]{2,1,0:T(1,128)} %bitcast.7), calls=%async_computation | async-start | bytes 16384 | tf_op jit(solution)/shard_map/all_to_all | solution.py:115
  33.3 235.1 %collective-permute-start.14 = (f32[2,1,64,256]{3,2,1,0:T(8,128)}, f32[2,1,64,256]{3,2,1,0:T(8,128)}, u32[]{:S(2)}, u32[]{:S(2)}) collective-permute-start(f32[2,1,64,256]{3,2,1,0:T(8,128)} %get-tuple-element.24), channel_id=1, source_target_pairs={{1,0},{2,1},{3,2},{4,3},{5,4},{6,5},{7,6},{9,8},{10,9},{11,10},{12... | collective-permute-start | bytes 393224 | tf_op jit(solution)/shard_map/ppermute | solution.py:20
  39.7 228.7 %collective-permute-start.15 = (f32[2,1,64,256]{3,2,1,0:T(8,128)}, f32[2,1,64,256]{3,2,1,0:T(8,128)}, u32[]{:S(2)}, u32[]{:S(2)}) collective-permute-start(f32[2,1,64,256]{3,2,1,0:T(8,128)} %get-tuple-element.25), channel_id=1, source_target_pairs={{0,1},{1,2},{2,3},{3,4},{4,5},{5,6},{6,7},{8,9},{9,10},{10,11},{11... | collective-permute-start | bytes 393224 | tf_op jit(solution)/shard_map/ppermute | solution.py:17
  46.8 18.8 %collective-permute-start.4 = (f32[2,1,64,256]{3,2,1,0:T(8,128)S(1)}, f32[2,1,64,256]{3,2,1,0:T(8,128)}, u32[]{:S(2)}, u32[]{:S(2)}) collective-permute-start(f32[2,1,64,256]{3,2,1,0:T(8,128)S(1)} %get-tuple-element.34), channel_id=1, source_target_pairs={{1,0},{2,1},{3,2},{4,3},{5,4},{6,5},{7,6},{9,8},{10,9},{11,10},{12... | collective-permute-start | bytes 393224 | tf_op jit(solution)/shard_map/ppermute | solution.py:20
  50.4 15.2 %collective-permute-start.5 = (f32[2,1,64,256]{3,2,1,0:T(8,128)S(1)}, f32[2,1,64,256]{3,2,1,0:T(8,128)}, u32[]{:S(2)}, u32[]{:S(2)}) collective-permute-start(f32[2,1,64,256]{3,2,1,0:T(8,128)S(1)} %get-tuple-element.35), channel_id=1, source_target_pairs={{0,1},{1,2},{2,3},{3,4},{4,5},{5,6},{6,7},{8,9},{9,10},{10,11},{11... | collective-permute-start | bytes 393224 | tf_op jit(solution)/shard_map/ppermute | solution.py:17
  71.5 11.0 %collective-permute-start.6 = (f32[2,1,64,256]{3,2,1,0:T(8,128)S(1)}, f32[2,1,64,256]{3,2,1,0:T(8,128)}, u32[]{:S(2)}, u32[]{:S(2)}) collective-permute-start(f32[2,1,64,256]{3,2,1,0:T(8,128)S(1)} %get-tuple-element.32), channel_id=1, source_target_pairs={{1,0},{2,1},{3,2},{4,3},{5,4},{6,5},{7,6},{9,8},{10,9},{11,10},{12... | collective-permute-start | bytes 393224 | tf_op jit(solution)/shard_map/ppermute | solution.py:20
  75.2 7.4 %collective-permute-start.7 = (f32[2,1,64,256]{3,2,1,0:T(8,128)S(1)}, f32[2,1,64,256]{3,2,1,0:T(8,128)}, u32[]{:S(2)}, u32[]{:S(2)}) collective-permute-start(f32[2,1,64,256]{3,2,1,0:T(8,128)S(1)} %get-tuple-element.33), channel_id=1, source_target_pairs={{0,1},{1,2},{2,3},{3,4},{4,5},{5,6},{6,7},{8,9},{9,10},{10,11},{11... | collective-permute-start | bytes 393224 | tf_op jit(solution)/shard_map/ppermute | solution.py:17
  77.1 36.4 %all-to-all-start.1 = ((f32[4,2,512]{2,1,0:T(2,128)}), f32[4,2,512]{2,1,0:T(2,128)}, u32[]{:S(2)}, u32[]{:S(2)}) async-start(f32[4,2,512]{2,1,0:T(2,128)} %reshape.188), calls=%async_computation.1 | async-start | bytes 32768 | tf_op jit(solution)/shard_map/all_to_all | solution.py:114
  81.3 277.3 %reduce-scatter.2.cloned.1.call-start = ((), (), s32[]{:S(2)}) async-start(), calls=%async_computation.3 | async-start | bytes 1310720 | tf_op jit(solution)/shard_map/reduce_scatter | solution.py:169
  87.5 5.8 %collective-permute-start.8 = (f32[2,1,64,256]{3,2,1,0:T(8,128)S(1)}, f32[2,1,64,256]{3,2,1,0:T(8,128)S(1)}, u32[]{:S(2)}, u32[]{:S(2)}) collective-permute-start(f32[2,1,64,256]{3,2,1,0:T(8,128)S(1)} %get-tuple-element.30), channel_id=1, source_target_pairs={{1,0},{2,1},{3,2},{4,3},{5,4},{6,5},{7,6},{9,8},{10,9},{11,10},{12... | collective-permute-start | bytes 393224 | tf_op jit(solution)/shard_map/ppermute | solution.py:20
  90.9 6.3 %collective-permute-start.9 = (f32[2,1,64,256]{3,2,1,0:T(8,128)S(1)}, f32[2,1,64,256]{3,2,1,0:T(8,128)S(1)}, u32[]{:S(2)}, u32[]{:S(2)}) collective-permute-start(f32[2,1,64,256]{3,2,1,0:T(8,128)S(1)} %get-tuple-element.31), channel_id=1, source_target_pairs={{0,1},{1,2},{2,3},{3,4},{4,5},{5,6},{6,7},{8,9},{9,10},{10,11},{11... | collective-permute-start | bytes 393224 | tf_op jit(solution)/shard_map/ppermute | solution.py:17
  98.2 5.2 %collective-permute-start.10 = (f32[2,1,64,256]{3,2,1,0:T(8,128)S(1)}, f32[2,1,64,256]{3,2,1,0:T(8,128)S(1)}, u32[]{:S(2)}, u32[]{:S(2)}) collective-permute-start(f32[2,1,64,256]{3,2,1,0:T(8,128)S(1)} %get-tuple-element.28), channel_id=1, source_target_pairs={{1,0},{2,1},{3,2},{4,3},{5,4},{6,5},{7,6},{9,8},{10,9},{11,10},{12... | collective-permute-start | bytes 393224 | tf_op jit(solution)/shard_map/ppermute | solution.py:20
  100.2 6.3 %collective-permute-start.11 = (f32[2,1,64,256]{3,2,1,0:T(8,128)S(1)}, f32[2,1,64,256]{3,2,1,0:T(8,128)S(1)}, u32[]{:S(2)}, u32[]{:S(2)}) collective-permute-start(f32[2,1,64,256]{3,2,1,0:T(8,128)S(1)} %get-tuple-element.29), channel_id=1, source_target_pairs={{0,1},{1,2},{2,3},{3,4},{4,5},{5,6},{6,7},{8,9},{9,10},{10,11},{11... | collective-permute-start | bytes 393224 | tf_op jit(solution)/shard_map/ppermute | solution.py:17
  109.2 5.7 %collective-permute-start.12 = (f32[2,1,64,256]{3,2,1,0:T(8,128)}, f32[2,1,64,256]{3,2,1,0:T(8,128)S(1)}, u32[]{:S(2)}, u32[]{:S(2)}) collective-permute-start(f32[2,1,64,256]{3,2,1,0:T(8,128)} %get-tuple-element.26), channel_id=1, source_target_pairs={{1,0},{2,1},{3,2},{4,3},{5,4},{6,5},{7,6},{9,8},{10,9},{11,10},{12... | collective-permute-start | bytes 393224 | tf_op jit(solution)/shard_map/ppermute | solution.py:20
  111.1 6.3 %collective-permute-start.13 = (f32[2,1,64,256]{3,2,1,0:T(8,128)S(1)}, f32[2,1,64,256]{3,2,1,0:T(8,128)S(1)}, u32[]{:S(2)}, u32[]{:S(2)}) collective-permute-start(f32[2,1,64,256]{3,2,1,0:T(8,128)S(1)} %get-tuple-element.27), channel_id=1, source_target_pairs={{0,1},{1,2},{2,3},{3,4},{4,5},{5,6},{6,7},{8,9},{9,10},{10,11},{11... | collective-permute-start | bytes 393224 | tf_op jit(solution)/shard_map/ppermute | solution.py:17
  123.2 35.1 %copy-start.18 = (pred[128]{0:T(512)(128)(4,1)S(1)}, pred[128]{0:T(512)(128)(4,1)}, u32[]{:S(2)}) copy-start(pred[128]{0:T(512)(128)(4,1)} %get-tuple-element.10) | copy-start | bytes 388
  273.4 4.4 %collective-permute-start.16 = (f32[2,1,64,256]{3,2,1,0:T(8,128)S(1)}, f32[2,1,64,256]{3,2,1,0:T(8,128)S(1)}, u32[]{:S(2)}, u32[]{:S(2)}) collective-permute-start(f32[2,1,64,256]{3,2,1,0:T(8,128)S(1)} %get-tuple-element.22), channel_id=1, source_target_pairs={{1,0},{2,1},{3,2},{4,3},{5,4},{6,5},{7,6},{9,8},{10,9},{11,10},{12... | collective-permute-start | bytes 393224 | tf_op jit(solution)/shard_map/ppermute | solution.py:20
  275.3 6.3 %collective-permute-start.17 = (f32[2,1,64,256]{3,2,1,0:T(8,128)S(1)}, f32[2,1,64,256]{3,2,1,0:T(8,128)S(1)}, u32[]{:S(2)}, u32[]{:S(2)}) collective-permute-start(f32[2,1,64,256]{3,2,1,0:T(8,128)S(1)} %get-tuple-element.23), channel_id=1, source_target_pairs={{0,1},{1,2},{2,3},{3,4},{4,5},{5,6},{6,7},{8,9},{9,10},{10,11},{11... | collective-permute-start | bytes 393224 | tf_op jit(solution)/shard_map/ppermute | solution.py:17
  282.6 4.4 %collective-permute-start.18 = (f32[2,1,64,256]{3,2,1,0:T(8,128)S(1)}, f32[2,1,64,256]{3,2,1,0:T(8,128)S(1)}, u32[]{:S(2)}, u32[]{:S(2)}) collective-permute-start(f32[2,1,64,256]{3,2,1,0:T(8,128)S(1)} %get-tuple-element.20), channel_id=1, source_target_pairs={{1,0},{2,1},{3,2},{4,3},{5,4},{6,5},{7,6},{9,8},{10,9},{11,10},{12... | collective-permute-start | bytes 393224 | tf_op jit(solution)/shard_map/ppermute | solution.py:20
  284.5 6.3 %collective-permute-start.19 = (f32[2,1,64,256]{3,2,1,0:T(8,128)S(1)}, f32[2,1,64,256]{3,2,1,0:T(8,128)S(1)}, u32[]{:S(2)}, u32[]{:S(2)}) collective-permute-start(f32[2,1,64,256]{3,2,1,0:T(8,128)S(1)} %get-tuple-element.21), channel_id=1, source_target_pairs={{0,1},{1,2},{2,3},{3,4},{4,5},{5,6},{6,7},{8,9},{9,10},{10,11},{11... | collective-permute-start | bytes 393224 | tf_op jit(solution)/shard_map/ppermute | solution.py:17
  291.8 4.4 %collective-permute-start.20 = (f32[2,1,64,256]{3,2,1,0:T(8,128)S(1)}, f32[2,1,64,256]{3,2,1,0:T(8,128)S(1)}, u32[]{:S(2)}, u32[]{:S(2)}) collective-permute-start(f32[2,1,64,256]{3,2,1,0:T(8,128)S(1)} %get-tuple-element.18), channel_id=1, source_target_pairs={{1,0},{2,1},{3,2},{4,3},{5,4},{6,5},{7,6},{9,8},{10,9},{11,10},{12... | collective-permute-start | bytes 393224 | tf_op jit(solution)/shard_map/ppermute | solution.py:20
  293.7 6.3 %collective-permute-start.21 = (f32[2,1,64,256]{3,2,1,0:T(8,128)S(1)}, f32[2,1,64,256]{3,2,1,0:T(8,128)S(1)}, u32[]{:S(2)}, u32[]{:S(2)}) collective-permute-start(f32[2,1,64,256]{3,2,1,0:T(8,128)S(1)} %get-tuple-element.19), channel_id=1, source_target_pairs={{0,1},{1,2},{2,3},{3,4},{4,5},{5,6},{6,7},{8,9},{9,10},{10,11},{11... | collective-permute-start | bytes 393224 | tf_op jit(solution)/shard_map/ppermute | solution.py:17
  301.0 4.5 %collective-permute-start.22 = (f32[2,1,64,256]{3,2,1,0:T(8,128)S(1)}, f32[2,1,64,256]{3,2,1,0:T(8,128)S(1)}, u32[]{:S(2)}, u32[]{:S(2)}) collective-permute-start(f32[2,1,64,256]{3,2,1,0:T(8,128)S(1)} %get-tuple-element.16), channel_id=1, source_target_pairs={{1,0},{2,1},{3,2},{4,3},{5,4},{6,5},{7,6},{9,8},{10,9},{11,10},{12... | collective-permute-start | bytes 393224 | tf_op jit(solution)/shard_map/ppermute | solution.py:20
  302.9 6.4 %collective-permute-start.23 = (f32[2,1,64,256]{3,2,1,0:T(8,128)S(1)}, f32[2,1,64,256]{3,2,1,0:T(8,128)S(1)}, u32[]{:S(2)}, u32[]{:S(2)}) collective-permute-start(f32[2,1,64,256]{3,2,1,0:T(8,128)S(1)} %get-tuple-element.17), channel_id=1, source_target_pairs={{0,1},{1,2},{2,3},{3,4},{4,5},{5,6},{6,7},{8,9},{9,10},{10,11},{11... | collective-permute-start | bytes 393224 | tf_op jit(solution)/shard_map/ppermute | solution.py:17
  310.3 4.4 %collective-permute-start.24 = (f32[2,1,64,256]{3,2,1,0:T(8,128)S(1)}, f32[2,1,64,256]{3,2,1,0:T(8,128)S(1)}, u32[]{:S(2)}, u32[]{:S(2)}) collective-permute-start(f32[2,1,64,256]{3,2,1,0:T(8,128)S(1)} %get-tuple-element.14), channel_id=1, source_target_pairs={{1,0},{2,1},{3,2},{4,3},{5,4},{6,5},{7,6},{9,8},{10,9},{11,10},{12... | collective-permute-start | bytes 393224 | tf_op jit(solution)/shard_map/ppermute | solution.py:20
  312.3 6.3 %collective-permute-start.25 = (f32[2,1,64,256]{3,2,1,0:T(8,128)S(1)}, f32[2,1,64,256]{3,2,1,0:T(8,128)S(1)}, u32[]{:S(2)}, u32[]{:S(2)}) collective-permute-start(f32[2,1,64,256]{3,2,1,0:T(8,128)S(1)} %get-tuple-element.15), channel_id=1, source_target_pairs={{0,1},{1,2},{2,3},{3,4},{4,5},{5,6},{6,7},{8,9},{9,10},{10,11},{11... | collective-permute-start | bytes 393224 | tf_op jit(solution)/shard_map/ppermute | solution.py:17
  319.6 5.8 %collective-permute-start.26 = (f32[2,2,64,256]{3,2,1,0:T(8,128)S(1)}, f32[2,2,64,256]{3,2,1,0:T(8,128)S(1)}, u32[]{:S(2)}, u32[]{:S(2)}) collective-permute-start(f32[2,2,64,256]{3,2,1,0:T(8,128)S(1)} %pad_maximum_fusion.25), channel_id=1, source_target_pairs={{1,0},{2,1},{3,2},{4,3},{5,4},{6,5},{7,6},{9,8},{10,9},{11,10},{12... | collective-permute-start | bytes 786440 | tf_op jit(solution)/shard_map/ppermute | solution.py:28
  (22 other events, 155.7 us)
Sparse Core Ops, SparseCore 0:
  329.3 29.2 reduce-scatter.1
where the time goes:
time: 375 us; the launch traced here: 367 us
  local copies, waits for them, and re-layouts  115 us (31%)
  other arithmetic  104 us (28%)
  starting transfers between devices  72.1 us (19%)
  waiting for transfers between devices  61.5 us (16%)
  between operations  15.1 us (4%)
    scatter-add x3, other arithmetic, body(): placed = jnp.zeros((source_count, depth_x * plane_size), jnp.float32).at[...  45.6 us
    reshape x1, local copies, waits for them, and re-layouts, body(): back_source = placed.reshape(source_count, depth_x, width_y, width_z)  39.1 us
    div x1, local copies, waits for them, and re-layouts, jacobi_sweep(): return (source + inflow) / diagonal  33.3 us
    ppermute x13, starting transfers between devices, extended(): lax.ppermute(lax.slice_in_dim(block, 0, width, axis=dim), axis, backward)  32.3 us
    reduce_scatter x1, waiting for transfers between devices, body(): lax.psum_scatter(jnp.stack([grad_mua, grad_kappa]), 'src', scatter_dimens...  29.4 us
    div x12, other arithmetic, jacobi_sweep(): return (source + inflow) / diagonal  29.4 us
    ppermute x13, starting transfers between devices, extended(): lax.ppermute(lax.slice_in_dim(block, block.shape[dim] - width, None, axis...  29.4 us
    ppermute x13, waiting for transfers between devices, extended(): lax.ppermute(lax.slice_in_dim(block, block.shape[dim] - width, None, axis...  28.3 us
  transfers between devices with their start and end apart: 30, of which 15 were waited for; matrix products, arithmetic and copies ran while one was open for 54% of the time, Pallas kernels for 0%

commit v1 on v0

v1 whole, which is shorter than its diff:
```python
import functools

import jax
import jax.numpy as jnp
from jax import lax
from jax.experimental import pallas as pl
from jax.experimental.pallas import tpu as pltpu
from jax.sharding import PartitionSpec as P

SWEEPS = 6
HALO = SWEEPS + 1
LANES = 128
SUB = 8

source_gain = 10.0


def gather_planes(src, src_first, dst, dst_first, count):
    groups, chunks = src.shape[-2] // SUB, src.shape[-1] // LANES

    def step(i, carry):
        for y in range(0, groups * SUB, SUB):
            for j in range(chunks):
                part = src[src_first + i, pl.ds(y, SUB), pl.ds(LANES * j, LANES)]
                if groups == SUB:
                    dst[dst_first + i, j, pl.ds(y // SUB, SUB, stride=SUB), :] = part
                else:
                    for k in range(SUB):
                        row = (y + k) % groups * SUB + (y + k) // groups
                        dst[dst_first + i, j, pl.ds(row, 1), :] = part[k : k + 1]
        return carry

    lax.fori_loop(0, count, step, 0)


def lane_ids():
    return lax.broadcasted_iota(jnp.int32, (SUB, LANES), 1)


def sub_ids():
    return lax.broadcasted_iota(jnp.int32, (SUB, LANES), 0)


def next_z(chunks, lane):
    turned = [pltpu.roll(c, LANES - 1, 1) for c in chunks]
    return [jnp.where(lane == LANES - 1, turned[i + 1], turned[i]) if i + 1 < len(chunks) else turned[i] for i in range(len(chunks))]


def prev_z(chunks, lane):
    turned = [pltpu.roll(c, 1, 1) for c in chunks]
    return [jnp.where(lane == 0, turned[i - 1], turned[i]) if i > 0 else turned[i] for i in range(len(chunks))]


def load_rows(ref, lead, g, chunks):
    return [ref[(*lead, j, pl.ds(SUB * g, SUB), slice(None))] for j in range(chunks)]


def store_rows(ref, lead, g, values):
    for j, value in enumerate(values):
        ref[(*lead, j, pl.ds(SUB * g, SUB), slice(None))] = value


def coefficient_kernel(grid_planes, meta, kappa, mua, near, far, out, kap, mu):
    depth, width_y, width_z = kappa.shape
    groups, chunks = width_y // SUB, width_z // LANES
    lane, sub = lane_ids(), sub_ids()
    slab, parity = meta[0], meta[1]
    near_at = jnp.where(parity == 0, HALO + depth, 0)
    far_at = HALO + depth - near_at
    gather_planes(kappa, 0, kap, HALO, depth)
    gather_planes(near, 0, kap, near_at, HALO)
    gather_planes(far, 0, kap, far_at, HALO)
    mu_near = jnp.where(parity == 0, SWEEPS + depth, 0)
    mu_far = SWEEPS + depth - mu_near
    gather_planes(mua, 0, mu, SWEEPS, depth)
    gather_planes(near, HALO, mu, mu_near, SWEEPS)
    gather_planes(far, HALO, mu, mu_far, SWEEPS)

    def plane(i, carry):
        at = i + HALO - (SWEEPS - 1)
        place = slab * depth + i - (SWEEPS - 1)
        inside = jnp.logical_and(place >= 0, place < grid_planes)
        rows = [load_rows(kap, (at,), g, chunks) for g in range(groups)]
        for g in range(groups):
            mid = rows[g]
            low = load_rows(kap, (at - 1,), g, chunks)
            high = load_rows(kap, (at + 1,), g, chunks)
            if g > 0:
                before = rows[g - 1]
            else:
                before = [jnp.where(sub == 0, 0.0, pltpu.roll(c, 1, 0)) for c in rows[-1]]
            if g + 1 < groups:
                after = rows[g + 1]
            else:
                after = [jnp.where(sub == SUB - 1, 0.0, pltpu.roll(c, SUB - 1, 0)) for c in rows[0]]
            left = prev_z(mid, lane)
            left[0] = jnp.where(lane == 0, 0.0, left[0])
            right = next_z(mid, lane)
            right[-1] = jnp.where(lane == LANES - 1, 0.0, right[-1])
            absorb = load_rows(mu, (i + SWEEPS - (SWEEPS - 1),), g, chunks)
            for j in range(chunks):
                face = [0.5 * (mid[j] + other[j]) for other in (low, high, before, after, left, right)]
                diagonal = absorb[j] + face[0] + face[1] + face[2] + face[3] + face[4] + face[5]
                inverse = jnp.where(inside, 1.0 / diagonal, 0.0)
                if g == 0:
                    face[2] = jnp.where(sub == 0, 0.0, face[2])
                if g + 1 == groups:
                    face[3] = jnp.where(sub == SUB - 1, 0.0, face[3])
                if j == 0:
                    face[4] = jnp.where(lane == 0, 0.0, face[4])
                if j + 1 == chunks:
                    face[5] = jnp.where(lane == LANES - 1, 0.0, face[5])
                for k in range(6):
                    out[k, i, j, pl.ds(SUB * g, SUB), :] = face[k] * inverse
                out[6, i, j, pl.ds(SUB * g, SUB), :] = inverse
        return carry

    lax.fori_loop(0, depth + 2 * SWEEPS - 1, plane, 0)


def sweep_planes(coef, src, dst, first, last, bias):
    count, unused, chunks, width_y, lanes = src.shape
    groups = width_y // SUB
    lane = lane_ids()

    def plane(at, carry):
        c_at = at - (HALO - SWEEPS + 1)
        mids = [[load_rows(src, (s, at), g, chunks) for g in range(groups)] for s in range(count)]
        for g in range(groups):
            faces = [load_rows(coef, (k, c_at), g, chunks) for k in range(6)]
            for s in range(count):
                mid = mids[s][g]
                low = load_rows(src, (s, at - 1), g, chunks)
                high = load_rows(src, (s, at + 1), g, chunks)
                before = mids[s][g - 1] if g > 0 else [pltpu.roll(c, 1, 0) for c in mids[s][-1]]
                after = mids[s][g + 1] if g + 1 < groups else [pltpu.roll(c, SUB - 1, 0) for c in mids[s][0]]
                left, right = prev_z(mid, lane), next_z(mid, lane)
                result = []
                for j in range(chunks):
                    total = faces[0][j] * low[j] + faces[1][j] * high[j]
                    total = total + (faces[2][j] * before[j] + faces[3][j] * after[j])
                    total = total + (faces[4][j] * left[j] + faces[5][j] * right[j])
                    result.append(total)
                if bias is not None:
                    extra = load_rows(bias, (s, c_at), g, chunks)
                    result = [a + b for a, b in zip(result, extra)]
                store_rows(dst, (s, at), g, result)
        return carry

    lax.fori_loop(first + HALO, last + HALO + 1, plane, 0)


def detector_masks(cells, first, planes, width_y, width_z):
    groups = width_y // SUB
    y = cells // width_z % width_y
    row = (cells // (width_y * width_z) - first) * width_y + y % groups * SUB + y // groups
    row_at = lax.broadcasted_iota(jnp.int32, (planes * width_y, cells.shape[1]), 0)
    z_at = lax.broadcasted_iota(jnp.int32, (width_z, cells.shape[1]), 0)
    return row_at == row, z_at == cells % width_z


def split(values):
    high = values.astype(jnp.bfloat16)
    rest = values - high.astype(jnp.float32)
    middle = rest.astype(jnp.bfloat16)
    low = (rest - middle.astype(jnp.float32)).astype(jnp.bfloat16)
    return high, middle, low


def load_fields(meta, own, near, far, field):
    count, depth = own.shape[:2]
    near_at = jnp.where(meta[1] == 0, HALO + depth, 0)
    far_at = HALO + depth - near_at
    for s in range(count):
        gather_planes(own.at[s], 0, field.at[s], HALO, depth)
        gather_planes(near.at[s], 0, field.at[s], near_at, HALO)
        gather_planes(far.at[s], 0, field.at[s], far_at, HALO)


def forward_kernel(meta, coef, own, near, far, cells, totals, forward, adjoint_source, one, two):
    count, depth, width_y, width_z = own.shape
    groups = width_y // SUB
    slab = meta[0]
    load_fields(meta, own, near, far, one)
    src, dst = one, two
    for t in range(SWEEPS):
        reach = SWEEPS - 1 - t
        sweep_planes(coef, src, dst, -reach, depth + reach, None)
        for s in range(count):
            spot = meta[2 + s]
            p = spot // (width_y * width_z) - slab * depth
            y, z = spot // width_z % width_y, spot % width_z

            @pl.when(jnp.logical_and(p >= -reach, p <= depth + reach))
            def _():
                row = y % groups * SUB + y // groups
                tile = pl.multiple_of(row // SUB * SUB, SUB)
                at = (z // LANES, pl.ds(tile, SUB), slice(None))
                inverse = coef[(6, p + SWEEPS - 1, *at)]
                hit = jnp.logical_and(sub_ids() == row - tile, lane_ids() == z % LANES)
                old = dst[(s, p + HALO, *at)]
                dst[(s, p + HALO, *at)] = old + jnp.where(hit, source_gain * inverse, 0.0)

        src, dst = dst, src
    for s in range(count):
        forward[s] = src[s, pl.ds(HALO, depth + 1)]
    row_mask, z_mask = detector_masks(cells[...], 0, depth, width_y, width_z)
    z_hot = z_mask.astype(jnp.bfloat16)
    for s in range(count):
        sampled = 0.0
        for j in range(width_z // LANES):
            field = src[s, pl.ds(HALO, depth), j].reshape(depth * width_y, LANES)
            for part in split(field):
                sampled = sampled + jnp.dot(part, z_hot[LANES * j : LANES * (j + 1)], preferred_element_type=jnp.float32)
        predicted = jnp.sum(jnp.where(row_mask, sampled, 0.0), axis=0, keepdims=True)
        adjoint_source[pl.ds(s, 1), :] = predicted * totals[pl.ds(s, 1), :] - totals[pl.ds(count + s, 1), :]


def adjoint_kernel(
    meta, coef, own, near, far, forward, cells, source, near_cells, near_source, far_cells, far_source, grad_mua, grad_kappa, one, two, bias, plane_out
):
    count, depth, width_y, width_z = own.shape
    groups, chunks = width_y // SUB, width_z // LANES
    parity = meta[1]
    load_fields(meta, own, near, far, one)
    reach = SWEEPS - 1
    near_at = jnp.where(parity == 0, reach + depth, 0)
    far_at = jnp.where(parity == 0, 0, reach + depth)

    def add_sources(cell_ref, source_ref, at, planes, relative):
        row_mask, z_mask = detector_masks(cell_ref[...] + relative * (width_y * width_z), at, planes, width_y, width_z)
        z_hot = z_mask.astype(jnp.bfloat16)
        for s in range(count):
            spreads = [jnp.where(row_mask, part.astype(jnp.float32), 0.0).astype(jnp.bfloat16) for part in split(source_ref[pl.ds(s, 1), :])]
            for j in range(chunks):
                placed = 0.0
                for spread in spreads:
                    z_part = z_hot[LANES * j : LANES * (j + 1)]
                    placed = placed + lax.dot_general(spread, z_part, (((1,), (1,)), ((), ())), preferred_element_type=jnp.float32)
                placed = placed.reshape(planes, width_y, LANES)
                bias[s, pl.ds(at, planes), j] = placed * coef[6, pl.ds(at, planes), j]

    shift = jnp.where(parity == 0, depth, -depth)
    add_sources(near_cells, near_source, near_at, reach + 1, reach + shift)
    add_sources(far_cells, far_source, far_at, reach + 1, reach - shift)
    add_sources(cells, source, reach, depth, reach)
    src, dst = one, two
    for t in range(SWEEPS):
        reach = SWEEPS - 1 - t
        sweep_planes(coef, src, dst, -reach, depth + reach, bias)
        src, dst = dst, src
    lane, sub = lane_ids(), sub_ids()

    def steps(ref, s, at, mids, g):
        mid = mids[g]
        high = load_rows(ref, (s, at + 1), g, chunks)
        if g + 1 < groups:
            after = mids[g + 1]
        else:
            after = [jnp.where(sub == SUB - 1, 0.0, pltpu.roll(c, SUB - 1, 0)) for c in mids[0]]
        right = next_z(mid, lane)
        right[-1] = jnp.where(lane == LANES - 1, 0.0, right[-1])
        return [[other[j] - mid[j] for j in range(chunks)] for other in (high, after, right)]

    def plane(p, carry):
        mids_f = [[load_rows(forward, (s, p), g, chunks) for g in range(groups)] for s in range(count)]
        mids_a = [[load_rows(src, (s, p + HALO), g, chunks) for g in range(groups)] for s in range(count)]
        for g in range(groups):
            mua_sum, kappa_sum = [0.0] * chunks, [0.0] * chunks
            for s in range(count):
                d_f = steps(forward, s, p, mids_f[s], g)
                d_a = steps(src, s, p + HALO, mids_a[s], g)
                for j in range(chunks):
                    mua_sum[j] = mua_sum[j] - mids_f[s][g][j] * mids_a[s][g][j]
                    for a, b in zip(d_f, d_a):
                        kappa_sum[j] = kappa_sum[j] - a[j] * b[j]
            for j in range(chunks):
                plane_out[0, j, pl.ds(g, SUB, stride=groups), :] = mua_sum[j]
                plane_out[1, j, pl.ds(g, SUB, stride=groups), :] = kappa_sum[j]
        for j in range(chunks):
            grad_mua[p, :, pl.ds(LANES * j, LANES)] = plane_out[0, j]
            grad_kappa[p, :, pl.ds(LANES * j, LANES)] = plane_out[1, j]
        return carry

    lax.fori_loop(0, depth, plane, 0)


def measured_kernel(sources, detectors, data, weight, out):
    source_total = out.shape[0] // 2
    detector_count = out.shape[1]
    chunks, width = sources.shape
    total = jnp.zeros(out.shape, jnp.float32)
    detector_at = lax.broadcasted_iota(jnp.int32, (detector_count, width), 0)
    source_at = lax.broadcasted_iota(jnp.int32, (source_total, width), 0)
    for i in range(chunks):
        row = pl.ds(i, 1)
        hot = (detector_at == detectors[row, :]).astype(jnp.bfloat16)
        mine = source_at == sources[row, :]
        w = weight[row, :]
        left = jnp.concatenate([jnp.where(mine, w, 0.0), jnp.where(mine, w * data[row, :], 0.0)], axis=0)
        for part in split(left):
            total = total + lax.dot_general(part, hot, (((1,), (1,)), ((), ())), preferred_element_type=jnp.float32)
    out[...] = total


VMEM = pl.BlockSpec(memory_space=pltpu.VMEM)
SMEM = pl.BlockSpec(memory_space=pltpu.SMEM)


def call(kernel, outs, specs, scratch, *args):
    return pl.pallas_call(
        kernel,
        out_shape=outs,
        in_specs=specs,
        out_specs=jax.tree.map(lambda unused: VMEM, outs),
        scratch_shapes=scratch,
        compiler_params=pltpu.CompilerParams(vmem_limit_bytes=60 * 1024 * 1024),
    )(*args)


def near_swap(block, count):
    return lax.ppermute(block, "vox", [(i, i ^ 1) for i in range(count) if i ^ 1 < count])


def far_swap(block, count):
    pairs = [(i, i + 1) for i in range(1, count - 1, 2)]
    return lax.ppermute(block, "vox", pairs + [(b, a) for a, b in pairs])


def tile_sum(block, axis_name, order):
    count = lax.axis_size(axis_name)
    bits = count.bit_length() - 1
    me = lax.axis_index(axis_name)
    left = list(range(bits))
    for bit in order:
        dim = left.index(bit)
        shift = bits - 1 - bit
        mine = me >> shift & 1
        away = lax.dynamic_index_in_dim(block, 1 - mine, dim, False)
        kept = lax.dynamic_index_in_dim(block, mine, dim, False)
        block = kept + lax.ppermute(away, axis_name, [(i, i ^ (1 << shift)) for i in range(count)])
        left.remove(bit)
    return block


def body(
    kappa,
    mua,
    prior_forward_fields,
    prior_adjoint_fields,
    source_position,
    detector_voxel,
    measured_source,
    measured_detector,
    measured_data,
    measured_weight,
):
    count, depth, width_y, width_z = prior_forward_fields.shape
    plane_size = width_y * width_z
    slab, slabs = lax.axis_index("vox"), lax.axis_size("vox")
    group, groups = lax.axis_index("src"), lax.axis_size("src")
    parity = slab % 2
    detectors = detector_voxel.shape[0]
    f32 = jnp.float32

    def rims(block, dim, width, first):
        low = lax.slice_in_dim(block, 0, width, axis=dim)
        high = lax.slice_in_dim(block, block.shape[dim] - width, None, axis=dim)
        return jnp.where(parity == first, high, low)

    def coefficient_rims(first):
        return jnp.concatenate([rims(kappa, 0, HALO, first), rims(mua, 0, SWEEPS, first)], axis=0)

    coef_far = far_swap(coefficient_rims(1), slabs)
    coef_near = near_swap(coefficient_rims(0), slabs)
    fwd_far = far_swap(rims(prior_forward_fields, 1, HALO, 1), slabs)
    fwd_near = near_swap(rims(prior_forward_fields, 1, HALO, 0), slabs)
    adj_far = far_swap(rims(prior_adjoint_fields, 1, HALO, 1), slabs)
    adj_near = near_swap(rims(prior_adjoint_fields, 1, HALO, 0), slabs)

    cells = (detector_voxel - slab * depth * plane_size).reshape(1, detectors)
    cells_far = far_swap(cells, slabs)
    cells_near = near_swap(cells, slabs)

    rows = measured_source.shape[0]
    shaped = lambda a: a.reshape(rows // LANES, LANES)
    sums = call(
        measured_kernel,
        jax.ShapeDtypeStruct((2 * count * groups, detectors), f32),
        [VMEM] * 4,
        [],
        shaped(measured_source),
        shaped(measured_detector - slab * detectors),
        shaped(measured_data),
        shaped(measured_weight),
    )
    sums = sums.reshape(2, groups, count, detectors).transpose(1, 0, 2, 3).reshape(groups, 2 * count, detectors)
    totals = jnp.sum(lax.all_to_all(sums, "src", split_axis=0, concat_axis=0, tiled=True), axis=0)

    mine = lax.dynamic_slice_in_dim(source_position, group * count, count)
    meta = jnp.concatenate([jnp.stack([slab, parity]).astype(jnp.int32), mine])

    planes = depth + 2 * HALO
    plane = (width_z // LANES, width_y, LANES)
    coef = call(
        functools.partial(coefficient_kernel, depth * slabs),
        jax.ShapeDtypeStruct((7, depth + 2 * SWEEPS - 1, *plane), f32),
        [SMEM] + [VMEM] * 4,
        [pltpu.VMEM((planes, *plane), f32), pltpu.VMEM((planes - 2, *plane), f32)],
        meta,
        kappa,
        mua,
        coef_near,
        coef_far,
    )
    field = pltpu.VMEM((count, planes, *plane), f32)
    forward, source = call(
        forward_kernel,
        (
            jax.ShapeDtypeStruct((count, depth + 1, *plane), f32),
            jax.ShapeDtypeStruct((count, detectors), f32),
        ),
        [SMEM] + [VMEM] * 6,
        [field, field],
        meta,
        coef,
        prior_forward_fields,
        fwd_near,
        fwd_far,
        cells,
        totals,
    )
    source_far = far_swap(source, slabs)
    source_near = near_swap(source, slabs)
    grad_mua, grad_kappa = call(
        adjoint_kernel,
        (jax.ShapeDtypeStruct(kappa.shape, f32), jax.ShapeDtypeStruct(kappa.shape, f32)),
        [SMEM] + [VMEM] * 11,
        [field, field, pltpu.VMEM((count, depth + 2 * SWEEPS - 1, *plane), f32), pltpu.VMEM((2, *plane), f32)],
        meta,
        coef,
        prior_adjoint_fields,
        adj_near,
        adj_far,
        forward,
        cells,
        source,
        cells_near,
        source_near,
        cells_far,
        source_far,
    )
    bits = groups.bit_length() - 1

    def tiled(block):
        block = block.reshape(depth, groups, width_y // groups, width_z).transpose(1, 0, 2, 3)
        return block.reshape((2,) * bits + (depth, width_y // groups, width_z))

    return (
        tile_sum(tiled(grad_mua), "src", list(range(bits))),
        tile_sum(tiled(grad_kappa), "src", list(range(bits))[::-1]),
    )


def solution(mesh):
    in_specs = (
        P("vox", None, None),
        P("vox", None, None),
        P("src", "vox", None, None),
        P("src", "vox", None, None),
        P(),
        P("vox"),
        P(("src", "vox")),
        P(("src", "vox")),
        P(("src", "vox")),
        P(("src", "vox")),
    )
    out_specs = (P("vox", "src", None), P("vox", "src", None))
    return jax.shard_map(body, mesh=mesh, in_specs=in_specs, out_specs=out_specs, check_vma=False)
```

time: 375 us -> 107 us (0.29); the launches traced: 367 us -> 106 us
  local copies, waits for them, and re-layouts: 115 us -> 5.72 us
  other arithmetic: 104 us -> 11.3 us
  starting transfers between devices: 72.1 us -> 22.8 us
  Pallas kernels: 0 us -> 48.9 us
  waiting for transfers between devices: 61.5 us -> 16.2 us
  between operations: 15.1 us -> 0.9 us
    scatter-add x4 -> x0, other arithmetic: 60.4 us -> none  [the longest x3 45.6 us: body(): placed = jnp.zeros((source_count, depth_x * plane_size), jnp.float32).at[...]
    pallas_call x0 -> x4, Pallas kernels: none -> 48.9 us  [call(): pl.pallas_call(kernel, out_shape=outs, in_specs=specs, out_specs=jax.tree...]
    ppermute x27 -> x14, starting transfers between devices: 63.6 us -> 18.6 us  [the longest x5 11.4 us: far_swap(): return lax.ppermute(block, 'vox', pairs + [(b, a) for a, b in pairs])]
    reshape x2 -> x1, local copies, waits for them, and re-layouts: 39.2 us -> 1.3 us  [body(): sums.reshape(2, groups, count, detectors).transpose(1, 0, 2, 3)]
    div x1 -> x0, local copies, waits for them, and re-layouts: 33.3 us -> none  [jacobi_sweep(): return (source + inflow) / diagonal]
    reduce_scatter x1 -> x0, waiting for transfers between devices: 29.4 us -> none  [body(): lax.psum_scatter(jnp.stack([grad_mua, grad_kappa]), 'src', scatter_dimens...]
    div x12 -> x0, other arithmetic: 29.4 us -> none  [jacobi_sweep(): return (source + inflow) / diagonal]
    ppermute x27 -> x14, waiting for transfers between devices: 32 us -> 13.7 us  [the longest x4 10.6 us: tile_sum(): lax.ppermute(away, axis_name, [(i, i ^ 1 << shift) for i in range(count)])]
  transfers between devices with their start and end apart: 30 -> 15, of which waited for: 15 -> 6; matrix products, arithmetic and copies ran while one was open for 54% -> 10% of each run, Pallas kernels for 0% -> 27%
where the time goes in v1:
time: 107 us; the launch traced here: 106 us
  Pallas kernels  48.9 us (46%)
  starting transfers between devices  22.8 us (21%)
  waiting for transfers between devices  16.2 us (15%)
  other arithmetic  11.3 us (11%)
  local copies, waits for them, and re-layouts  5.72 us (5%)
    pallas_call x4, Pallas kernels, call(): pl.pallas_call(kernel, out_shape=outs, in_specs=specs, out_specs=jax.tree...  48.9 us
    ppermute x5, starting transfers between devices, far_swap(): return lax.ppermute(block, 'vox', pairs + [(b, a) for a, b in pairs])  11.4 us
    ppermute x4, waiting for transfers between devices, tile_sum(): lax.ppermute(away, axis_name, [(i, i ^ 1 << shift) for i in range(count)])  10.6 us
    select_n x4, other arithmetic, rims(): return jnp.where(parity == first, high, low)  7 us
    all_to_all x1, starting transfers between devices, body(): lax.all_to_all(sums, 'src', split_axis=0, concat_axis=0, tiled=True)  4.25 us
    ppermute x5, starting transfers between devices, near_swap(): lax.ppermute(block, 'vox', [(i, i ^ 1) for i in range(count) if i ^ 1 < c...  3.82 us
    ppermute x4, starting transfers between devices, tile_sum(): lax.ppermute(away, axis_name, [(i, i ^ 1 << shift) for i in range(count)])  3.36 us
    ppermute x5, waiting for transfers between devices, far_swap(): return lax.ppermute(block, 'vox', pairs + [(b, a) for a, b in pairs])  3.1 us
  transfers between devices with their start and end apart: 15, of which 6 were waited for; matrix products, arithmetic and copies ran while one was open for 10% of the time, Pallas kernels for 27%

profile of v1, /device:TPU:10, one launch (start us, length us, event | category | flops | bytes accessed | tf_op | source)
XLA Modules:
  0.0 105.8 jit_solution(5996139385186715095)
XLA Ops:
  0.7 1.3 %slice_select_fusion.4 = (f32[7,64,256]{2,1,0:T(8,128)S(1)}, f32[7,64,256]{2,1,0:T(8,128)S(1)}) fusion(f32[8,64,256]{2,1,0:T(8,128)} %kappa.1, pred[]{:T(512)S(6)} %eq.7, pred[]{:T(512)S(6)} %eq.6), kind=kLoop, calls=%fused_computation.6 | loop fusion | flops 229376 | bytes 1835010 | tf_op jit(solution)/shard_map/jit(_where)/select_n | solution.py:369
  2.0 1.2 %slice_select_fusion.6 = (f32[6,64,256]{2,1,0:T(8,128)S(1)}, f32[6,64,256]{2,1,0:T(8,128)S(1)}) fusion(f32[8,64,256]{2,1,0:T(8,128)} %mua.1, pred[]{:T(512)S(6)} %eq.7, pred[]{:T(512)S(6)} %eq.6), kind=kLoop, calls=%fused_computation.8 | loop fusion | flops 196608 | bytes 1572866 | tf_op jit(solution)/shard_map/jit(_where)/select_n | solution.py:369
  3.2 1.9 %collective-permute-start.1 = (f32[13,64,256]{2,1,0:T(8,128)S(1)}, f32[13,64,256]{2,1,0:T(8,128)}, u32[]{:S(2)}, u32[]{:S(2)}) collective-permute-start(f32[13,64,256]{2,1,0:T(8,128)S(1)} %pad_maximum_fusion.1), channel_id=1, source_target_pairs={{1,2},{3,4},{5,6},{2,1},{4,3},{6,5},{9,10},{11,12},{13,14},{10,9},... | collective-permute-start | bytes 2555912 | tf_op jit(solution)/shard_map/ppermute | solution.py:327
  5.2 3.0 %slice_select_fusion = (f32[2,7,64,256]{3,2,1,0:T(8,128)}, f32[2,7,64,256]{3,2,1,0:T(8,128)}) fusion(f32[2,8,64,256]{3,2,1,0:T(8,128)} %own.2, pred[]{:T(512)S(6)} %eq.7, pred[]{:T(512)S(6)} %eq.6), kind=kLoop, calls=%fused_computation | loop fusion | flops 458752 | bytes 3670018 | tf_op jit(solution)/shard_map/jit(_where)/select_n | solution.py:369
  8.2 1.7 %collective-permute-start.4 = (f32[2,7,64,256]{3,2,1,0:T(8,128)}, f32[2,7,64,256]{3,2,1,0:T(8,128)S(1)}, u32[]{:S(2)}, u32[]{:S(2)}) collective-permute-start(f32[2,7,64,256]{3,2,1,0:T(8,128)} %get-tuple-element.11), channel_id=1, source_target_pairs={{0,1},{1,0},{2,3},{3,2},{4,5},{5,4},{6,7},{7,6},{8,9},{9,8},{10,11... | collective-permute-start | bytes 2752520 | tf_op jit(solution)/shard_map/ppermute | solution.py:322
  9.9 2.0 %collective-permute-start.5 = (f32[2,7,64,256]{3,2,1,0:T(8,128)}, f32[2,7,64,256]{3,2,1,0:T(8,128)}, u32[]{:S(2)}, u32[]{:S(2)}) collective-permute-start(f32[2,7,64,256]{3,2,1,0:T(8,128)} %get-tuple-element.10), channel_id=1, source_target_pairs={{1,2},{3,4},{5,6},{2,1},{4,3},{6,5},{9,10},{11,12},{13,14},{10,9},... | collective-permute-start | bytes 2752520 | tf_op jit(solution)/shard_map/ppermute | solution.py:327
  11.8 1.5 %slice_select_fusion.2 = (f32[2,7,64,256]{3,2,1,0:T(8,128)}, f32[2,7,64,256]{3,2,1,0:T(8,128)}) fusion(f32[2,8,64,256]{3,2,1,0:T(8,128)S(1)} %copy-done, pred[]{:T(512)S(6)} %eq.7, pred[]{:T(512)S(6)} %eq.6), kind=kLoop, calls=%fused_computation.2 | loop fusion | flops 458752 | bytes 3670018 | tf_op jit(solution)/shard_map/jit(_where)/select_n | solution.py:369
  13.3 1.6 %collective-permute-start.2 = (f32[2,7,64,256]{3,2,1,0:T(8,128)}, f32[2,7,64,256]{3,2,1,0:T(8,128)S(1)}, u32[]{:S(2)}, u32[]{:S(2)}) collective-permute-start(f32[2,7,64,256]{3,2,1,0:T(8,128)} %get-tuple-element.13), channel_id=1, source_target_pairs={{0,1},{1,0},{2,3},{3,2},{4,5},{5,4},{6,7},{7,6},{8,9},{9,8},{10,11... | collective-permute-start | bytes 2752520 | tf_op jit(solution)/shard_map/ppermute | solution.py:322
  15.0 2.0 %collective-permute-start.3 = (f32[2,7,64,256]{3,2,1,0:T(8,128)}, f32[2,7,64,256]{3,2,1,0:T(8,128)S(1)}, u32[]{:S(2)}, u32[]{:S(2)}) collective-permute-start(f32[2,7,64,256]{3,2,1,0:T(8,128)} %get-tuple-element.12), channel_id=1, source_target_pairs={{1,2},{3,4},{5,6},{2,1},{4,3},{6,5},{9,10},{11,12},{13,14},{10,9},... | collective-permute-start | bytes 2752520 | tf_op jit(solution)/shard_map/ppermute | solution.py:327
  16.9 1.0 pad_maximum_fusion
  17.9 0.6 subtract_bitcast_fusion.detectors
  18.5 1.9 %shard_map.114 = f32[16,128]{1,0:T(8,128)} custom-call(s32[8,128]{1,0:T(8,128)} %bitcast.46, s32[8,128]{1,0:T(8,128)} %subtract_bitcast_fusion.detectors, f32[8,128]{1,0:T(8,128)} %bitcast.47, f32[8,128]{1,0:T(8,128)} %bitcast.48), custom_call_target="tpu_custom_call" | custom-call | tf_op jit(solution)/shard_map/pallas_call | solution.py:311
  20.4 1.3 %copy.16 = f32[2,4,2,128]{3,2,0,1:T(2,128)} copy(f32[2,4,2,128]{3,2,1,0:T(2,128)} %bitcast.45) | data formatting | bytes 16384 | tf_op jit(solution)/shard_map/reshape | solution.py:397
  21.7 4.2 %all-to-all-start = ((f32[4,4,128]{2,1,0:T(4,128)}), f32[4,4,128]{2,1,0:T(4,128)S(1)}, u32[]{:S(2)}, u32[]{:S(2)}) async-start(f32[4,4,128]{2,1,0:T(4,128)} %bitcast.9), calls=%async_computation | async-start | bytes 16384 | tf_op jit(solution)/shard_map/all_to_all | solution.py:398
  26.0 0.7 pad_add_fusion.meta
  26.7 2.5 %all-to-all-done = f32[4,4,128]{2,1,0:T(4,128)S(1)} async-done(((f32[4,4,128]{2,1,0:T(4,128)}), f32[4,4,128]{2,1,0:T(4,128)S(1)}, u32[]{:S(2)}, u32[]{:S(2)}) %all-to-all-start) | async-done | bytes 8224 | tf_op jit(solution)/shard_map/all_to_all | solution.py:398
  29.8 8.6 %shard_map.113.coef = f32[7,19,2,64,128]{4,3,2,1,0:T(8,128)} custom-call(s32[4]{0:T(128)} %pad_add_fusion.meta, f32[8,64,256]{2,1,0:T(8,128)} %kappa.1, f32[8,64,256]{2,1,0:T(8,128)} %mua.1, f32[13,64,256]{2,1,0:T(8,128)} %collective-permute-done.near, f32[13,64,256]{2,1,0:T(8,128)} %collective-permute-done.1.far), custom_call_target="tpu_custom_call" | custom-call | tf_op jit(solution)/shard_map/pallas_call | solution.py:311
  38.4 0.9 copy-done.3
  39.3 18.3 %shard_map.115 = (f32[2,9,2,64,128]{4,3,2,1,0:T(8,128)}, f32[2,128]{1,0:T(2,128)}) custom-call(s32[4]{0:T(128)} %pad_add_fusion.meta, f32[7,19,2,64,128]{4,3,2,1,0:T(8,128)} %shard_map.113.coef, f32[2,8,64,256]{3,2,1,0:T(8,128)} %own.2, f32[2,7,64,256]{3,2,1,0:T(8,128)} %copy-done.3, f32[2,7,64,256]{3,2,1,0:T(8,128)} %collective-permute-done.5.far, ...), custom_call_target="tpu_custom_call" | custom-call | tf_op jit(solution)/shard_map/pallas_call | solution.py:311
  58.0 3.6 %collective-permute-start.9 = (f32[2,128]{1,0:T(2,128)}, f32[2,128]{1,0:T(2,128)S(1)}, u32[]{:S(2)}, u32[]{:S(2)}) collective-permute-start(f32[2,128]{1,0:T(2,128)} %get-tuple-element.7.source), channel_id=1, source_target_pairs={{1,2},{3,4},{5,6},{2,1},{4,3},{6,5},{9,10},{11,12},{13,14},{10,9},... | collective-permute-start | bytes 3080 | tf_op jit(solution)/shard_map/ppermute | solution.py:327
  61.7 2.0 %collective-permute-start.8 = (s32[1,128]{1,0:T(1,128)}, s32[1,128]{1,0:T(1,128)S(1)}, u32[]{:S(2)}, u32[]{:S(2)}) collective-permute-start(s32[1,128]{1,0:T(1,128)} %copy-done.5), channel_id=1, source_target_pairs={{1,2},{3,4},{5,6},{2,1},{4,3},{6,5},{9,10},{11,12},{13,14},{10,9},... | collective-permute-start | bytes 1544 | tf_op jit(solution)/shard_map/ppermute | solution.py:327
  63.6 3.1 %collective-permute-done.8.far_cells = s32[1,128]{1,0:T(1,128)S(1)} collective-permute-done((s32[1,128]{1,0:T(1,128)}, s32[1,128]{1,0:T(1,128)S(1)}, u32[]{:S(2)}, u32[]{:S(2)}) %collective-permute-start.8) | collective-permute-done | bytes 544 | tf_op jit(solution)/shard_map/ppermute | solution.py:327
  68.0 20.2 %shard_map.116 = (f32[8,64,256]{2,1,0:T(8,128)}, f32[8,64,256]{2,1,0:T(8,128)}) custom-call(s32[4]{0:T(128)} %pad_add_fusion.meta, f32[7,19,2,64,128]{4,3,2,1,0:T(8,128)} %shard_map.113.coef, f32[2,8,64,256]{3,2,1,0:T(8,128)} %own.3, f32[2,7,64,256]{3,2,1,0:T(8,128)} %copy-done.1, f32[2,7,64,256]{3,2,1,0:T(8,128)} %copy-done.2, ...), custom_call_target="tpu_custom_call" | custom-call | tf_op jit(solution)/shard_map/pallas_call | solution.py:311
  88.2 1.1 %constant_dynamic-slice_fusion.1 = (f32[2,1,8,16,256]{4,3,1,0,2:T(8,128)S(1)}, f32[2,1,8,16,256]{4,3,1,0,2:T(8,128)S(1)}) fusion(f32[2,2,8,16,256]{4,3,1,0,2:T(8,128)} %bitcast.42, s32[]{:T(128)S(6)} %select_n.97, s32[]{:T(128)S(6)} %select_n.98), kind=kLoop, calls=%fused_computation.20 | loop fusion | bytes 1048584 | tf_op jit(solution)/shard_map/jit(dynamic_index_in_dim)/dynamic_slice | solution.py:340
  89.3 1.7 %collective-permute-start.12 = (f32[2,8,16,256]{3,2,1,0:T(8,128)S(1)}, f32[2,8,16,256]{3,2,1,0:T(8,128)S(1)}, u32[]{:S(2)}, u32[]{:S(2)}) collective-permute-start(f32[2,8,16,256]{3,2,1,0:T(8,128)S(1)} %bitcast.43), channel_id=1, source_target_pairs={{0,8},{8,0},{16,24},{24,16},{1,9},{9,1},{17,25},{25,17},{2,10},{10... | collective-permute-start | bytes 786440 | tf_op jit(solution)/shard_map/ppermute | solution.py:341
  91.1 1.1 %constant_dynamic-slice_fusion.3 = (f32[1,2,8,16,256]{4,3,1,0,2:T(8,128)S(1)}, f32[1,2,8,16,256]{4,3,1,0,2:T(8,128)S(1)}) fusion(f32[2,2,8,16,256]{4,3,1,0,2:T(8,128)} %bitcast.41, s32[]{:T(128)S(6)} %select_n.95, s32[]{:T(128)S(6)} %select_n.96), kind=kLoop, calls=%fused_computation.22 | loop fusion | bytes 1048584 | tf_op jit(solution)/shard_map/jit(dynamic_index_in_dim)/dynamic_slice | solution.py:340
  92.7 4.8 %collective-permute-done.12 = f32[2,8,16,256]{3,2,1,0:T(8,128)S(1)} collective-permute-done((f32[2,8,16,256]{3,2,1,0:T(8,128)S(1)}, f32[2,8,16,256]{3,2,1,0:T(8,128)S(1)}, u32[]{:S(2)}, u32[]{:S(2)}) %collective-permute-start.12) | collective-permute-done | bytes 262176 | tf_op jit(solution)/shard_map/ppermute | solution.py:341
  98.1 1.9 %collective-permute-done.10 = f32[2,8,16,256]{3,2,1,0:T(8,128)S(1)} collective-permute-done((f32[2,8,16,256]{3,2,1,0:T(8,128)S(1)}, f32[2,8,16,256]{3,2,1,0:T(8,128)S(1)}, u32[]{:S(2)}, u32[]{:S(2)}) %collective-permute-start.10) | collective-permute-done | bytes 262176 | tf_op jit(solution)/shard_map/ppermute | solution.py:341
  100.7 2.0 %collective-permute-done.13 = f32[8,16,256]{2,1,0:T(8,128)S(1)} collective-permute-done((f32[8,16,256]{2,1,0:T(8,128)S(1)}, f32[8,16,256]{2,1,0:T(8,128)S(1)}, u32[]{:S(2)}, u32[]{:S(2)}) %collective-permute-start.13) | collective-permute-done | bytes 131104 | tf_op jit(solution)/shard_map/ppermute | solution.py:341
  102.7 0.7 bitcast_add_fusion.2
  103.3 1.8 %collective-permute-done.11 = f32[8,16,256]{2,1,0:T(8,128)S(1)} collective-permute-done((f32[8,16,256]{2,1,0:T(8,128)S(1)}, f32[8,16,256]{2,1,0:T(8,128)S(1)}, u32[]{:S(2)}, u32[]{:S(2)}) %collective-permute-start.11) | collective-permute-done | bytes 131104 | tf_op jit(solution)/shard_map/ppermute | solution.py:341
  105.2 0.7 bitcast_add_fusion.3
  (48 shorter events, 4.3 us)
Async XLA Ops:
  0.6 11.2 %copy-start = (f32[2,8,64,256]{3,2,1,0:T(8,128)S(1)}, f32[2,8,64,256]{3,2,1,0:T(8,128)}, u32[]{:S(2)}) copy-start(f32[2,8,64,256]{3,2,1,0:T(8,128)} %own.3) | copy-start | bytes 3145732
  0.6 17.3 %copy-start.4 = (s32[1024]{0:T(1024)S(1)}, s32[1024]{0:T(1024)}, u32[]{:S(2)}) copy-start(s32[1024]{0:T(1024)} %param.17) | copy-start | bytes 12292
  0.7 25.3 %copy-start.10 = (s32[8]{0:T(128)S(1)}, s32[8]{0:T(128)}, u32[]{:S(2)}) copy-start(s32[8]{0:T(128)} %param.14) | copy-start | bytes 100
  0.7 25.3 %copy-start.11 = (s32[128]{0:T(128)S(1)}, s32[128]{0:T(128)}, u32[]{:S(2)}) copy-start(s32[128]{0:T(128)} %param.15) | copy-start | bytes 1540
  3.2 14.7 %collective-permute-start.1 = (f32[13,64,256]{2,1,0:T(8,128)S(1)}, f32[13,64,256]{2,1,0:T(8,128)}, u32[]{:S(2)}, u32[]{:S(2)}) collective-permute-start(f32[13,64,256]{2,1,0:T(8,128)S(1)} %pad_maximum_fusion.1), channel_id=1, source_target_pairs={{1,2},{3,4},{5,6},{2,1},{4,3},{6,5},{9,10},{11,12},{13,14},{10,9},... | collective-permute-start | bytes 2555912 | tf_op jit(solution)/shard_map/ppermute | solution.py:327
  8.2 30.2 %collective-permute-start.4 = (f32[2,7,64,256]{3,2,1,0:T(8,128)}, f32[2,7,64,256]{3,2,1,0:T(8,128)S(1)}, u32[]{:S(2)}, u32[]{:S(2)}) collective-permute-start(f32[2,7,64,256]{3,2,1,0:T(8,128)} %get-tuple-element.11), channel_id=1, source_target_pairs={{0,1},{1,0},{2,3},{3,2},{4,5},{5,4},{6,7},{7,6},{8,9},{9,8},{10,11... | collective-permute-start | bytes 2752520 | tf_op jit(solution)/shard_map/ppermute | solution.py:322
  9.9 28.5 %collective-permute-start.5 = (f32[2,7,64,256]{3,2,1,0:T(8,128)}, f32[2,7,64,256]{3,2,1,0:T(8,128)}, u32[]{:S(2)}, u32[]{:S(2)}) collective-permute-start(f32[2,7,64,256]{3,2,1,0:T(8,128)} %get-tuple-element.10), channel_id=1, source_target_pairs={{1,2},{3,4},{5,6},{2,1},{4,3},{6,5},{9,10},{11,12},{13,14},{10,9},... | collective-permute-start | bytes 2752520 | tf_op jit(solution)/shard_map/ppermute | solution.py:327
  13.3 53.4 %collective-permute-start.2 = (f32[2,7,64,256]{3,2,1,0:T(8,128)}, f32[2,7,64,256]{3,2,1,0:T(8,128)S(1)}, u32[]{:S(2)}, u32[]{:S(2)}) collective-permute-start(f32[2,7,64,256]{3,2,1,0:T(8,128)} %get-tuple-element.13), channel_id=1, source_target_pairs={{0,1},{1,0},{2,3},{3,2},{4,5},{5,4},{6,7},{7,6},{8,9},{9,8},{10,11... | collective-permute-start | bytes 2752520 | tf_op jit(solution)/shard_map/ppermute | solution.py:322
  15.0 51.8 %collective-permute-start.3 = (f32[2,7,64,256]{3,2,1,0:T(8,128)}, f32[2,7,64,256]{3,2,1,0:T(8,128)S(1)}, u32[]{:S(2)}, u32[]{:S(2)}) collective-permute-start(f32[2,7,64,256]{3,2,1,0:T(8,128)} %get-tuple-element.12), channel_id=1, source_target_pairs={{1,2},{3,4},{5,6},{2,1},{4,3},{6,5},{9,10},{11,12},{13,14},{10,9},... | collective-permute-start | bytes 2752520 | tf_op jit(solution)/shard_map/ppermute | solution.py:327
  17.9 11.9 %collective-permute-start = (f32[13,64,256]{2,1,0:T(8,128)}, f32[13,64,256]{2,1,0:T(8,128)}, u32[]{:S(2)}, u32[]{:S(2)}) collective-permute-start(f32[13,64,256]{2,1,0:T(8,128)} %pad_maximum_fusion), channel_id=1, source_target_pairs={{0,1},{1,0},{2,3},{3,2},{4,5},{5,4},{6,7},{7,6},{8,9},{9,8},{10,11... | collective-permute-start | bytes 2555912 | tf_op jit(solution)/shard_map/ppermute | solution.py:322
  21.7 7.5 %all-to-all-start = ((f32[4,4,128]{2,1,0:T(4,128)}), f32[4,4,128]{2,1,0:T(4,128)S(1)}, u32[]{:S(2)}, u32[]{:S(2)}) async-start(f32[4,4,128]{2,1,0:T(4,128)} %bitcast.9), calls=%async_computation | async-start | bytes 16384 | tf_op jit(solution)/shard_map/all_to_all | solution.py:398
  26.0 12.3 %copy-start.5 = (s32[1,128]{1,0:T(1,128)}, s32[1,128]{1,0:T(1,128)S(1)}, u32[]{:S(2)}) copy-start(s32[1,128]{1,0:T(1,128)S(1)} %subtract_bitcast_fusion.1.cells) | copy-start | bytes 1540
  29.8 31.9 %collective-permute-start.6 = (s32[1,128]{1,0:T(1,128)S(1)}, s32[1,128]{1,0:T(1,128)S(1)}, u32[]{:S(2)}, u32[]{:S(2)}) collective-permute-start(s32[1,128]{1,0:T(1,128)S(1)} %subtract_bitcast_fusion.1.cells), channel_id=1, source_target_pairs={{0,1},{1,0},{2,3},{3,2},{4,5},{5,4},{6,7},{7,6},{8,9},{9,8},{10,11... | collective-permute-start | bytes 1544 | tf_op jit(solution)/shard_map/ppermute | solution.py:322
  38.3 0.9 copy-start.3
  57.5 9.2 %collective-permute-start.7 = (f32[2,128]{1,0:T(2,128)}, f32[2,128]{1,0:T(2,128)S(1)}, u32[]{:S(2)}, u32[]{:S(2)}) collective-permute-start(f32[2,128]{1,0:T(2,128)} %get-tuple-element.7.source), channel_id=1, source_target_pairs={{0,1},{1,0},{2,3},{3,2},{4,5},{5,4},{6,7},{7,6},{8,9},{9,8},{10,11... | collective-permute-start | bytes 3080 | tf_op jit(solution)/shard_map/ppermute | solution.py:322
  58.0 8.7 %collective-permute-start.9 = (f32[2,128]{1,0:T(2,128)}, f32[2,128]{1,0:T(2,128)S(1)}, u32[]{:S(2)}, u32[]{:S(2)}) collective-permute-start(f32[2,128]{1,0:T(2,128)} %get-tuple-element.7.source), channel_id=1, source_target_pairs={{1,2},{3,4},{5,6},{2,1},{4,3},{6,5},{9,10},{11,12},{13,14},{10,9},... | collective-permute-start | bytes 3080 | tf_op jit(solution)/shard_map/ppermute | solution.py:327
  61.6 5.1 %copy-start.8 = (s32[1,128]{1,0:T(1,128)}, s32[1,128]{1,0:T(1,128)S(1)}, u32[]{:S(2)}) copy-start(s32[1,128]{1,0:T(1,128)S(1)} %collective-permute-done.6.near_cells) | copy-start | bytes 1540
  61.7 5.1 %collective-permute-start.8 = (s32[1,128]{1,0:T(1,128)}, s32[1,128]{1,0:T(1,128)S(1)}, u32[]{:S(2)}, u32[]{:S(2)}) collective-permute-start(s32[1,128]{1,0:T(1,128)} %copy-done.5), channel_id=1, source_target_pairs={{1,2},{3,4},{5,6},{2,1},{4,3},{6,5},{9,10},{11,12},{13,14},{10,9},... | collective-permute-start | bytes 1544 | tf_op jit(solution)/shard_map/ppermute | solution.py:327
  66.7 0.6 copy-start.9
  66.7 1.0 copy-start.1
  66.7 1.3 %copy-start.2 = (f32[2,7,64,256]{3,2,1,0:T(8,128)}, f32[2,7,64,256]{3,2,1,0:T(8,128)S(1)}, u32[]{:S(2)}) copy-start(f32[2,7,64,256]{3,2,1,0:T(8,128)S(1)} %collective-permute-done.3.far) | copy-start | bytes 2752516
  66.8 1.2 %copy-start.6 = (f32[2,128]{1,0:T(2,128)}, f32[2,128]{1,0:T(2,128)S(1)}, u32[]{:S(2)}) copy-start(f32[2,128]{1,0:T(2,128)S(1)} %collective-permute-done.7.near_source) | copy-start | bytes 3076
  66.8 1.2 %copy-start.7 = (f32[2,128]{1,0:T(2,128)}, f32[2,128]{1,0:T(2,128)S(1)}, u32[]{:S(2)}) copy-start(f32[2,128]{1,0:T(2,128)S(1)} %collective-permute-done.9.far_source) | copy-start | bytes 3076
  89.3 8.2 %collective-permute-start.12 = (f32[2,8,16,256]{3,2,1,0:T(8,128)S(1)}, f32[2,8,16,256]{3,2,1,0:T(8,128)S(1)}, u32[]{:S(2)}, u32[]{:S(2)}) collective-permute-start(f32[2,8,16,256]{3,2,1,0:T(8,128)S(1)} %bitcast.43), channel_id=1, source_target_pairs={{0,8},{8,0},{16,24},{24,16},{1,9},{9,1},{17,25},{25,17},{2,10},{10... | collective-permute-start | bytes 786440 | tf_op jit(solution)/shard_map/ppermute | solution.py:341
  92.2 7.9 %collective-permute-start.10 = (f32[2,8,16,256]{3,2,1,0:T(8,128)S(1)}, f32[2,8,16,256]{3,2,1,0:T(8,128)S(1)}, u32[]{:S(2)}, u32[]{:S(2)}) collective-permute-start(f32[2,8,16,256]{3,2,1,0:T(8,128)S(1)} %bitcast.44), channel_id=1, source_target_pairs={{0,16},{8,24},{16,0},{24,8},{1,17},{9,25},{17,1},{25,9},{2,18},{10... | collective-permute-start | bytes 786440 | tf_op jit(solution)/shard_map/ppermute | solution.py:341
  97.6 5.0 %collective-permute-start.13 = (f32[8,16,256]{2,1,0:T(8,128)S(1)}, f32[8,16,256]{2,1,0:T(8,128)S(1)}, u32[]{:S(2)}, u32[]{:S(2)}) collective-permute-start(f32[8,16,256]{2,1,0:T(8,128)S(1)} %dynamic-slice_bitcast_fusion), channel_id=1, source_target_pairs={{0,16},{8,24},{16,0},{24,8},{1,17},{9,25},{17,1},{25,9},{2,18},{10... | collective-permute-start | bytes 393224 | tf_op jit(solution)/shard_map/ppermute | solution.py:341
  100.1 5.0 %collective-permute-start.11 = (f32[8,16,256]{2,1,0:T(8,128)S(1)}, f32[8,16,256]{2,1,0:T(8,128)S(1)}, u32[]{:S(2)}, u32[]{:S(2)}) collective-permute-start(f32[8,16,256]{2,1,0:T(8,128)S(1)} %dynamic-slice_bitcast_fusion.1), channel_id=1, source_target_pairs={{0,8},{8,0},{16,24},{24,16},{1,9},{9,1},{17,25},{25,17},{2,10},{10... | collective-permute-start | bytes 393224 | tf_op jit(solution)/shard_map/ppermute | solution.py:341

commit v2 on v1

v2 whole, which is shorter than its diff:
```python
import functools

import jax
import jax.numpy as jnp
from jax import lax
from jax.experimental import pallas as pl
from jax.experimental.pallas import tpu as pltpu
from jax.sharding import PartitionSpec as P

SWEEPS = 6
HALO = SWEEPS + 1
LANES = 128
SUB = 8

source_gain = 10.0


def lane_ids():
    return lax.broadcasted_iota(jnp.int32, (SUB, LANES), 1)


def sub_ids():
    return lax.broadcasted_iota(jnp.int32, (SUB, LANES), 0)


def next_z(chunks):
    return chunks[1:] + [pltpu.roll(chunks[0], LANES - 1, 1)]


def prev_z(chunks):
    return [pltpu.roll(chunks[-1], 1, 1)] + chunks[:-1]


def next_y(rows, g):
    return rows[g + 1] if g + 1 < len(rows) else [pltpu.roll(c, SUB - 1, 0) for c in rows[0]]


def prev_y(rows, g):
    return rows[g - 1] if g > 0 else [pltpu.roll(c, 1, 0) for c in rows[-1]]


def load_rows(ref, lead, g, chunks):
    return [ref[(*lead, j, pl.ds(SUB * g, SUB), slice(None))] for j in range(chunks)]


def load_plane(ref, lead, groups, chunks):
    return [load_rows(ref, lead, g, chunks) for g in range(groups)]


def store_rows(ref, lead, g, values):
    for j, value in enumerate(values):
        ref[(*lead, j, pl.ds(SUB * g, SUB), slice(None))] = value


def copy_planes(src, src_lead, src_first, dst, dst_lead, dst_first, count):
    for i in range(count):
        dst[(*dst_lead, dst_first + i)] = src[(*src_lead, src_first + i)]


def split(values):
    high = values.astype(jnp.bfloat16)
    rest = values - high.astype(jnp.float32)
    middle = rest.astype(jnp.bfloat16)
    low = (rest - middle.astype(jnp.float32)).astype(jnp.bfloat16)
    return high, middle, low


def z_order(width_z, natural_dim):
    chunks = width_z // LANES
    z = lax.broadcasted_iota(jnp.int32, (width_z, width_z), natural_dim)
    place = lax.broadcasted_iota(jnp.int32, (width_z, width_z), 1 - natural_dim)
    return (z == place % LANES * chunks + place // LANES).astype(jnp.bfloat16)


def pack_kernel(kinds, *refs):
    owns, (near, far) = refs[-2 - len(kinds) : -2], refs[-2:]
    blocks = []
    for ref in refs[: -2 - len(kinds)]:
        blocks += [ref] if ref.ndim == 3 else [ref.at[b] for b in range(ref.shape[0])]
    depth, width_y, width_z = blocks[0].shape
    chunks, groups = width_z // LANES, width_y // SUB
    parity = lax.axis_index("vox") % 2
    order = z_order(width_z, 0)
    together = 4
    at = 0
    for own, widths in zip(owns, kinds):
        for b, width in enumerate(widths):
            block = blocks.pop(0)
            for first in range(0, depth, together):
                values = block[pl.ds(first, together)].reshape(together * width_y, width_z)
                packed = sum(jnp.dot(part, order, preferred_element_type=jnp.float32) for part in split(values))
                for i in range(together):
                    for y in range(0, width_y, SUB):
                        for j in range(chunks):
                            part = packed[i * width_y + y : i * width_y + y + SUB, LANES * j : LANES * (j + 1)]
                            if groups == SUB:
                                own[b, first + i, j, pl.ds(y // SUB, SUB, stride=SUB), :] = part
                            else:
                                for k in range(SUB):
                                    row = (y + k) % groups * SUB + (y + k) // groups
                                    own[b, first + i, j, pl.ds(row, 1), :] = part[k : k + 1]
            low, high = 0, depth - width
            copy_planes(own, (b,), jnp.where(parity == 0, low, high), far, (), at, width)
            copy_planes(own, (b,), jnp.where(parity == 0, high, low), near, (), at, width)
            at += width


def early_part(t, depth, parity):
    return jnp.where(parity == 0, HALO + 1 + t, 1 + t), depth + HALO - 2 - 2 * t


def late_part(t, depth, parity):
    return jnp.where(parity == 0, 1 + t, depth + HALO - 1 - t), HALO


def halo_place(parity, near, depth, width):
    return jnp.where((parity == 0) == near, width + depth, 0)


def coefficient_planes(slab, kap, mu, out, first, count, depth):
    chunks, width_y = kap.shape[1:3]
    groups = width_y // SUB
    lane, sub = lane_ids(), sub_ids()
    grid_planes = lax.axis_size("vox") * depth

    def plane(n, carry):
        at = first + n
        i = at - (HALO - SWEEPS)
        place = slab * depth + i
        inside = jnp.logical_and(place >= SWEEPS, place < grid_planes + SWEEPS)
        rows = load_plane(kap, (at,), groups, chunks)
        for g in range(groups):
            mid = rows[g]
            low = load_rows(kap, (at - 1,), g, chunks)
            high = load_rows(kap, (at + 1,), g, chunks)
            before, after = prev_y(rows, g), next_y(rows, g)
            if g == 0:
                before = [jnp.where(sub == 0, 0.0, c) for c in before]
            if g + 1 == groups:
                after = [jnp.where(sub == SUB - 1, 0.0, c) for c in after]
            left, right = prev_z(mid), next_z(mid)
            left[0] = jnp.where(lane == 0, 0.0, left[0])
            right[-1] = jnp.where(lane == LANES - 1, 0.0, right[-1])
            absorb = load_rows(mu, (i,), g, chunks)
            for j in range(chunks):
                face = [0.5 * (mid[j] + other[j]) for other in (low, high, before, after, left, right)]
                diagonal = absorb[j] + face[0] + face[1] + face[2] + face[3] + face[4] + face[5]
                inverse = jnp.where(inside, 1.0 / diagonal, 0.0)
                if g == 0:
                    face[2] = jnp.where(sub == 0, 0.0, face[2])
                if g + 1 == groups:
                    face[3] = jnp.where(sub == SUB - 1, 0.0, face[3])
                if j == 0:
                    face[4] = jnp.where(lane == 0, 0.0, face[4])
                if j + 1 == chunks:
                    face[5] = jnp.where(lane == LANES - 1, 0.0, face[5])
                for k in range(6):
                    out[k, i, j, pl.ds(SUB * g, SUB), :] = face[k] * inverse
                out[6, i, j, pl.ds(SUB * g, SUB), :] = inverse
        return carry

    lax.fori_loop(0, count, plane, 0)


def sweep_planes(coef, src, dst, first, planes, bias):
    count, unused, chunks, width_y, lanes = src.shape
    groups = width_y // SUB

    def one(at):
        c_at = at - (HALO - SWEEPS)
        mids = [load_plane(src, (s, at), groups, chunks) for s in range(count)]
        for g in range(groups):
            faces = [load_rows(coef, (k, c_at), g, chunks) for k in range(6)]
            for s in range(count):
                mid = mids[s][g]
                low = load_rows(src, (s, at - 1), g, chunks)
                high = load_rows(src, (s, at + 1), g, chunks)
                before, after = prev_y(mids[s], g), next_y(mids[s], g)
                left, right = prev_z(mid), next_z(mid)
                result = []
                for j in range(chunks):
                    total = faces[0][j] * low[j] + faces[1][j] * high[j]
                    total = total + (faces[2][j] * before[j] + faces[3][j] * after[j])
                    total = total + (faces[4][j] * left[j] + faces[5][j] * right[j])
                    result.append(total)
                if bias is not None:
                    extra = load_rows(bias, (s, c_at), g, chunks)
                    result = [a + b for a, b in zip(result, extra)]
                store_rows(dst, (s, at), g, result)

    def pair(i, carry):
        one(first + 2 * i)
        one(first + 2 * i + 1)
        return carry

    lax.fori_loop(0, planes // 2, pair, 0)
    if planes % 2:
        one(first + planes - 1)


def detector_masks(cells, first, planes, width_y, width_z):
    groups, chunks = width_y // SUB, width_z // LANES
    y, z = cells // width_z % width_y, cells % width_z
    row = (cells // (width_y * width_z) - first) * width_y + y % groups * SUB + y // groups
    row_at = lax.broadcasted_iota(jnp.int32, (planes * width_y, cells.shape[1]), 0)
    lane_at = lax.broadcasted_iota(jnp.int32, (LANES, cells.shape[1]), 0)
    return row_at == row, [(lane_at * chunks + j == z).astype(jnp.bfloat16) for j in range(chunks)]


def forward_sweeps(part, positions, coef, one, two, depth):
    count, unused, chunks, width_y, lanes = one.shape
    width_z, groups = chunks * LANES, width_y // SUB
    slab, group = lax.axis_index("vox"), lax.axis_index("src")
    src, dst = one, two
    for t in range(SWEEPS):
        first, planes = part(t, depth, slab % 2)
        sweep_planes(coef, src, dst, first, planes, None)
        for s in range(count):
            spot = positions[group * count + s]
            at = spot // (width_y * width_z) + HALO - slab * depth
            y, z = spot // width_z % width_y, spot % width_z

            @pl.when(jnp.logical_and(at >= first, at < first + planes))
            def _():
                row = y % groups * SUB + y // groups
                tile = pl.multiple_of(row // SUB * SUB, SUB)
                where = (z % chunks, pl.ds(tile, SUB), slice(None))
                inverse = coef[(6, at - (HALO - SWEEPS), *where)]
                hit = jnp.logical_and(sub_ids() == row - tile, lane_ids() == z // chunks)
                old = dst[(s, at, *where)]
                dst[(s, at, *where)] = old + jnp.where(hit, source_gain * inverse, 0.0)

        src, dst = dst, src


def early_kernel(positions, coef_own, own, near, coef, one, two, kap, mu):
    count, depth = own.shape[:2]
    slab = lax.axis_index("vox")
    parity = slab % 2
    copy_planes(coef_own, (0,), 0, kap, (), HALO, depth)
    copy_planes(near, (), 0, kap, (), halo_place(parity, True, depth, HALO), HALO)
    copy_planes(coef_own, (1,), 0, mu, (), SWEEPS, depth)
    copy_planes(near, (), HALO, mu, (), halo_place(parity, True, depth, SWEEPS), SWEEPS)
    coefficient_planes(slab, kap, mu, coef, *early_part(0, depth, parity), depth)
    for s in range(count):
        copy_planes(own, (s,), 0, one, (s,), HALO, depth)
        copy_planes(near, (), HALO + SWEEPS + s * HALO, one, (s,), halo_place(parity, True, depth, HALO), HALO)
    forward_sweeps(early_part, positions, coef, one, two, depth)


def forward_kernel(positions, one_in, two_in, coef_in, coef_own, far, *rest):
    totals, (cells, one, two, coef, forward, adjoint_source, kap, mu) = rest[:-8], rest[-8:]
    count, planes, chunks, width_y = one.shape[:4]
    depth = planes - 2 * HALO
    width_z, groups = chunks * LANES, width_y // SUB
    slab = lax.axis_index("vox")
    parity = slab % 2
    copy_planes(coef_own, (0,), 0, kap, (), HALO, depth)
    copy_planes(far, (), 0, kap, (), halo_place(parity, False, depth, HALO), HALO)
    copy_planes(coef_own, (1,), 0, mu, (), SWEEPS, depth)
    copy_planes(far, (), HALO, mu, (), halo_place(parity, False, depth, SWEEPS), SWEEPS)
    coefficient_planes(slab, kap, mu, coef, *late_part(0, depth, parity), depth)
    for s in range(count):
        copy_planes(far, (), HALO + SWEEPS + s * HALO, one, (s,), halo_place(parity, False, depth, HALO), HALO)
    forward_sweeps(late_part, positions, coef, one, two, depth)
    for s in range(count):
        copy_planes(one, (s,), HALO, forward, (s,), 0, depth + 1)
    local_cells = cells[...] - slab * (depth * width_y * width_z)
    row_mask, z_hot = detector_masks(local_cells, 0, depth, width_y, width_z)
    total = sum(part[...] for part in totals)
    for s in range(count):
        sampled = 0.0
        for j in range(chunks):
            field = one[s, pl.ds(HALO, depth), j].reshape(depth * width_y, LANES)
            for part in split(field):
                sampled = sampled + jnp.dot(part, z_hot[j], preferred_element_type=jnp.float32)
        predicted = jnp.sum(jnp.where(row_mask, sampled, 0.0), axis=0, keepdims=True)
        adjoint_source[pl.ds(s, 1), :] = predicted * total[s : s + 1] - total[count + s : count + s + 1]
    adjoint_source[pl.ds(count, 1), :] = local_cells.astype(jnp.float32)


def adjoint_first_kernel(coef, own, near, one, two):
    count, depth = own.shape[:2]
    parity = lax.axis_index("vox") % 2
    for s in range(count):
        copy_planes(own, (s,), 0, one, (s,), HALO, depth)
        copy_planes(near, (), s * HALO, one, (s,), halo_place(parity, True, depth, HALO), HALO)
    sweep_planes(coef, one, two, *early_part(0, depth, parity), None)


def add_sources(coef, source, bias, at, planes, moved):
    count, unused, chunks, width_y, lanes = bias.shape
    width_z = chunks * LANES
    cells = source[pl.ds(count, 1), :].astype(jnp.int32) + moved * (width_y * width_z)
    row_mask, z_hot = detector_masks(cells, at, planes, width_y, width_z)
    for s in range(count):
        spreads = [jnp.where(row_mask, part.astype(jnp.float32), 0.0).astype(jnp.bfloat16) for part in split(source[pl.ds(s, 1), :])]
        for j in range(chunks):
            placed = 0.0
            for spread in spreads:
                placed = placed + lax.dot_general(spread, z_hot[j], (((1,), (1,)), ((), ())), preferred_element_type=jnp.float32)
            placed = placed.reshape(planes, width_y, LANES)
            bias[s, pl.ds(at, planes), j] = placed * coef[6, pl.ds(at, planes), j]


def adjoint_early_kernel(one_in, two_in, coef, source, near_source, one, two, bias):
    count, planes, chunks, width_y = one.shape[:4]
    depth = planes - 2 * HALO
    parity = lax.axis_index("vox") % 2
    moved = SWEEPS + jnp.where(parity == 0, depth, -depth)
    add_sources(coef, near_source, bias, halo_place(parity, True, depth, SWEEPS), SWEEPS, moved)
    add_sources(coef, source, bias, SWEEPS, depth, SWEEPS)
    first, count_first = early_part(0, depth, parity)

    def add(n, carry):
        at = first + n
        for s in range(count):
            two[s, at] = two[s, at] + bias[s, at - (HALO - SWEEPS)]
        return carry

    lax.fori_loop(0, count_first, add, 0)
    src, dst = two, one
    for t in range(1, SWEEPS):
        sweep_planes(coef, src, dst, *early_part(t, depth, parity), bias)
        src, dst = dst, src


def places(order):
    found = [0]
    for bit in reversed(order):
        found = found + [place | 1 << bit for place in found]
    return found


def adjoint_kernel(orders, one_in, two_in, bias_in, coef, far, forward, far_source, one, two, bias, *rest):
    outs, plane_out = rest[:-1], rest[-1]
    count, planes, chunks, width_y = one.shape[:4]
    depth = planes - 2 * HALO
    groups = width_y // SUB
    parity, group = lax.axis_index("vox") % 2, lax.axis_index("src")
    for s in range(count):
        copy_planes(far, (), s * HALO, one, (s,), halo_place(parity, False, depth, HALO), HALO)
    moved = SWEEPS - jnp.where(parity == 0, depth, -depth)
    add_sources(coef, far_source, bias, halo_place(parity, False, depth, SWEEPS), SWEEPS, moved)
    src, dst = one, two
    for t in range(SWEEPS):
        sweep_planes(coef, src, dst, *late_part(t, depth, parity), bias)
        src, dst = dst, src
    lane, sub = lane_ids(), sub_ids()

    def steps(ref, s, at, mids, g):
        mid = mids[g]
        high = load_rows(ref, (s, at + 1), g, chunks)
        after = next_y(mids, g)
        if g + 1 == groups:
            after = [jnp.where(sub == SUB - 1, 0.0, c) for c in after]
        right = next_z(mid)
        right[-1] = jnp.where(lane == LANES - 1, 0.0, right[-1])
        return [[other[j] - mid[j] for j in range(chunks)] for other in (high, after, right)]

    tiles = 1 << len(orders[0])
    tile_rows = width_y // tiles

    def plane(p, carry):
        mids_f = [load_plane(forward, (s, p), groups, chunks) for s in range(count)]
        mids_a = [load_plane(src, (s, p + HALO), groups, chunks) for s in range(count)]
        for g in range(groups):
            mua_sum, kappa_sum = [0.0] * chunks, [0.0] * chunks
            for s in range(count):
                d_f = steps(forward, s, p, mids_f[s], g)
                d_a = steps(src, s, p + HALO, mids_a[s], g)
                for j in range(chunks):
                    mua_sum[j] = mua_sum[j] - mids_f[s][g][j] * mids_a[s][g][j]
                    for a, b in zip(d_f, d_a):
                        kappa_sum[j] = kappa_sum[j] - a[j] * b[j]
            for j in range(chunks):
                plane_out[0, j, pl.ds(g, SUB, stride=groups), :] = mua_sum[j]
                plane_out[1, j, pl.ds(g, SUB, stride=groups), :] = kappa_sum[j]
        for k, order in enumerate(orders):
            for i, place in enumerate(places(order)):
                out = outs[2 * k + (0 if i < tiles // 2 else 1)]
                first = pl.multiple_of((group ^ place) * tile_rows, SUB)
                for j in range(chunks):
                    out[i % (tiles // 2), p, j] = plane_out[k, j, pl.ds(first, tile_rows), :]
        return carry

    lax.fori_loop(0, depth, plane, 0)


def unpack_kernel(*refs):
    pairs, outs = refs[: -len(refs) // 3], refs[-(len(refs) // 3) :]
    depth, chunks, rows, lanes = pairs[0].shape
    order = z_order(chunks * LANES, 1)
    for k, out in enumerate(outs):
        total = pairs[2 * k][...] + pairs[2 * k + 1][...]
        total = jnp.concatenate([total[:, j].reshape(depth * rows, LANES) for j in range(chunks)], axis=1)
        natural = sum(jnp.dot(part, order, preferred_element_type=jnp.float32) for part in split(total))
        out[...] = natural.reshape(out.shape)


def measured_kernel(count, sources, detectors, data, weight, *outs):
    kinds, detector_count = outs[0].shape
    chunks, width = sources.shape
    total = jnp.zeros((len(outs) * kinds, detector_count), jnp.float32)
    detector_at = lax.broadcasted_iota(jnp.int32, (detector_count, width), 0) + lax.axis_index("vox") * detector_count
    kind_at = lax.broadcasted_iota(jnp.int32, (len(outs) * kinds, width), 0)
    source_at = (kind_at // kinds ^ lax.axis_index("src")) * count + kind_at % count
    with_data = kind_at % kinds >= count
    for i in range(chunks):
        row = pl.ds(i, 1)
        hot = (detector_at == detectors[row, :]).astype(jnp.bfloat16)
        w = weight[row, :]
        left = jnp.where(source_at == sources[row, :], jnp.where(with_data, w * data[row, :], w), 0.0)
        for part in split(left):
            total = total + lax.dot_general(part, hot, (((1,), (1,)), ((), ())), preferred_element_type=jnp.float32)
    for d, out in enumerate(outs):
        out[...] = total[d * kinds : (d + 1) * kinds]


VMEM = pl.BlockSpec(memory_space=pltpu.VMEM)
SMEM = pl.BlockSpec(memory_space=pltpu.SMEM)


def held(*shape):
    return pltpu.VMEM(shape, jnp.float32)


def call(kernel, outs, scratch, limit, *args, raw=(), positions=None, kept=0, after=()):
    args = [pltpu.with_memory_space_constraint(a, pltpu.VMEM) for a in args]
    args += [pltpu.with_memory_space_constraint(a, pltpu.HBM) for a in raw]
    specs = [VMEM] * len(args)
    if after:
        inner, used = kernel, len(args) + (positions is not None)
        kernel = lambda *refs: inner(*refs[:used], *refs[used + len(after) :])
        args += [pltpu.with_memory_space_constraint(a, pltpu.VMEM) for a in after]
        specs += [VMEM] * len(after)
    shift = 0
    if positions is not None:
        args, specs = [positions, *args], [SMEM, *specs]
        shift = 1
    return pl.pallas_call(
        kernel,
        out_shape=outs,
        in_specs=specs,
        out_specs=[VMEM] * len(outs),
        scratch_shapes=scratch,
        input_output_aliases={k + shift: k for k in range(kept)},
        compiler_params=pltpu.CompilerParams(vmem_limit_bytes=limit * 1024 * 1024),
        cost_estimate=pl.CostEstimate(flops=1, bytes_accessed=1, transcendentals=0),
    )(*args)


def near_swap(block, count):
    return lax.ppermute(block, "vox", [(i, i ^ 1) for i in range(count) if i ^ 1 < count])


def far_swap(block, count):
    pairs = [(i, i + 1) for i in range(1, count - 1, 2)]
    return lax.ppermute(block, "vox", pairs + [(b, a) for a, b in pairs])


def body(
    kappa,
    mua,
    prior_forward_fields,
    prior_adjoint_fields,
    source_position,
    detector_voxel,
    measured_source,
    measured_detector,
    measured_data,
    measured_weight,
):
    count, depth, width_y, width_z = prior_forward_fields.shape
    slabs, groups = lax.axis_size("vox"), lax.axis_size("src")
    detectors = detector_voxel.shape[0]
    f32 = jnp.float32
    plane = (width_z // LANES, width_y, LANES)

    def pack(kinds, *blocks, after=()):
        rim = held(sum(sum(widths) for widths in kinds), *plane)
        outs = [held(len(widths), depth, *plane) for widths in kinds] + [rim, rim]
        return call(functools.partial(pack_kernel, kinds), outs, [], 6, raw=blocks, after=after)

    def sides(near, far):
        return near_swap(near, slabs), far_swap(far, slabs)

    planes = depth + 2 * HALO
    field = held(count, planes, *plane)
    coef_held = held(7, planes - 2, *plane)
    coef_work = [held(planes, *plane), held(planes - 2, *plane)]

    field_rims = (HALO,) * count
    coef_own, fwd_own, near, far = pack([(HALO, SWEEPS), field_rims], kappa, mua, prior_forward_fields)
    near, far = sides(near, far)
    adj_own, adj_near, adj_far = pack([field_rims], prior_adjoint_fields, after=[near])
    adj_near, adj_far = sides(adj_near, adj_far)
    coef, one, two = call(
        early_kernel,
        [coef_held, field, field],
        coef_work,
        6,
        coef_own,
        fwd_own,
        near,
        positions=source_position,
        after=[adj_near],
    )
    rows = measured_source.shape[0]
    sums = call(
        functools.partial(measured_kernel, count),
        [held(2 * count, detectors)] * groups,
        [],
        2,
        raw=[a.reshape(rows // LANES, LANES) for a in (measured_source, measured_detector, measured_data, measured_weight)],
        after=[adj_near],
    )
    totals = [sums[0]] + [lax.ppermute(sums[d], "src", [(i, i ^ d) for i in range(groups)]) for d in range(1, groups)]
    unused, unused, coef, forward, source = call(
        forward_kernel,
        [field, field, coef_held, held(count, depth + 1, *plane), held(count + 1, detectors)],
        coef_work,
        6,
        one,
        two,
        coef,
        coef_own,
        far,
        *totals,
        raw=[detector_voxel.reshape(1, detectors)],
        positions=source_position,
        kept=3,
    )
    source_near, source_far = sides(source, source)
    one, two = call(adjoint_first_kernel, [field, field], [], 3, coef, adj_own, adj_near, after=[source])
    one, two, bias = call(
        adjoint_early_kernel,
        [field, field, held(count, planes - 2, *plane)],
        [],
        6,
        one,
        two,
        coef,
        source,
        source_near,
        kept=2,
    )
    bits = list(range(groups.bit_length() - 1))
    orders = (bits, bits[::-1])
    half = held(groups // 2, depth, plane[0], width_y // groups, LANES)
    unused, unused, unused, *parts = call(
        functools.partial(adjoint_kernel, orders),
        [field, field, held(count, planes - 2, *plane)] + [half] * 4,
        [held(2, *plane)],
        6,
        one,
        two,
        bias,
        coef,
        adj_far,
        forward,
        source_far,
        kept=3,
    )

    def swap(block, bit):
        return lax.ppermute(block, "src", [(i, i ^ 1 << bit) for i in range(groups)])

    kept, sent = [parts[0], parts[2]], [parts[1], parts[3]]
    for step in range(len(bits)):
        got = [swap(sent[k], orders[k][step]) for k in range(2)]
        if step + 1 < len(bits):
            total = [kept[k] + got[k] for k in range(2)]
            middle = total[0].shape[0] // 2
            kept, sent = [t[:middle] for t in total], [t[middle:] for t in total]
    tile = jax.ShapeDtypeStruct((depth, width_y // groups, width_z), f32)
    return tuple(call(unpack_kernel, [tile, tile], [], 3, kept[0][0], got[0][0], kept[1][0], got[1][0]))


def solution(mesh):
    in_specs = (
        P("vox", None, None),
        P("vox", None, None),
        P("src", "vox", None, None),
        P("src", "vox", None, None),
        P(),
        P("vox"),
        P(("src", "vox")),
        P(("src", "vox")),
        P(("src", "vox")),
        P(("src", "vox")),
    )
    out_specs = (P("vox", "src", None), P("vox", "src", None))
    return jax.shard_map(body, mesh=mesh, in_specs=in_specs, out_specs=out_specs, check_vma=False)
```

time: 107 us -> 66 us (0.62)
  Pallas kernels: 48.9 us -> 31.8 us
  other arithmetic: 11.3 us -> 0.07 us
  starting transfers between devices: 22.8 us -> 16 us
  local copies, waits for them, and re-layouts: 5.72 us -> 0.04 us
    pallas_call x4 -> x9, Pallas kernels: 48.9 us -> 31.8 us  [call(): pl.pallas_call(kernel, out_shape=outs, in_specs=specs, out_specs=[VMEM] *...]
    select_n x4 -> x0, other arithmetic: 7 us -> none  [rims(): return jnp.where(parity == first, high, low)]
    ppermute x4 -> x7, starting transfers between devices: 3.36 us -> 8 us  [the longest x4 4.49 us: swap(): lax.ppermute(block, 'src', [(i, i ^ 1 << bit) for i in range(groups)])]
    ppermute x5 -> x3, starting transfers between devices: 11.4 us -> 6.86 us  [far_swap(): return lax.ppermute(block, 'vox', pairs + [(b, a) for a, b in pairs])]
    all_to_all x1 -> x0, starting transfers between devices: 4.25 us -> none  [body(): lax.all_to_all(sums, 'src', split_axis=0, concat_axis=0, tiled=True)]
    ppermute x5 -> x3, starting transfers between devices: 3.82 us -> 1.12 us  [near_swap(): lax.ppermute(block, 'vox', [(i, i ^ 1) for i in range(count) if i ^ 1 < c...]
    all_to_all x1 -> x0, waiting for transfers between devices: 2.51 us -> none  [body(): lax.all_to_all(sums, 'src', split_axis=0, concat_axis=0, tiled=True)]
    dynamic_slice x5 -> x0, local copies, waits for them, and re-layouts: 2.24 us -> none  [the longest x2 2.13 us: tile_sum(): kept = lax.dynamic_index_in_dim(block, mine, dim, False)]
  transfers between devices with their start and end apart: 15 -> 13, of which waited for: 6 -> 5; matrix products, arithmetic and copies ran while one was open for 10% -> 0% of each run, Pallas kernels for 27% -> 34%
where the time goes in v2:
time: 66 us; the launch traced here: 65.8 us
  Pallas kernels  31.8 us (48%)
  waiting for transfers between devices  17.1 us (26%)
  starting transfers between devices  16 us (24%)
  between operations  0.78 us (1%)
    pallas_call x9, Pallas kernels, call(): pl.pallas_call(kernel, out_shape=outs, in_specs=specs, out_specs=[VMEM] *...  31.8 us
    ppermute x4, waiting for transfers between devices, swap(): lax.ppermute(block, 'src', [(i, i ^ 1 << bit) for i in range(groups)])  11.7 us
    ppermute x3, starting transfers between devices, far_swap(): return lax.ppermute(block, 'vox', pairs + [(b, a) for a, b in pairs])  6.86 us
    ppermute x4, starting transfers between devices, swap(): lax.ppermute(block, 'src', [(i, i ^ 1 << bit) for i in range(groups)])  4.49 us
    ppermute x3, waiting for transfers between devices, far_swap(): return lax.ppermute(block, 'vox', pairs + [(b, a) for a, b in pairs])  4.16 us
    ppermute x3, starting transfers between devices, body(): lax.ppermute(sums[d], 'src', [(i, i ^ d) for i in range(groups)])  3.51 us
  transfers between devices with their start and end apart: 13, of which 5 were waited for; matrix products, arithmetic and copies ran while one was open for 0% of the time, Pallas kernels for 34%

profile of v2, /device:TPU:10, one launch (start us, length us, event | category | flops | bytes accessed | tf_op | source)
XLA Modules:
  0.0 65.8 jit_solution(12155435807763953071)
XLA Ops:
  0.6 3.0 %shard_map.113 = (f32[2,8,2,64,128]{4,3,2,1,0:T(8,128)S(1)}, f32[2,8,2,64,128]{4,3,2,1,0:T(8,128)S(1)}, f32[27,2,64,128]{3,2,1,0:T(8,128)S(1)}, f32[27,2,64,128]{3,2,1,0:T(8,128)S(1)}) custom-call(f32[8,64,256]{2,1,0:T(8,128)} %refs_0_.3, f32[8,64,256]{2,1,0:T(8,128)} %refs_1_.1, f32[2,8,64,256]{3,2,1,0:T(8,128)} %refs_2_.1), custom_call_target="tpu_custom_call" | custom-call | flops 1 | bytes 1 | tf_op jit(solution)/shard_map/pallas_call | solution.py:441
  3.7 0.1 collective-permute-start
  3.8 2.4 %collective-permute-start.2 = (f32[27,2,64,128]{3,2,1,0:T(8,128)S(1)}, f32[27,2,64,128]{3,2,1,0:T(8,128)S(1)}, u32[]{:S(2)}, u32[]{:S(2)}) collective-permute-start(f32[27,2,64,128]{3,2,1,0:T(8,128)S(1)} %get-tuple-element.35), channel_id=1, source_target_pairs={{1,2},{3,4},{5,6},{2,1},{4,3},{6,5},{9,10},{11,12},{13,14},{10,9},... | collective-permute-start | bytes 5308424 | tf_op jit(solution)/shard_map/ppermute | solution.py:459
  6.2 1.2 %collective-permute-done.refs_1_.refs_3_ = f32[27,2,64,128]{3,2,1,0:T(8,128)S(1)} collective-permute-done((f32[27,2,64,128]{3,2,1,0:T(8,128)S(1)}, f32[27,2,64,128]{3,2,1,0:T(8,128)S(1)}, u32[]{:S(2)}, u32[]{:S(2)}) %collective-permute-start) | collective-permute-done | bytes 1769504 | tf_op jit(solution)/shard_map/ppermute | solution.py:454
  7.4 2.1 %shard_map.114 = (f32[2,8,2,64,128]{4,3,2,1,0:T(8,128)S(1)}, f32[14,2,64,128]{3,2,1,0:T(8,128)S(1)}, f32[14,2,64,128]{3,2,1,0:T(8,128)S(1)}) custom-call(f32[2,8,64,256]{3,2,1,0:T(8,128)} %refs_0_.4, f32[27,2,64,128]{3,2,1,0:T(8,128)S(1)} %collective-permute-done.refs_1_.refs_3_), custom_call_target="tpu_custom_call" | custom-call | flops 1 | bytes 1 | tf_op jit(solution)/shard_map/pallas_call | solution.py:441
  9.5 0.2 collective-permute-start.1
  9.7 2.3 %collective-permute-start.7 = (f32[14,2,64,128]{3,2,1,0:T(8,128)S(1)}, f32[14,2,64,128]{3,2,1,0:T(8,128)S(1)}, u32[]{:S(2)}, u32[]{:S(2)}) collective-permute-start(f32[14,2,64,128]{3,2,1,0:T(8,128)S(1)} %get-tuple-element.48), channel_id=1, source_target_pairs={{1,2},{3,4},{5,6},{2,1},{4,3},{6,5},{9,10},{11,12},{13,14},{10,9},... | collective-permute-start | bytes 2752520 | tf_op jit(solution)/shard_map/ppermute | solution.py:459
  12.0 0.0 collective-permute-done.1.refs_4_.refs_2_
  12.0 1.2 %shard_map.116 = (f32[4,128]{1,0:T(4,128)S(1)}, f32[4,128]{1,0:T(4,128)S(1)}, f32[4,128]{1,0:T(4,128)S(1)}, f32[4,128]{1,0:T(4,128)S(1)}) custom-call(s32[8,128]{1,0:T(8,128)} %bitcast.13, s32[8,128]{1,0:T(8,128)} %bitcast.14, f32[8,128]{1,0:T(8,128)} %bitcast.15, f32[8,128]{1,0:T(8,128)} %bitcast.16, ...), custom_call_target="tpu_custom_call" | custom-call | flops 1 | bytes 1 | tf_op jit(solution)/shard_map/pallas_call | solution.py:441
  13.3 0.6 collective-permute-start.3
  13.8 1.5 %collective-permute-start.4 = (f32[4,128]{1,0:T(4,128)S(1)}, f32[4,128]{1,0:T(4,128)S(1)}, u32[]{:S(2)}, u32[]{:S(2)}) collective-permute-start(f32[4,128]{1,0:T(4,128)S(1)} %get-tuple-element.38), channel_id=1, source_target_pairs={{0,16},{8,24},{16,0},{24,8},{1,17},{9,25},{17,1},{25,9},{2,18},{10... | collective-permute-start | bytes 6152 | tf_op jit(solution)/shard_map/ppermute | solution.py:518
  15.4 1.4 %collective-permute-start.5 = (f32[4,128]{1,0:T(4,128)S(1)}, f32[4,128]{1,0:T(4,128)S(1)}, u32[]{:S(2)}, u32[]{:S(2)}) collective-permute-start(f32[4,128]{1,0:T(4,128)S(1)} %get-tuple-element.39), channel_id=1, source_target_pairs={{0,24},{8,16},{16,8},{24,0},{1,25},{9,17},{17,9},{25,1},{2,26},{10... | collective-permute-start | bytes 6152 | tf_op jit(solution)/shard_map/ppermute | solution.py:518
  16.8 6.6 %shard_map.115 = (f32[7,20,2,64,128]{4,3,2,1,0:T(8,128)S(1)}, f32[2,22,2,64,128]{4,3,2,1,0:T(8,128)S(1)}, f32[2,22,2,64,128]{4,3,2,1,0:T(8,128)S(1)}) custom-call(s32[8]{0:T(128)S(1)} %copy-done, f32[2,8,2,64,128]{4,3,2,1,0:T(8,128)S(1)} %get-tuple-element.28.refs_1_.coef_own, f32[2,8,2,64,128]{4,3,2,1,0:T(8,128)S(1)} %get-tuple-element.29.refs_2_, ...), custom_call_target="tpu_custom_call" | custom-call | flops 1 | bytes 1 | tf_op jit(solution)/shard_map/pallas_call | solution.py:441
  23.5 4.2 %collective-permute-done.2.far = f32[27,2,64,128]{3,2,1,0:T(8,128)S(1)} collective-permute-done((f32[27,2,64,128]{3,2,1,0:T(8,128)S(1)}, f32[27,2,64,128]{3,2,1,0:T(8,128)S(1)}, u32[]{:S(2)}, u32[]{:S(2)}) %collective-permute-start.2) | collective-permute-done | bytes 1769504 | tf_op jit(solution)/shard_map/ppermute | solution.py:459
  27.6 0.0 collective-permute-done.3.rest_1_
  27.6 0.0 collective-permute-done.4.rest_2_
  27.6 0.0 collective-permute-done.5.rest_3_
  27.6 6.3 %shard_map.117 = (f32[2,22,2,64,128]{4,3,2,1,0:T(8,128)S(1)}, f32[2,22,2,64,128]{4,3,2,1,0:T(8,128)S(1)}, f32[7,20,2,64,128]{4,3,2,1,0:T(8,128)S(1)}, f32[2,9,2,64,128]{4,3,2,1,0:T(8,128)S(1)}, f32[3,128]{1,0:T(4,128)S(1)}) custom-call(s32[8]{0:T(128)S(1)} %copy-done, ...), custom_call_target="tpu_custom_call", output_to_operand_aliasing={{0}: (1, {}), {1}: (2, {}), {2}: (3, {})} | custom-call | flops 1 | bytes 1 | tf_op jit(solution)/shard_map/pallas_call | solution.py:441
  33.9 0.8 %collective-permute-start.6 = (f32[3,128]{1,0:T(4,128)S(1)}, f32[3,128]{1,0:T(4,128)S(1)}, u32[]{:S(2)}, u32[]{:S(2)}) collective-permute-start(f32[3,128]{1,0:T(4,128)S(1)} %get-tuple-element.42.refs_3_.source), channel_id=1, source_target_pairs={{0,1},{1,0},{2,3},{3,2},{4,5},{5,4},{6,7},{7,6},{8,9},{9,8},{10,11... | collective-permute-start | bytes 4616 | tf_op jit(solution)/shard_map/ppermute | solution.py:454
  34.7 2.1 %collective-permute-start.8 = (f32[3,128]{1,0:T(4,128)S(1)}, f32[3,128]{1,0:T(4,128)S(1)}, u32[]{:S(2)}, u32[]{:S(2)}) collective-permute-start(f32[3,128]{1,0:T(4,128)S(1)} %get-tuple-element.42.refs_3_.source), channel_id=1, source_target_pairs={{1,2},{3,4},{5,6},{2,1},{4,3},{6,5},{9,10},{11,12},{13,14},{10,9},... | collective-permute-start | bytes 4616 | tf_op jit(solution)/shard_map/ppermute | solution.py:459
  36.8 1.3 %shard_map.118 = (f32[2,22,2,64,128]{4,3,2,1,0:T(8,128)S(1)}, f32[2,22,2,64,128]{4,3,2,1,0:T(8,128)S(1)}) custom-call(f32[7,20,2,64,128]{4,3,2,1,0:T(8,128)S(1)} %get-tuple-element.40.refs_0_.coef, f32[2,8,2,64,128]{4,3,2,1,0:T(8,128)S(1)} %get-tuple-element.41.refs_1_, f32[14,2,64,128]{3,2,1,0:T(8,128)S(1)} %collective-permute-done.1.refs_4_.refs_2_, ...), custom_call_target="tpu_custom_call" | custom-call | flops 1 | bytes 1 | tf_op jit(solution)/shard_map/pallas_call | solution.py:441
  38.1 4.7 %shard_map.119 = (f32[2,22,2,64,128]{4,3,2,1,0:T(8,128)S(1)}, f32[2,22,2,64,128]{4,3,2,1,0:T(8,128)S(1)}, f32[2,20,2,64,128]{4,3,2,1,0:T(8,128)S(1)}) custom-call(f32[2,22,2,64,128]{4,3,2,1,0:T(8,128)S(1)} %get-tuple-element.43.one_in, f32[2,22,2,64,128]{4,3,2,1,0:T(8,128)S(1)} %get-tuple-element.44.two_in, ...), custom_call_target="tpu_custom_call", output_to_operand_aliasing={{0}: (0, {}), {1}: (1, {})} | custom-call | flops 1 | bytes 1 | tf_op jit(solution)/shard_map/pallas_call | solution.py:441
  42.8 0.0 collective-permute-done.8.far_source
  42.8 5.7 %shard_map.120 = (f32[2,22,2,64,128]{4,3,2,1,0:T(8,128)S(1)}, f32[2,22,2,64,128]{4,3,2,1,0:T(8,128)S(1)}, f32[2,20,2,64,128]{4,3,2,1,0:T(8,128)S(1)}, f32[2,8,2,...) custom-call(f32[2,22,2,64,128]{4,3,2,1,0:T(8,128)S(1)} %get-tuple-el, ...), custom_call_target="tpu_custom_call", output_to_operand_aliasing={{0}: (0, {}), {1}: (1, {}), {2}: (2, {})} | custom-call | flops 1 | bytes 1 | tf_op jit(solution)/shard_map/pallas_call | solution.py:441
  48.4 0.7 %collective-permute-start.9 = (f32[2,8,2,16,128]{4,3,2,1,0:T(8,128)S(1)}, f32[2,8,2,16,128]{4,3,2,1,0:T(8,128)S(1)}, u32[]{:S(2)}, u32[]{:S(2)}) collective-permute-start(f32[2,8,2,16,128]{4,3,2,1,0:T(8,128)S(1)} %get-tuple-element.51), channel_id=1, source_target_pairs={{0,8},{8,0},{16,24},{24,16},{1,9},{9,1},{17,25},{25,17},{2,10},{10... | collective-permute-start | bytes 786440 | tf_op jit(solution)/shard_map/ppermute | solution.py:567
  49.1 1.5 %collective-permute-start.11 = (f32[2,8,2,16,128]{4,3,2,1,0:T(8,128)S(1)}, f32[2,8,2,16,128]{4,3,2,1,0:T(8,128)S(1)}, u32[]{:S(2)}, u32[]{:S(2)}) collective-permute-start(f32[2,8,2,16,128]{4,3,2,1,0:T(8,128)S(1)} %get-tuple-element.53), channel_id=1, source_target_pairs={{0,16},{8,24},{16,0},{24,8},{1,17},{9,25},{17,1},{25,9},{2,18},{10... | collective-permute-start | bytes 786440 | tf_op jit(solution)/shard_map/ppermute | solution.py:567
  50.6 6.4 %collective-permute-done.9 = f32[2,8,2,16,128]{4,3,2,1,0:T(8,128)S(1)} collective-permute-done((f32[2,8,2,16,128]{4,3,2,1,0:T(8,128)S(1)}, f32[2,8,2,16,128]{4,3,2,1,0:T(8,128)S(1)}, u32[]{:S(2)}, u32[]{:S(2)}) %collective-permute-start.9) | collective-permute-done | bytes 262176 | tf_op jit(solution)/shard_map/ppermute | solution.py:567
  57.1 1.7 %collective-permute-start.10 = (f32[1,8,2,16,128]{4,3,2,1,0:T(8,128)S(1)}, f32[1,8,2,16,128]{4,3,2,1,0:T(8,128)S(1)}, u32[]{:S(2)}, u32[]{:S(2)}) collective-permute-start(f32[1,8,2,16,128]{4,3,2,1,0:T(8,128)S(1)} %get-tuple-element.56), channel_id=1, source_target_pairs={{0,16},{8,24},{16,0},{24,8},{1,17},{9,25},{17,1},{25,9},{2,18},{10... | collective-permute-start | bytes 393224 | tf_op jit(solution)/shard_map/ppermute | solution.py:567
  58.9 0.6 collective-permute-start.12
  59.5 3.8 %collective-permute-done.10 = f32[1,8,2,16,128]{4,3,2,1,0:T(8,128)S(1)} collective-permute-done((f32[1,8,2,16,128]{4,3,2,1,0:T(8,128)S(1)}, f32[1,8,2,16,128]{4,3,2,1,0:T(8,128)S(1)}, u32[]{:S(2)}, u32[]{:S(2)}) %collective-permute-start.10) | collective-permute-done | bytes 131104 | tf_op jit(solution)/shard_map/ppermute | solution.py:567
  63.3 1.4 %collective-permute-done.12 = f32[1,8,2,16,128]{4,3,2,1,0:T(8,128)S(1)} collective-permute-done((f32[1,8,2,16,128]{4,3,2,1,0:T(8,128)S(1)}, f32[1,8,2,16,128]{4,3,2,1,0:T(8,128)S(1)}, u32[]{:S(2)}, u32[]{:S(2)}) %collective-permute-start.12) | collective-permute-done | bytes 131104 | tf_op jit(solution)/shard_map/ppermute | solution.py:567
  64.8 1.0 %shard_map.121 = (f32[8,16,256]{2,1,0:T(8,128)}, f32[8,16,256]{2,1,0:T(8,128)}) custom-call(f32[8,2,16,128]{3,2,1,0:T(8,128)S(1)} %get-tuple-element.57.refs_0_, f32[8,2,16,128]{3,2,1,0:T(8,128)S(1)} %bitcast.11, f32[8,2,16,128]{3,2,1,0:T(8,128)S(1)} %get-tuple-element.55.refs_2_, f32[8,2,16,128]{3,2,1,0:T(8,128)S(1)} %bitcast.12), custom_call_target="tpu_custom_call" | custom-call | flops 1 | bytes 1 | tf_op jit(solution)/shard_map/pallas_call | solution.py:441
  (9 shorter events, 0.1 us)
Async XLA Ops:
  0.6 16.2 %copy-start = (s32[8]{0:T(128)S(1)}, s32[8]{0:T(128)}, u32[]{:S(2)}) copy-start(s32[8]{0:T(128)} %positions.1) | copy-start | bytes 100
  3.7 3.8 %collective-permute-start = (f32[27,2,64,128]{3,2,1,0:T(8,128)S(1)}, f32[27,2,64,128]{3,2,1,0:T(8,128)S(1)}, u32[]{:S(2)}, u32[]{:S(2)}) collective-permute-start(f32[27,2,64,128]{3,2,1,0:T(8,128)S(1)} %get-tuple-element.30), channel_id=1, source_target_pairs={{0,1},{1,0},{2,3},{3,2},{4,5},{5,4},{6,7},{7,6},{8,9},{9,8},{10,11... | collective-permute-start | bytes 5308424 | tf_op jit(solution)/shard_map/ppermute | solution.py:454
  3.8 23.8 %collective-permute-start.2 = (f32[27,2,64,128]{3,2,1,0:T(8,128)S(1)}, f32[27,2,64,128]{3,2,1,0:T(8,128)S(1)}, u32[]{:S(2)}, u32[]{:S(2)}) collective-permute-start(f32[27,2,64,128]{3,2,1,0:T(8,128)S(1)} %get-tuple-element.35), channel_id=1, source_target_pairs={{1,2},{3,4},{5,6},{2,1},{4,3},{6,5},{9,10},{11,12},{13,14},{10,9},... | collective-permute-start | bytes 5308424 | tf_op jit(solution)/shard_map/ppermute | solution.py:459
  9.5 2.5 %collective-permute-start.1 = (f32[14,2,64,128]{3,2,1,0:T(8,128)S(1)}, f32[14,2,64,128]{3,2,1,0:T(8,128)S(1)}, u32[]{:S(2)}, u32[]{:S(2)}) collective-permute-start(f32[14,2,64,128]{3,2,1,0:T(8,128)S(1)} %get-tuple-element.31), channel_id=1, source_target_pairs={{0,1},{1,0},{2,3},{3,2},{4,5},{5,4},{6,7},{7,6},{8,9},{9,8},{10,11... | collective-permute-start | bytes 2752520 | tf_op jit(solution)/shard_map/ppermute | solution.py:454
  9.7 33.1 %collective-permute-start.7 = (f32[14,2,64,128]{3,2,1,0:T(8,128)S(1)}, f32[14,2,64,128]{3,2,1,0:T(8,128)S(1)}, u32[]{:S(2)}, u32[]{:S(2)}) collective-permute-start(f32[14,2,64,128]{3,2,1,0:T(8,128)S(1)} %get-tuple-element.48), channel_id=1, source_target_pairs={{1,2},{3,4},{5,6},{2,1},{4,3},{6,5},{9,10},{11,12},{13,14},{10,9},... | collective-permute-start | bytes 2752520 | tf_op jit(solution)/shard_map/ppermute | solution.py:459
  13.3 14.3 %collective-permute-start.3 = (f32[4,128]{1,0:T(4,128)S(1)}, f32[4,128]{1,0:T(4,128)S(1)}, u32[]{:S(2)}, u32[]{:S(2)}) collective-permute-start(f32[4,128]{1,0:T(4,128)S(1)} %get-tuple-element.37), channel_id=1, source_target_pairs={{0,8},{8,0},{16,24},{24,16},{1,9},{9,1},{17,25},{25,17},{2,10},{10... | collective-permute-start | bytes 6152 | tf_op jit(solution)/shard_map/ppermute | solution.py:518
  13.8 13.8 %collective-permute-start.4 = (f32[4,128]{1,0:T(4,128)S(1)}, f32[4,128]{1,0:T(4,128)S(1)}, u32[]{:S(2)}, u32[]{:S(2)}) collective-permute-start(f32[4,128]{1,0:T(4,128)S(1)} %get-tuple-element.38), channel_id=1, source_target_pairs={{0,16},{8,24},{16,0},{24,8},{1,17},{9,25},{17,1},{25,9},{2,18},{10... | collective-permute-start | bytes 6152 | tf_op jit(solution)/shard_map/ppermute | solution.py:518
  15.4 12.2 %collective-permute-start.5 = (f32[4,128]{1,0:T(4,128)S(1)}, f32[4,128]{1,0:T(4,128)S(1)}, u32[]{:S(2)}, u32[]{:S(2)}) collective-permute-start(f32[4,128]{1,0:T(4,128)S(1)} %get-tuple-element.39), channel_id=1, source_target_pairs={{0,24},{8,16},{16,8},{24,0},{1,25},{9,17},{17,9},{25,1},{2,26},{10... | collective-permute-start | bytes 6152 | tf_op jit(solution)/shard_map/ppermute | solution.py:518
  33.9 4.2 %collective-permute-start.6 = (f32[3,128]{1,0:T(4,128)S(1)}, f32[3,128]{1,0:T(4,128)S(1)}, u32[]{:S(2)}, u32[]{:S(2)}) collective-permute-start(f32[3,128]{1,0:T(4,128)S(1)} %get-tuple-element.42.refs_3_.source), channel_id=1, source_target_pairs={{0,1},{1,0},{2,3},{3,2},{4,5},{5,4},{6,7},{7,6},{8,9},{9,8},{10,11... | collective-permute-start | bytes 4616 | tf_op jit(solution)/shard_map/ppermute | solution.py:454
  34.7 8.0 %collective-permute-start.8 = (f32[3,128]{1,0:T(4,128)S(1)}, f32[3,128]{1,0:T(4,128)S(1)}, u32[]{:S(2)}, u32[]{:S(2)}) collective-permute-start(f32[3,128]{1,0:T(4,128)S(1)} %get-tuple-element.42.refs_3_.source), channel_id=1, source_target_pairs={{1,2},{3,4},{5,6},{2,1},{4,3},{6,5},{9,10},{11,12},{13,14},{10,9},... | collective-permute-start | bytes 4616 | tf_op jit(solution)/shard_map/ppermute | solution.py:459
  48.4 8.5 %collective-permute-start.9 = (f32[2,8,2,16,128]{4,3,2,1,0:T(8,128)S(1)}, f32[2,8,2,16,128]{4,3,2,1,0:T(8,128)S(1)}, u32[]{:S(2)}, u32[]{:S(2)}) collective-permute-start(f32[2,8,2,16,128]{4,3,2,1,0:T(8,128)S(1)} %get-tuple-element.51), channel_id=1, source_target_pairs={{0,8},{8,0},{16,24},{24,16},{1,9},{9,1},{17,25},{25,17},{2,10},{10... | collective-permute-start | bytes 786440 | tf_op jit(solution)/shard_map/ppermute | solution.py:567
  49.1 9.7 %collective-permute-start.11 = (f32[2,8,2,16,128]{4,3,2,1,0:T(8,128)S(1)}, f32[2,8,2,16,128]{4,3,2,1,0:T(8,128)S(1)}, u32[]{:S(2)}, u32[]{:S(2)}) collective-permute-start(f32[2,8,2,16,128]{4,3,2,1,0:T(8,128)S(1)} %get-tuple-element.53), channel_id=1, source_target_pairs={{0,16},{8,24},{16,0},{24,8},{1,17},{9,25},{17,1},{25,9},{2,18},{10... | collective-permute-start | bytes 786440 | tf_op jit(solution)/shard_map/ppermute | solution.py:567
  57.1 6.3 %collective-permute-start.10 = (f32[1,8,2,16,128]{4,3,2,1,0:T(8,128)S(1)}, f32[1,8,2,16,128]{4,3,2,1,0:T(8,128)S(1)}, u32[]{:S(2)}, u32[]{:S(2)}) collective-permute-start(f32[1,8,2,16,128]{4,3,2,1,0:T(8,128)S(1)} %get-tuple-element.56), channel_id=1, source_target_pairs={{0,16},{8,24},{16,0},{24,8},{1,17},{9,25},{17,1},{25,9},{2,18},{10... | collective-permute-start | bytes 393224 | tf_op jit(solution)/shard_map/ppermute | solution.py:567
  58.9 5.9 %collective-permute-start.12 = (f32[1,8,2,16,128]{4,3,2,1,0:T(8,128)S(1)}, f32[1,8,2,16,128]{4,3,2,1,0:T(8,128)S(1)}, u32[]{:S(2)}, u32[]{:S(2)}) collective-permute-start(f32[1,8,2,16,128]{4,3,2,1,0:T(8,128)S(1)} %get-tuple-element.54), channel_id=1, source_target_pairs={{0,8},{8,0},{16,24},{24,16},{1,9},{9,1},{17,25},{25,17},{2,10},{10... | collective-permute-start | bytes 393224 | tf_op jit(solution)/shard_map/ppermute | solution.py:567

commit v3 on v2

--- a/solution.py
+++ b/solution.py
@@ -59,10 +59,7 @@
 
 def split(values):
     high = values.astype(jnp.bfloat16)
-    rest = values - high.astype(jnp.float32)
-    middle = rest.astype(jnp.bfloat16)
-    low = (rest - middle.astype(jnp.float32)).astype(jnp.bfloat16)
-    return high, middle, low
+    return high, (values - high.astype(jnp.float32)).astype(jnp.bfloat16)
 
 
 def z_order(width_z, natural_dim):
@@ -73,11 +70,16 @@
 
 
 def pack_kernel(kinds, *refs):
-    owns, (near, far) = refs[-2 - len(kinds) : -2], refs[-2:]
-    blocks = []
-    for ref in refs[: -2 - len(kinds)]:
-        blocks += [ref] if ref.ndim == 3 else [ref.at[b] for b in range(ref.shape[0])]
-    depth, width_y, width_z = blocks[0].shape
+    (near, far, buffers, arrived), refs = refs[-4:], refs[:-4]
+    owns, fetched = refs[-len(kinds) :], refs[: -len(kinds)]
+    sources = []
+    for ref in fetched:
+        sources += [ref] if len(ref.shape) == 3 else [ref.at[b] for b in range(ref.shape[0])]
+    copies = [pltpu.make_async_copy(ref, buffers.at[b], arrived.at[b]) for b, ref in enumerate(sources)]
+    for copy in copies:
+        copy.start()
+    blocks = [buffers.at[b] for b in range(len(sources))]
+    depth, width_y, width_z = buffers.shape[1:]
     chunks, groups = width_z // LANES, width_y // SUB
     parity = lax.axis_index("vox") % 2
     order = z_order(width_z, 0)
@@ -86,6 +88,7 @@
     for own, widths in zip(owns, kinds):
         for b, width in enumerate(widths):
             block = blocks.pop(0)
+            copies.pop(0).wait()
             for first in range(0, depth, together):
                 values = block[pl.ds(first, together)].reshape(together * width_y, width_z)
                 packed = sum(jnp.dot(part, order, preferred_element_type=jnp.float32) for part in split(values))
@@ -106,7 +109,9 @@
 
 
 def early_part(t, depth, parity):
-    return jnp.where(parity == 0, HALO + 1 + t, 1 + t), depth + HALO - 2 - 2 * t
+    planes = depth + HALO - 2 - 2 * t
+    more = 1 if t > 0 and planes % 4 == 3 else 0
+    return jnp.where(parity == 0, HALO + 1 + t, 1 + t - more), planes + more
 
 
 def late_part(t, depth, parity):
@@ -162,20 +167,21 @@
     lax.fori_loop(0, count, plane, 0)
 
 
-def sweep_planes(coef, src, dst, first, planes, bias):
+def sweep_planes(coef, src, dst, first, planes, bias, together=4):
     count, unused, chunks, width_y, lanes = src.shape
     groups = width_y // SUB
 
     def one(at):
         c_at = at - (HALO - SWEEPS)
-        mids = [load_plane(src, (s, at), groups, chunks) for s in range(count)]
         for g in range(groups):
             faces = [load_rows(coef, (k, c_at), g, chunks) for k in range(6)]
             for s in range(count):
-                mid = mids[s][g]
+                rows = {h: load_rows(src, (s, at), h % groups, chunks) for h in (g - 1, g, g + 1)}
+                mid = rows[g]
                 low = load_rows(src, (s, at - 1), g, chunks)
                 high = load_rows(src, (s, at + 1), g, chunks)
-                before, after = prev_y(mids[s], g), next_y(mids[s], g)
+                before = rows[g - 1] if g > 0 else [pltpu.roll(c, 1, 0) for c in rows[g - 1]]
+                after = rows[g + 1] if g + 1 < groups else [pltpu.roll(c, SUB - 1, 0) for c in rows[g + 1]]
                 left, right = prev_z(mid), next_z(mid)
                 result = []
                 for j in range(chunks):
@@ -188,14 +194,15 @@
                     result = [a + b for a, b in zip(result, extra)]
                 store_rows(dst, (s, at), g, result)
 
-    def pair(i, carry):
-        one(first + 2 * i)
-        one(first + 2 * i + 1)
+    def several(i, carry):
+        for k in range(together):
+            one(first + together * i + k)
         return carry
 
-    lax.fori_loop(0, planes // 2, pair, 0)
-    if planes % 2:
-        one(first + planes - 1)
+    if planes >= together:
+        lax.fori_loop(0, planes // together, several, 0)
+    for k in range(planes // together * together, planes):
+        one(first + k)
 
 
 def detector_masks(cells, first, planes, width_y, width_z):
@@ -207,33 +214,50 @@
     return row_at == row, [(lane_at * chunks + j == z).astype(jnp.bfloat16) for j in range(chunks)]
 
 
-def forward_sweeps(part, positions, coef, one, two, depth):
-    count, unused, chunks, width_y, lanes = one.shape
+def find_sources(positions, spots, count, depth, chunks, width_y):
     width_z, groups = chunks * LANES, width_y // SUB
     slab, group = lax.axis_index("vox"), lax.axis_index("src")
-    src, dst = one, two
-    for t in range(SWEEPS):
-        first, planes = part(t, depth, slab % 2)
-        sweep_planes(coef, src, dst, first, planes, None)
-        for s in range(count):
-            spot = positions[group * count + s]
-            at = spot // (width_y * width_z) + HALO - slab * depth
-            y, z = spot // width_z % width_y, spot % width_z
-
-            @pl.when(jnp.logical_and(at >= first, at < first + planes))
-            def _():
-                row = y % groups * SUB + y // groups
-                tile = pl.multiple_of(row // SUB * SUB, SUB)
-                where = (z % chunks, pl.ds(tile, SUB), slice(None))
-                inverse = coef[(6, at - (HALO - SWEEPS), *where)]
-                hit = jnp.logical_and(sub_ids() == row - tile, lane_ids() == z // chunks)
-                old = dst[(s, at, *where)]
-                dst[(s, at, *where)] = old + jnp.where(hit, source_gain * inverse, 0.0)
-
-        src, dst = dst, src
-
-
-def early_kernel(positions, coef_own, own, near, coef, one, two, kap, mu):
+    for s in range(count):
+        spot = positions[group * count + s]
+        y, z = spot // width_z % width_y, spot % width_z
+        spots[s, 0] = spot // (width_y * width_z) + HALO - slab * depth
+        spots[s, 1] = z % chunks
+        spots[s, 2] = y % groups
+        spots[s, 3] = y // groups
+        spots[s, 4] = z // chunks
+
+
+def forward_sweep(part, spots, coef, src, dst, t, depth, together):
+    parity = lax.axis_index("vox") % 2
+    first, planes = part(t, depth, parity)
+    sweep_planes(coef, src, dst, first, planes, None, together)
+    for s in range(src.shape[0]):
+        at = spots[s, 0]
+
+        @pl.when(jnp.logical_and(at >= first, at < first + planes))
+        def _():
+            where = (spots[s, 1], pl.ds(pl.multiple_of(spots[s, 2] * SUB, SUB), SUB), slice(None))
+            inverse = coef[(6, at - (HALO - SWEEPS), *where)]
+            hit = jnp.logical_and(sub_ids() == spots[s, 3], lane_ids() == spots[s, 4])
+            dst[(s, at, *where)] = dst[(s, at, *where)] + jnp.where(hit, source_gain * inverse, 0.0)
+
+
+def early_sweeps(sweep, one, two, begin):
+    for t in range(begin, SWEEPS):
+        src, dst = (one, two) if t % 2 == 0 else (two, one)
+        sweep(early_part, src, dst, t, 4)
+
+
+def late_sweeps(sweep, one, two):
+    def step(i, carry):
+        sweep(late_part, one, two, 2 * i, HALO)
+        sweep(late_part, two, one, 2 * i + 1, HALO)
+        return carry
+
+    lax.fori_loop(0, SWEEPS // 2, step, 0)
+
+
+def early_kernel(positions, coef_own, own, near, coef, one, two, kap, mu, spots):
     count, depth = own.shape[:2]
     slab = lax.axis_index("vox")
     parity = slab % 2
@@ -245,11 +269,16 @@
     for s in range(count):
         copy_planes(own, (s,), 0, one, (s,), HALO, depth)
         copy_planes(near, (), HALO + SWEEPS + s * HALO, one, (s,), halo_place(parity, True, depth, HALO), HALO)
-    forward_sweeps(early_part, positions, coef, one, two, depth)
+    find_sources(positions, spots, count, depth, *own.shape[2:4])
+
+    def sweep(part, src, dst, t, together):
+        forward_sweep(part, spots, coef, src, dst, t, depth, together)
+
+    early_sweeps(sweep, one, two, 0)
 
 
 def forward_kernel(positions, one_in, two_in, coef_in, coef_own, far, *rest):
-    totals, (cells, one, two, coef, forward, adjoint_source, kap, mu) = rest[:-8], rest[-8:]
+    totals, (cells, one, two, coef, forward, adjoint_source, kap, mu, spots) = rest[:-9], rest[-9:]
     count, planes, chunks, width_y = one.shape[:4]
     depth = planes - 2 * HALO
     width_z, groups = chunks * LANES, width_y // SUB
@@ -262,7 +291,12 @@
     coefficient_planes(slab, kap, mu, coef, *late_part(0, depth, parity), depth)
     for s in range(count):
         copy_planes(far, (), HALO + SWEEPS + s * HALO, one, (s,), halo_place(parity, False, depth, HALO), HALO)
-    forward_sweeps(late_part, positions, coef, one, two, depth)
+    find_sources(positions, spots, count, depth, chunks, width_y)
+
+    def sweep(part, src, dst, t, together):
+        forward_sweep(part, spots, coef, src, dst, t, depth, together)
+
+    late_sweeps(sweep, one, two)
     for s in range(count):
         copy_planes(one, (s,), HALO, forward, (s,), 0, depth + 1)
     local_cells = cells[...] - slab * (depth * width_y * width_z)
@@ -279,7 +313,7 @@
     adjoint_source[pl.ds(count, 1), :] = local_cells.astype(jnp.float32)
 
 
-def adjoint_first_kernel(coef, own, near, one, two):
+def adjoint_first_kernel(coef, own, near, two, one):
     count, depth = own.shape[:2]
     parity = lax.axis_index("vox") % 2
     for s in range(count):
@@ -303,7 +337,7 @@
             bias[s, pl.ds(at, planes), j] = placed * coef[6, pl.ds(at, planes), j]
 
 
-def adjoint_early_kernel(one_in, two_in, coef, source, near_source, one, two, bias):
+def adjoint_early_kernel(two_in, coef, source, near_source, two, one, bias):
     count, planes, chunks, width_y = one.shape[:4]
     depth = planes - 2 * HALO
     parity = lax.axis_index("vox") % 2
@@ -319,10 +353,11 @@
         return carry
 
     lax.fori_loop(0, count_first, add, 0)
-    src, dst = two, one
-    for t in range(1, SWEEPS):
-        sweep_planes(coef, src, dst, *early_part(t, depth, parity), bias)
-        src, dst = dst, src
+
+    def sweep(part, src, dst, t, together):
+        sweep_planes(coef, src, dst, *part(t, depth, parity), bias, together)
+
+    early_sweeps(sweep, one, two, 1)
 
 
 def places(order):
@@ -332,7 +367,7 @@
     return found
 
 
-def adjoint_kernel(orders, one_in, two_in, bias_in, coef, far, forward, far_source, one, two, bias, *rest):
+def adjoint_kernel(orders, one_in, two_in, bias_in, coef, own, far, forward, far_source, one, two, bias, *rest):
     outs, plane_out = rest[:-1], rest[-1]
     count, planes, chunks, width_y = one.shape[:4]
     depth = planes - 2 * HALO
@@ -340,12 +375,16 @@
     parity, group = lax.axis_index("vox") % 2, lax.axis_index("src")
     for s in range(count):
         copy_planes(far, (), s * HALO, one, (s,), halo_place(parity, False, depth, HALO), HALO)
+        edge = jnp.where(parity == 0, 0, depth - 2)
+        copy_planes(own, (s,), edge, one, (s,), edge + HALO, 2)
     moved = SWEEPS - jnp.where(parity == 0, depth, -depth)
     add_sources(coef, far_source, bias, halo_place(parity, False, depth, SWEEPS), SWEEPS, moved)
-    src, dst = one, two
-    for t in range(SWEEPS):
-        sweep_planes(coef, src, dst, *late_part(t, depth, parity), bias)
-        src, dst = dst, src
+
+    def sweep(part, src, dst, t, together):
+        sweep_planes(coef, src, dst, *part(t, depth, parity), bias, together)
+
+    late_sweeps(sweep, one, two)
+    src = one
     lane, sub = lane_ids(), sub_ids()
 
     def steps(ref, s, at, mids, g):
@@ -425,10 +464,12 @@
     return pltpu.VMEM(shape, jnp.float32)
 
 
-def call(kernel, outs, scratch, limit, *args, raw=(), positions=None, kept=0, after=()):
+def call(kernel, outs, scratch, limit, *args, raw=(), fetched=(), positions=None, kept=0, after=()):
     args = [pltpu.with_memory_space_constraint(a, pltpu.VMEM) for a in args]
     args += [pltpu.with_memory_space_constraint(a, pltpu.HBM) for a in raw]
     specs = [VMEM] * len(args)
+    args += [pltpu.with_memory_space_constraint(a, pltpu.HBM) for a in fetched]
+    specs += [pl.BlockSpec(memory_space=pltpu.HBM)] * len(fetched)
     if after:
         inner, used = kernel, len(args) + (positions is not None)
         kernel = lambda *refs: inner(*refs[:used], *refs[used + len(after) :])
@@ -480,7 +521,9 @@
     def pack(kinds, *blocks, after=()):
         rim = held(sum(sum(widths) for widths in kinds), *plane)
         outs = [held(len(widths), depth, *plane) for widths in kinds] + [rim, rim]
-        return call(functools.partial(pack_kernel, kinds), outs, [], 6, raw=blocks, after=after)
+        blocks_held = sum(len(widths) for widths in kinds)
+        scratch = [held(blocks_held, depth, width_y, width_z), pltpu.SemaphoreType.DMA((blocks_held,))]
+        return call(functools.partial(pack_kernel, kinds), outs, scratch, 6, fetched=blocks, after=after)
 
     def sides(near, far):
         return near_swap(near, slabs), far_swap(far, slabs)
@@ -498,7 +541,7 @@
     coef, one, two = call(
         early_kernel,
         [coef_held, field, field],
-        coef_work,
+        [*coef_work, pltpu.SMEM((count, 5), jnp.int32)],
         6,
         coef_own,
         fwd_own,
@@ -516,10 +559,11 @@
         after=[adj_near],
     )
     totals = [sums[0]] + [lax.ppermute(sums[d], "src", [(i, i ^ d) for i in range(groups)]) for d in range(1, groups)]
+    (adj_two,) = call(adjoint_first_kernel, [field], [field], 10, coef, adj_own, adj_near)
     unused, unused, coef, forward, source = call(
         forward_kernel,
         [field, field, coef_held, held(count, depth + 1, *plane), held(count + 1, detectors)],
-        coef_work,
+        [*coef_work, pltpu.SMEM((count, 5), jnp.int32)],
         6,
         one,
         two,
@@ -530,20 +574,19 @@
         raw=[detector_voxel.reshape(1, detectors)],
         positions=source_position,
         kept=3,
+        after=[adj_two],
     )
     source_near, source_far = sides(source, source)
-    one, two = call(adjoint_first_kernel, [field, field], [], 3, coef, adj_own, adj_near, after=[source])
-    one, two, bias = call(
+    two, one, bias = call(
         adjoint_early_kernel,
         [field, field, held(count, planes - 2, *plane)],
         [],
         6,
-        one,
-        two,
+        adj_two,
         coef,
         source,
         source_near,
-        kept=2,
+        kept=1,
     )
     bits = list(range(groups.bit_length() - 1))
     orders = (bits, bits[::-1])
@@ -557,6 +600,7 @@
         two,
         bias,
         coef,
+        adj_own,
         adj_far,
         forward,
         source_far,

time: 66 us -> 61.8 us (0.936)
  Pallas kernels: 31.8 us -> 28.3 us
    pallas_call x9, Pallas kernels: 31.8 us -> 28.3 us  [call(): pl.pallas_call(kernel, out_shape=outs, in_specs=specs, out_specs=[VMEM] *...]
  transfers between devices with their start and end apart: 13 -> 13, of which waited for: 5 -> 5; matrix products, arithmetic and copies ran while one was open for 0% -> 0% of each run, Pallas kernels for 34% -> 32%
where the time goes in v3:
time: 61.8 us; the launch traced here: 61.6 us
  Pallas kernels  28.3 us (46%)
  waiting for transfers between devices  16.6 us (27%)
  starting transfers between devices  15.8 us (26%)
  between operations  0.78 us (1%)
    pallas_call x9, Pallas kernels, call(): pl.pallas_call(kernel, out_shape=outs, in_specs=specs, out_specs=[VMEM] *...  28.3 us
    ppermute x4, waiting for transfers between devices, swap(): lax.ppermute(block, 'src', [(i, i ^ 1 << bit) for i in range(groups)])  11.6 us
    ppermute x3, starting transfers between devices, far_swap(): return lax.ppermute(block, 'vox', pairs + [(b, a) for a, b in pairs])  6.68 us
    ppermute x4, starting transfers between devices, swap(): lax.ppermute(block, 'src', [(i, i ^ 1 << bit) for i in range(groups)])  4.49 us
    ppermute x3, waiting for transfers between devices, far_swap(): return lax.ppermute(block, 'vox', pairs + [(b, a) for a, b in pairs])  3.75 us
    ppermute x3, starting transfers between devices, body(): lax.ppermute(sums[d], 'src', [(i, i ^ d) for i in range(groups)])  3.51 us
  transfers between devices with their start and end apart: 13, of which 5 were waited for; matrix products, arithmetic and copies ran while one was open for 0% of the time, Pallas kernels for 32%

profile of v3, /device:TPU:10, one launch (start us, length us, event | category | flops | bytes accessed | tf_op | source)
XLA Modules:
  0.0 61.6 jit_solution(707524211745485970)
XLA Ops:
  0.6 2.7 %shard_map.113 = (f32[2,8,2,64,128]{4,3,2,1,0:T(8,128)S(1)}, f32[2,8,2,64,128]{4,3,2,1,0:T(8,128)S(1)}, f32[27,2,64,128]{3,2,1,0:T(8,128)S(1)}, f32[27,2,64,128]{3,2,1,0:T(8,128)S(1)}) custom-call(f32[8,64,256]{2,1,0:T(8,128)} %refs_0_.4, f32[8,64,256]{2,1,0:T(8,128)} %refs_1_.1, f32[2,8,64,256]{3,2,1,0:T(8,128)} %refs_2_.1), custom_call_target="tpu_custom_call" | custom-call | flops 1 | bytes 1 | tf_op jit(solution)/shard_map/pallas_call | solution.py:482
  3.4 0.1 collective-permute-start
  3.5 2.4 %collective-permute-start.2 = (f32[27,2,64,128]{3,2,1,0:T(8,128)S(1)}, f32[27,2,64,128]{3,2,1,0:T(8,128)S(1)}, u32[]{:S(2)}, u32[]{:S(2)}) collective-permute-start(f32[27,2,64,128]{3,2,1,0:T(8,128)S(1)} %get-tuple-element.34), channel_id=1, source_target_pairs={{1,2},{3,4},{5,6},{2,1},{4,3},{6,5},{9,10},{11,12},{13,14},{10,9},... | collective-permute-start | bytes 5308424 | tf_op jit(solution)/shard_map/ppermute | solution.py:500
  5.9 1.2 %collective-permute-done.refs_1_.refs_3_ = f32[27,2,64,128]{3,2,1,0:T(8,128)S(1)} collective-permute-done((f32[27,2,64,128]{3,2,1,0:T(8,128)S(1)}, f32[27,2,64,128]{3,2,1,0:T(8,128)S(1)}, u32[]{:S(2)}, u32[]{:S(2)}) %collective-permute-start) | collective-permute-done | bytes 1769504 | tf_op jit(solution)/shard_map/ppermute | solution.py:495
  7.1 1.9 %shard_map.114 = (f32[2,8,2,64,128]{4,3,2,1,0:T(8,128)S(1)}, f32[14,2,64,128]{3,2,1,0:T(8,128)S(1)}, f32[14,2,64,128]{3,2,1,0:T(8,128)S(1)}) custom-call(f32[2,8,64,256]{3,2,1,0:T(8,128)} %refs_0_.5, f32[27,2,64,128]{3,2,1,0:T(8,128)S(1)} %collective-permute-done.refs_1_.refs_3_), custom_call_target="tpu_custom_call" | custom-call | flops 1 | bytes 1 | tf_op jit(solution)/shard_map/pallas_call | solution.py:482
  9.0 0.2 collective-permute-start.1
  9.3 2.3 %collective-permute-start.7 = (f32[14,2,64,128]{3,2,1,0:T(8,128)S(1)}, f32[14,2,64,128]{3,2,1,0:T(8,128)S(1)}, u32[]{:S(2)}, u32[]{:S(2)}) collective-permute-start(f32[14,2,64,128]{3,2,1,0:T(8,128)S(1)} %get-tuple-element.44), channel_id=1, source_target_pairs={{1,2},{3,4},{5,6},{2,1},{4,3},{6,5},{9,10},{11,12},{13,14},{10,9},... | collective-permute-start | bytes 2752520 | tf_op jit(solution)/shard_map/ppermute | solution.py:500
  11.6 0.0 collective-permute-done.1.refs_4_.near
  11.6 1.1 %shard_map.117 = (f32[4,128]{1,0:T(4,128)S(1)}, f32[4,128]{1,0:T(4,128)S(1)}, f32[4,128]{1,0:T(4,128)S(1)}, f32[4,128]{1,0:T(4,128)S(1)}) custom-call(s32[8,128]{1,0:T(8,128)} %bitcast.13, s32[8,128]{1,0:T(8,128)} %bitcast.14, f32[8,128]{1,0:T(8,128)} %bitcast.15, f32[8,128]{1,0:T(8,128)} %bitcast.16, f32[14,2,64,128]{3,2,1,0:T(8,128)S(1)} %collective-permute-done.1.refs_4_.near), custom_call_target="tpu_custom_call" | custom-call | flops 1 | bytes 1 | tf_op jit(solution)/shard_map/pallas_call | solution.py:482
  12.7 0.5 collective-permute-start.3
  13.3 1.5 %collective-permute-start.4 = (f32[4,128]{1,0:T(4,128)S(1)}, f32[4,128]{1,0:T(4,128)S(1)}, u32[]{:S(2)}, u32[]{:S(2)}) collective-permute-start(f32[4,128]{1,0:T(4,128)S(1)} %get-tuple-element.37), channel_id=1, source_target_pairs={{0,16},{8,24},{16,0},{24,8},{1,17},{9,25},{17,1},{25,9},{2,18},{10... | collective-permute-start | bytes 6152 | tf_op jit(solution)/shard_map/ppermute | solution.py:561
  14.8 1.4 %collective-permute-start.5 = (f32[4,128]{1,0:T(4,128)S(1)}, f32[4,128]{1,0:T(4,128)S(1)}, u32[]{:S(2)}, u32[]{:S(2)}) collective-permute-start(f32[4,128]{1,0:T(4,128)S(1)} %get-tuple-element.38), channel_id=1, source_target_pairs={{0,24},{8,16},{16,8},{24,0},{1,25},{9,17},{17,9},{25,1},{2,26},{10... | collective-permute-start | bytes 6152 | tf_op jit(solution)/shard_map/ppermute | solution.py:561
  16.2 6.2 %shard_map.115 = (f32[7,20,2,64,128]{4,3,2,1,0:T(8,128)S(1)}, f32[2,22,2,64,128]{4,3,2,1,0:T(8,128)S(1)}, f32[2,22,2,64,128]{4,3,2,1,0:T(8,128)S(1)}) custom-call(s32[8]{0:T(128)S(1)} %copy-done, f32[2,8,2,64,128]{4,3,2,1,0:T(8,128)S(1)} %get-tuple-element.26.refs_1_.refs_4_, f32[2,8,2,64,128]{4,3,2,1,0:T(8,128)S(1)} %get-tuple-element.27.refs_2_, ...), custom_call_target="tpu_custom_call" | custom-call | flops 1 | bytes 1 | tf_op jit(solution)/shard_map/pallas_call | solution.py:482
  22.4 1.1 %shard_map.116.refs_11_.two_in = f32[2,22,2,64,128]{4,3,2,1,0:T(8,128)S(1)} custom-call(f32[7,20,2,64,128]{4,3,2,1,0:T(8,128)S(1)} %get-tuple-element.30.coef.refs_3_, f32[2,8,2,64,128]{4,3,2,1,0:T(8,128)S(1)} %get-tuple-element.31.own, f32[14,2,64,128]{3,2,1,0:T(8,128)S(1)} %collective-permute-done.1.refs_4_.near), custom_call_target="tpu_custom_call" | custom-call | flops 1 | bytes 1 | tf_op jit(solution)/shard_map/pallas_call | solution.py:482
  23.6 3.7 %collective-permute-done.2.refs_5_ = f32[27,2,64,128]{3,2,1,0:T(8,128)S(1)} collective-permute-done((f32[27,2,64,128]{3,2,1,0:T(8,128)S(1)}, f32[27,2,64,128]{3,2,1,0:T(8,128)S(1)}, u32[]{:S(2)}, u32[]{:S(2)}) %collective-permute-start.2) | collective-permute-done | bytes 1769504 | tf_op jit(solution)/shard_map/ppermute | solution.py:500
  27.3 0.0 collective-permute-done.3.refs_7_
  27.3 0.0 collective-permute-done.4.refs_8_
  27.3 0.0 collective-permute-done.5.refs_9_
  27.3 5.6 %shard_map.118 = (f32[2,22,2,64,128]{4,3,2,1,0:T(8,128)S(1)}, f32[2,22,2,64,128]{4,3,2,1,0:T(8,128)S(1)}, f32[7,20,2,64,128]{4,3,2,1,0:T(8,128)S(1)}, f32[2,9,2,64,128]{4,3,2,1,0:T(8,128)S(1)}, f32[3,128]{1,0:T(4,128)S(1)}) custom-call(s32[8]{0:T(128)S(1)} %copy-done, ...), custom_call_target="tpu_custom_call", output_to_operand_aliasing={{0}: (1, {}), {1}: (2, {}), {2}: (3, {})} | custom-call | flops 1 | bytes 1 | tf_op jit(solution)/shard_map/pallas_call | solution.py:482
  32.9 0.8 %collective-permute-start.6 = (f32[3,128]{1,0:T(4,128)S(1)}, f32[3,128]{1,0:T(4,128)S(1)}, u32[]{:S(2)}, u32[]{:S(2)}) collective-permute-start(f32[3,128]{1,0:T(4,128)S(1)} %get-tuple-element.40.source), channel_id=1, source_target_pairs={{0,1},{1,0},{2,3},{3,2},{4,5},{5,4},{6,7},{7,6},{8,9},{9,8},{10,11... | collective-permute-start | bytes 4616 | tf_op jit(solution)/shard_map/ppermute | solution.py:495
  33.8 1.9 %collective-permute-start.8 = (f32[3,128]{1,0:T(4,128)S(1)}, f32[3,128]{1,0:T(4,128)S(1)}, u32[]{:S(2)}, u32[]{:S(2)}) collective-permute-start(f32[3,128]{1,0:T(4,128)S(1)} %get-tuple-element.40.source), channel_id=1, source_target_pairs={{1,2},{3,4},{5,6},{2,1},{4,3},{6,5},{9,10},{11,12},{13,14},{10,9},... | collective-permute-start | bytes 4616 | tf_op jit(solution)/shard_map/ppermute | solution.py:500
  35.7 4.1 %shard_map.119 = (f32[2,22,2,64,128]{4,3,2,1,0:T(8,128)S(1)}, f32[2,22,2,64,128]{4,3,2,1,0:T(8,128)S(1)}, f32[2,20,2,64,128]{4,3,2,1,0:T(8,128)S(1)}) custom-call(f32[2,22,2,64,128]{4,3,2,1,0:T(8,128)S(1)} %shard_map.116.refs_11_.two_in, f32[7,20,2,64,128]{4,3,2,1,0:T(8,128)S(1)} %get-tuple-element.39.coef, ...), custom_call_target="tpu_custom_call", output_to_operand_aliasing={{0}: (0, {})} | custom-call | flops 1 | bytes 1 | tf_op jit(solution)/shard_map/pallas_call | solution.py:482
  39.7 0.0 collective-permute-done.7.far
  39.8 4.6 %shard_map.120 = (f32[2,22,2,64,128]{4,3,2,1,0:T(8,128)S(1)}, f32[2,22,2,64,128]{4,3,2,1,0:T(8,128)S(1)}, f32[2,20,2,64,128]{4,3,2,1,0:T(8,128)S(1)}, f32[2,8,2,...) custom-call(f32[2,22,2,64,128]{4,3,2,1,0:T(8,128)S(1)} %get-tuple-el, ...), custom_call_target="tpu_custom_call", output_to_operand_aliasing={{0}: (0, {}), {1}: (1, {}), {2}: (2, {})} | custom-call | flops 1 | bytes 1 | tf_op jit(solution)/shard_map/pallas_call | solution.py:482
  44.4 0.6 collective-permute-start.9
  45.0 1.5 %collective-permute-start.11 = (f32[2,8,2,16,128]{4,3,2,1,0:T(8,128)S(1)}, f32[2,8,2,16,128]{4,3,2,1,0:T(8,128)S(1)}, u32[]{:S(2)}, u32[]{:S(2)}) collective-permute-start(f32[2,8,2,16,128]{4,3,2,1,0:T(8,128)S(1)} %get-tuple-element.49), channel_id=1, source_target_pairs={{0,16},{8,24},{16,0},{24,8},{1,17},{9,25},{17,1},{25,9},{2,18},{10... | collective-permute-start | bytes 786440 | tf_op jit(solution)/shard_map/ppermute | solution.py:611
  46.5 6.4 %collective-permute-done.9 = f32[2,8,2,16,128]{4,3,2,1,0:T(8,128)S(1)} collective-permute-done((f32[2,8,2,16,128]{4,3,2,1,0:T(8,128)S(1)}, f32[2,8,2,16,128]{4,3,2,1,0:T(8,128)S(1)}, u32[]{:S(2)}, u32[]{:S(2)}) %collective-permute-start.9) | collective-permute-done | bytes 262176 | tf_op jit(solution)/shard_map/ppermute | solution.py:611
  53.0 1.6 %collective-permute-start.10 = (f32[1,8,2,16,128]{4,3,2,1,0:T(8,128)S(1)}, f32[1,8,2,16,128]{4,3,2,1,0:T(8,128)S(1)}, u32[]{:S(2)}, u32[]{:S(2)}) collective-permute-start(f32[1,8,2,16,128]{4,3,2,1,0:T(8,128)S(1)} %get-tuple-element.52), channel_id=1, source_target_pairs={{0,16},{8,24},{16,0},{24,8},{1,17},{9,25},{17,1},{25,9},{2,18},{10... | collective-permute-start | bytes 393224 | tf_op jit(solution)/shard_map/ppermute | solution.py:611
  54.7 0.8 %collective-permute-start.12 = (f32[1,8,2,16,128]{4,3,2,1,0:T(8,128)S(1)}, f32[1,8,2,16,128]{4,3,2,1,0:T(8,128)S(1)}, u32[]{:S(2)}, u32[]{:S(2)}) collective-permute-start(f32[1,8,2,16,128]{4,3,2,1,0:T(8,128)S(1)} %get-tuple-element.50), channel_id=1, source_target_pairs={{0,8},{8,0},{16,24},{24,16},{1,9},{9,1},{17,25},{25,17},{2,10},{10... | collective-permute-start | bytes 393224 | tf_op jit(solution)/shard_map/ppermute | solution.py:611
  55.4 3.8 %collective-permute-done.10 = f32[1,8,2,16,128]{4,3,2,1,0:T(8,128)S(1)} collective-permute-done((f32[1,8,2,16,128]{4,3,2,1,0:T(8,128)S(1)}, f32[1,8,2,16,128]{4,3,2,1,0:T(8,128)S(1)}, u32[]{:S(2)}, u32[]{:S(2)}) %collective-permute-start.10) | collective-permute-done | bytes 131104 | tf_op jit(solution)/shard_map/ppermute | solution.py:611
  59.2 1.4 %collective-permute-done.12 = f32[1,8,2,16,128]{4,3,2,1,0:T(8,128)S(1)} collective-permute-done((f32[1,8,2,16,128]{4,3,2,1,0:T(8,128)S(1)}, f32[1,8,2,16,128]{4,3,2,1,0:T(8,128)S(1)}, u32[]{:S(2)}, u32[]{:S(2)}) %collective-permute-start.12) | collective-permute-done | bytes 131104 | tf_op jit(solution)/shard_map/ppermute | solution.py:611
  60.6 1.0 %shard_map.121 = (f32[8,16,256]{2,1,0:T(8,128)}, f32[8,16,256]{2,1,0:T(8,128)}) custom-call(f32[8,2,16,128]{3,2,1,0:T(8,128)S(1)} %get-tuple-element.53.refs_0_, f32[8,2,16,128]{3,2,1,0:T(8,128)S(1)} %bitcast.11, f32[8,2,16,128]{3,2,1,0:T(8,128)S(1)} %get-tuple-element.51.refs_2_, f32[8,2,16,128]{3,2,1,0:T(8,128)S(1)} %bitcast.12), custom_call_target="tpu_custom_call" | custom-call | flops 1 | bytes 1 | tf_op jit(solution)/shard_map/pallas_call | solution.py:482
  (9 shorter events, 0.1 us)
Async XLA Ops:
  0.6 15.6 %copy-start = (s32[8]{0:T(128)S(1)}, s32[8]{0:T(128)}, u32[]{:S(2)}) copy-start(s32[8]{0:T(128)} %refs_0_.7) | copy-start | bytes 100
  3.4 3.8 %collective-permute-start = (f32[27,2,64,128]{3,2,1,0:T(8,128)S(1)}, f32[27,2,64,128]{3,2,1,0:T(8,128)S(1)}, u32[]{:S(2)}, u32[]{:S(2)}) collective-permute-start(f32[27,2,64,128]{3,2,1,0:T(8,128)S(1)} %get-tuple-element.28), channel_id=1, source_target_pairs={{0,1},{1,0},{2,3},{3,2},{4,5},{5,4},{6,7},{7,6},{8,9},{9,8},{10,11... | collective-permute-start | bytes 5308424 | tf_op jit(solution)/shard_map/ppermute | solution.py:495
  3.5 23.8 %collective-permute-start.2 = (f32[27,2,64,128]{3,2,1,0:T(8,128)S(1)}, f32[27,2,64,128]{3,2,1,0:T(8,128)S(1)}, u32[]{:S(2)}, u32[]{:S(2)}) collective-permute-start(f32[27,2,64,128]{3,2,1,0:T(8,128)S(1)} %get-tuple-element.34), channel_id=1, source_target_pairs={{1,2},{3,4},{5,6},{2,1},{4,3},{6,5},{9,10},{11,12},{13,14},{10,9},... | collective-permute-start | bytes 5308424 | tf_op jit(solution)/shard_map/ppermute | solution.py:500
  9.0 2.5 %collective-permute-start.1 = (f32[14,2,64,128]{3,2,1,0:T(8,128)S(1)}, f32[14,2,64,128]{3,2,1,0:T(8,128)S(1)}, u32[]{:S(2)}, u32[]{:S(2)}) collective-permute-start(f32[14,2,64,128]{3,2,1,0:T(8,128)S(1)} %get-tuple-element.29), channel_id=1, source_target_pairs={{0,1},{1,0},{2,3},{3,2},{4,5},{5,4},{6,7},{7,6},{8,9},{9,8},{10,11... | collective-permute-start | bytes 2752520 | tf_op jit(solution)/shard_map/ppermute | solution.py:495
  9.3 30.5 %collective-permute-start.7 = (f32[14,2,64,128]{3,2,1,0:T(8,128)S(1)}, f32[14,2,64,128]{3,2,1,0:T(8,128)S(1)}, u32[]{:S(2)}, u32[]{:S(2)}) collective-permute-start(f32[14,2,64,128]{3,2,1,0:T(8,128)S(1)} %get-tuple-element.44), channel_id=1, source_target_pairs={{1,2},{3,4},{5,6},{2,1},{4,3},{6,5},{9,10},{11,12},{13,14},{10,9},... | collective-permute-start | bytes 2752520 | tf_op jit(solution)/shard_map/ppermute | solution.py:500
  12.7 14.6 %collective-permute-start.3 = (f32[4,128]{1,0:T(4,128)S(1)}, f32[4,128]{1,0:T(4,128)S(1)}, u32[]{:S(2)}, u32[]{:S(2)}) collective-permute-start(f32[4,128]{1,0:T(4,128)S(1)} %get-tuple-element.36), channel_id=1, source_target_pairs={{0,8},{8,0},{16,24},{24,16},{1,9},{9,1},{17,25},{25,17},{2,10},{10... | collective-permute-start | bytes 6152 | tf_op jit(solution)/shard_map/ppermute | solution.py:561
  13.3 14.1 %collective-permute-start.4 = (f32[4,128]{1,0:T(4,128)S(1)}, f32[4,128]{1,0:T(4,128)S(1)}, u32[]{:S(2)}, u32[]{:S(2)}) collective-permute-start(f32[4,128]{1,0:T(4,128)S(1)} %get-tuple-element.37), channel_id=1, source_target_pairs={{0,16},{8,24},{16,0},{24,8},{1,17},{9,25},{17,1},{25,9},{2,18},{10... | collective-permute-start | bytes 6152 | tf_op jit(solution)/shard_map/ppermute | solution.py:561
  14.8 12.5 %collective-permute-start.5 = (f32[4,128]{1,0:T(4,128)S(1)}, f32[4,128]{1,0:T(4,128)S(1)}, u32[]{:S(2)}, u32[]{:S(2)}) collective-permute-start(f32[4,128]{1,0:T(4,128)S(1)} %get-tuple-element.38), channel_id=1, source_target_pairs={{0,24},{8,16},{16,8},{24,0},{1,25},{9,17},{17,9},{25,1},{2,26},{10... | collective-permute-start | bytes 6152 | tf_op jit(solution)/shard_map/ppermute | solution.py:561
  32.9 2.8 %collective-permute-start.6 = (f32[3,128]{1,0:T(4,128)S(1)}, f32[3,128]{1,0:T(4,128)S(1)}, u32[]{:S(2)}, u32[]{:S(2)}) collective-permute-start(f32[3,128]{1,0:T(4,128)S(1)} %get-tuple-element.40.source), channel_id=1, source_target_pairs={{0,1},{1,0},{2,3},{3,2},{4,5},{5,4},{6,7},{7,6},{8,9},{9,8},{10,11... | collective-permute-start | bytes 4616 | tf_op jit(solution)/shard_map/ppermute | solution.py:495
  33.8 6.0 %collective-permute-start.8 = (f32[3,128]{1,0:T(4,128)S(1)}, f32[3,128]{1,0:T(4,128)S(1)}, u32[]{:S(2)}, u32[]{:S(2)}) collective-permute-start(f32[3,128]{1,0:T(4,128)S(1)} %get-tuple-element.40.source), channel_id=1, source_target_pairs={{1,2},{3,4},{5,6},{2,1},{4,3},{6,5},{9,10},{11,12},{13,14},{10,9},... | collective-permute-start | bytes 4616 | tf_op jit(solution)/shard_map/ppermute | solution.py:500
  44.4 8.6 %collective-permute-start.9 = (f32[2,8,2,16,128]{4,3,2,1,0:T(8,128)S(1)}, f32[2,8,2,16,128]{4,3,2,1,0:T(8,128)S(1)}, u32[]{:S(2)}, u32[]{:S(2)}) collective-permute-start(f32[2,8,2,16,128]{4,3,2,1,0:T(8,128)S(1)} %get-tuple-element.47), channel_id=1, source_target_pairs={{0,8},{8,0},{16,24},{24,16},{1,9},{9,1},{17,25},{25,17},{2,10},{10... | collective-permute-start | bytes 786440 | tf_op jit(solution)/shard_map/ppermute | solution.py:611
  45.0 9.6 %collective-permute-start.11 = (f32[2,8,2,16,128]{4,3,2,1,0:T(8,128)S(1)}, f32[2,8,2,16,128]{4,3,2,1,0:T(8,128)S(1)}, u32[]{:S(2)}, u32[]{:S(2)}) collective-permute-start(f32[2,8,2,16,128]{4,3,2,1,0:T(8,128)S(1)} %get-tuple-element.49), channel_id=1, source_target_pairs={{0,16},{8,24},{16,0},{24,8},{1,17},{9,25},{17,1},{25,9},{2,18},{10... | collective-permute-start | bytes 786440 | tf_op jit(solution)/shard_map/ppermute | solution.py:611
  53.0 6.3 %collective-permute-start.10 = (f32[1,8,2,16,128]{4,3,2,1,0:T(8,128)S(1)}, f32[1,8,2,16,128]{4,3,2,1,0:T(8,128)S(1)}, u32[]{:S(2)}, u32[]{:S(2)}) collective-permute-start(f32[1,8,2,16,128]{4,3,2,1,0:T(8,128)S(1)} %get-tuple-element.52), channel_id=1, source_target_pairs={{0,16},{8,24},{16,0},{24,8},{1,17},{9,25},{17,1},{25,9},{2,18},{10... | collective-permute-start | bytes 393224 | tf_op jit(solution)/shard_map/ppermute | solution.py:611
  54.7 6.0 %collective-permute-start.12 = (f32[1,8,2,16,128]{4,3,2,1,0:T(8,128)S(1)}, f32[1,8,2,16,128]{4,3,2,1,0:T(8,128)S(1)}, u32[]{:S(2)}, u32[]{:S(2)}) collective-permute-start(f32[1,8,2,16,128]{4,3,2,1,0:T(8,128)S(1)} %get-tuple-element.50), channel_id=1, source_target_pairs={{0,8},{8,0},{16,24},{24,16},{1,9},{9,1},{17,25},{25,17},{2,10},{10... | collective-permute-start | bytes 393224 | tf_op jit(solution)/shard_map/ppermute | solution.py:611

commit v4 on v3

--- a/solution.py
+++ b/solution.py
@@ -60,6 +60,11 @@
 def split(values):
     high = values.astype(jnp.bfloat16)
     return high, (values - high.astype(jnp.float32)).astype(jnp.bfloat16)
+
+
+def exact_dot(values, hot, hot_dim):
+    dims = (((1,), (hot_dim,)), ((), ()))
+    return sum(lax.dot_general(part, hot, dims, preferred_element_type=jnp.float32) for part in split(values))
 
 
 def z_order(width_z, natural_dim):
@@ -88,10 +93,11 @@
     for own, widths in zip(owns, kinds):
         for b, width in enumerate(widths):
             block = blocks.pop(0)
-            copies.pop(0).wait()
+            copies[0].wait()
+            copies.pop(0)
             for first in range(0, depth, together):
                 values = block[pl.ds(first, together)].reshape(together * width_y, width_z)
-                packed = sum(jnp.dot(part, order, preferred_element_type=jnp.float32) for part in split(values))
+                packed = exact_dot(values, order, 0)
                 for i in range(together):
                     for y in range(0, width_y, SUB):
                         for j in range(chunks):
@@ -284,9 +290,10 @@
     width_z, groups = chunks * LANES, width_y // SUB
     slab = lax.axis_index("vox")
     parity = slab % 2
-    copy_planes(coef_own, (0,), 0, kap, (), HALO, depth)
+    edge = jnp.where(parity == 0, 0, depth - 2)
+    copy_planes(coef_own, (0,), edge, kap, (), edge + HALO, 2)
     copy_planes(far, (), 0, kap, (), halo_place(parity, False, depth, HALO), HALO)
-    copy_planes(coef_own, (1,), 0, mu, (), SWEEPS, depth)
+    copy_planes(coef_own, (1,), edge, mu, (), edge + SWEEPS, 2)
     copy_planes(far, (), HALO, mu, (), halo_place(parity, False, depth, SWEEPS), SWEEPS)
     coefficient_planes(slab, kap, mu, coef, *late_part(0, depth, parity), depth)
     for s in range(count):
@@ -303,11 +310,8 @@
     row_mask, z_hot = detector_masks(local_cells, 0, depth, width_y, width_z)
     total = sum(part[...] for part in totals)
     for s in range(count):
-        sampled = 0.0
-        for j in range(chunks):
-            field = one[s, pl.ds(HALO, depth), j].reshape(depth * width_y, LANES)
-            for part in split(field):
-                sampled = sampled + jnp.dot(part, z_hot[j], preferred_element_type=jnp.float32)
+        field = [one[s, pl.ds(HALO, depth), j].reshape(depth * width_y, LANES) for j in range(chunks)]
+        sampled = exact_dot(jnp.concatenate(field, axis=1), jnp.concatenate(z_hot, axis=0), 0)
         predicted = jnp.sum(jnp.where(row_mask, sampled, 0.0), axis=0, keepdims=True)
         adjoint_source[pl.ds(s, 1), :] = predicted * total[s : s + 1] - total[count + s : count + s + 1]
     adjoint_source[pl.ds(count, 1), :] = local_cells.astype(jnp.float32)
@@ -334,7 +338,7 @@
             for spread in spreads:
                 placed = placed + lax.dot_general(spread, z_hot[j], (((1,), (1,)), ((), ())), preferred_element_type=jnp.float32)
             placed = placed.reshape(planes, width_y, LANES)
-            bias[s, pl.ds(at, planes), j] = placed * coef[6, pl.ds(at, planes), j]
+            bias[s, pl.ds(at, planes), j, pl.ds(0, width_y)] = placed * coef[6, pl.ds(at, planes), j, pl.ds(0, width_y)]
 
 
 def adjoint_early_kernel(two_in, coef, source, near_source, two, one, bias):
@@ -368,7 +372,7 @@
 
 
 def adjoint_kernel(orders, one_in, two_in, bias_in, coef, own, far, forward, far_source, one, two, bias, *rest):
-    outs, plane_out = rest[:-1], rest[-1]
+    outs, plane_outs = rest[:-2], rest[-2:]
     count, planes, chunks, width_y = one.shape[:4]
     depth = planes - 2 * HALO
     groups = width_y // SUB
@@ -400,7 +404,7 @@
     tiles = 1 << len(orders[0])
     tile_rows = width_y // tiles
 
-    def plane(p, carry):
+    def plane(p, plane_out):
         mids_f = [load_plane(forward, (s, p), groups, chunks) for s in range(count)]
         mids_a = [load_plane(src, (s, p + HALO), groups, chunks) for s in range(count)]
         for g in range(groups):
@@ -421,9 +425,13 @@
                 first = pl.multiple_of((group ^ place) * tile_rows, SUB)
                 for j in range(chunks):
                     out[i % (tiles // 2), p, j] = plane_out[k, j, pl.ds(first, tile_rows), :]
+
+    def pair(i, carry):
+        plane(2 * i, plane_outs[0])
+        plane(2 * i + 1, plane_outs[1])
         return carry
 
-    lax.fori_loop(0, depth, plane, 0)
+    lax.fori_loop(0, depth // 2, pair, 0)
 
 
 def unpack_kernel(*refs):
@@ -433,7 +441,7 @@
     for k, out in enumerate(outs):
         total = pairs[2 * k][...] + pairs[2 * k + 1][...]
         total = jnp.concatenate([total[:, j].reshape(depth * rows, LANES) for j in range(chunks)], axis=1)
-        natural = sum(jnp.dot(part, order, preferred_element_type=jnp.float32) for part in split(total))
+        natural = exact_dot(total, order, 0)
         out[...] = natural.reshape(out.shape)
 
 
@@ -530,7 +538,8 @@
 
     planes = depth + 2 * HALO
     field = held(count, planes, *plane)
-    coef_held = held(7, planes - 2, *plane)
+    padded = (plane[0], width_y + SUB, LANES)
+    coef_held = held(7, planes - 2, *padded)
     coef_work = [held(planes, *plane), held(planes - 2, *plane)]
 
     field_rims = (HALO,) * count
@@ -594,7 +603,7 @@
     unused, unused, unused, *parts = call(
         functools.partial(adjoint_kernel, orders),
         [field, field, held(count, planes - 2, *plane)] + [half] * 4,
-        [held(2, *plane)],
+        [held(2, *plane)] * 2,
         6,
         one,
         two,

time: 61.8 us -> 60.7 us (0.982)
  Pallas kernels: 28.3 us -> 26.9 us
    pallas_call x9, Pallas kernels: 28.3 us -> 26.9 us  [call(): pl.pallas_call(kernel, out_shape=outs, in_specs=specs, out_specs=[VMEM] *...]
where the time goes in v4:
time: 60.7 us; the launch traced here: 60.5 us
  Pallas kernels  26.9 us (44%)
  waiting for transfers between devices  17 us (28%)
  starting transfers between devices  15.7 us (26%)
  between operations  0.79 us (1%)
    pallas_call x9, Pallas kernels, call(): pl.pallas_call(kernel, out_shape=outs, in_specs=specs, out_specs=[VMEM] *...  26.9 us
    ppermute x4, waiting for transfers between devices, swap(): lax.ppermute(block, 'src', [(i, i ^ 1 << bit) for i in range(groups)])  11.8 us
    ppermute x3, starting transfers between devices, far_swap(): return lax.ppermute(block, 'vox', pairs + [(b, a) for a, b in pairs])  6.68 us
    ppermute x4, starting transfers between devices, swap(): lax.ppermute(block, 'src', [(i, i ^ 1 << bit) for i in range(groups)])  4.34 us
    ppermute x3, waiting for transfers between devices, far_swap(): return lax.ppermute(block, 'vox', pairs + [(b, a) for a, b in pairs])  3.91 us
    ppermute x3, starting transfers between devices, body(): lax.ppermute(sums[d], 'src', [(i, i ^ d) for i in range(groups)])  3.51 us
    ppermute x3, waiting for transfers between devices, near_swap(): lax.ppermute(block, 'vox', [(i, i ^ 1) for i in range(count) if i ^ 1 < c...  1.23 us
  transfers between devices with their start and end apart: 13, of which 5 were waited for; matrix products, arithmetic and copies ran while one was open for 0% of the time, Pallas kernels for 32%

profile of v4, /device:TPU:10, one launch (start us, length us, event | category | flops | bytes accessed | tf_op | source)
XLA Modules:
  0.0 60.5 jit_solution(7450773667335664329)
XLA Ops:
  0.6 2.7 %shard_map.113 = (f32[2,8,2,64,128]{4,3,2,1,0:T(8,128)S(1)}, f32[2,8,2,64,128]{4,3,2,1,0:T(8,128)S(1)}, f32[27,2,64,128]{3,2,1,0:T(8,128)S(1)}, f32[27,2,64,128]{3,2,1,0:T(8,128)S(1)}) custom-call(f32[8,64,256]{2,1,0:T(8,128)} %refs_0_.4, f32[8,64,256]{2,1,0:T(8,128)} %refs_1_.1, f32[2,8,64,256]{3,2,1,0:T(8,128)} %refs_2_.1), custom_call_target="tpu_custom_call" | custom-call | flops 1 | bytes 1 | tf_op jit(solution)/shard_map/pallas_call | solution.py:490
  3.4 0.1 collective-permute-start
  3.5 2.4 %collective-permute-start.2 = (f32[27,2,64,128]{3,2,1,0:T(8,128)S(1)}, f32[27,2,64,128]{3,2,1,0:T(8,128)S(1)}, u32[]{:S(2)}, u32[]{:S(2)}) collective-permute-start(f32[27,2,64,128]{3,2,1,0:T(8,128)S(1)} %get-tuple-element.34), channel_id=1, source_target_pairs={{1,2},{3,4},{5,6},{2,1},{4,3},{6,5},{9,10},{11,12},{13,14},{10,9},... | collective-permute-start | bytes 5308424 | tf_op jit(solution)/shard_map/ppermute | solution.py:508
  5.9 1.2 %collective-permute-done.refs_1_.refs_3_ = f32[27,2,64,128]{3,2,1,0:T(8,128)S(1)} collective-permute-done((f32[27,2,64,128]{3,2,1,0:T(8,128)S(1)}, f32[27,2,64,128]{3,2,1,0:T(8,128)S(1)}, u32[]{:S(2)}, u32[]{:S(2)}) %collective-permute-start) | collective-permute-done | bytes 1769504 | tf_op jit(solution)/shard_map/ppermute | solution.py:503
  7.1 1.9 %shard_map.114 = (f32[2,8,2,64,128]{4,3,2,1,0:T(8,128)S(1)}, f32[14,2,64,128]{3,2,1,0:T(8,128)S(1)}, f32[14,2,64,128]{3,2,1,0:T(8,128)S(1)}) custom-call(f32[2,8,64,256]{3,2,1,0:T(8,128)} %refs_0_.5, f32[27,2,64,128]{3,2,1,0:T(8,128)S(1)} %collective-permute-done.refs_1_.refs_3_), custom_call_target="tpu_custom_call" | custom-call | flops 1 | bytes 1 | tf_op jit(solution)/shard_map/pallas_call | solution.py:490
  9.0 0.2 collective-permute-start.1
  9.3 2.3 %collective-permute-start.7 = (f32[14,2,64,128]{3,2,1,0:T(8,128)S(1)}, f32[14,2,64,128]{3,2,1,0:T(8,128)S(1)}, u32[]{:S(2)}, u32[]{:S(2)}) collective-permute-start(f32[14,2,64,128]{3,2,1,0:T(8,128)S(1)} %get-tuple-element.44), channel_id=1, source_target_pairs={{1,2},{3,4},{5,6},{2,1},{4,3},{6,5},{9,10},{11,12},{13,14},{10,9},... | collective-permute-start | bytes 2752520 | tf_op jit(solution)/shard_map/ppermute | solution.py:508
  11.6 0.0 collective-permute-done.1.refs_4_.near
  11.6 1.1 %shard_map.117 = (f32[4,128]{1,0:T(4,128)S(1)}, f32[4,128]{1,0:T(4,128)S(1)}, f32[4,128]{1,0:T(4,128)S(1)}, f32[4,128]{1,0:T(4,128)S(1)}) custom-call(s32[8,128]{1,0:T(8,128)} %bitcast.13, s32[8,128]{1,0:T(8,128)} %bitcast.14, f32[8,128]{1,0:T(8,128)} %bitcast.15, f32[8,128]{1,0:T(8,128)} %bitcast.16, f32[14,2,64,128]{3,2,1,0:T(8,128)S(1)} %collective-permute-done.1.refs_4_.near), custom_call_target="tpu_custom_call" | custom-call | flops 1 | bytes 1 | tf_op jit(solution)/shard_map/pallas_call | solution.py:490
  12.7 0.5 collective-permute-start.3
  13.3 1.5 %collective-permute-start.4 = (f32[4,128]{1,0:T(4,128)S(1)}, f32[4,128]{1,0:T(4,128)S(1)}, u32[]{:S(2)}, u32[]{:S(2)}) collective-permute-start(f32[4,128]{1,0:T(4,128)S(1)} %get-tuple-element.37), channel_id=1, source_target_pairs={{0,16},{8,24},{16,0},{24,8},{1,17},{9,25},{17,1},{25,9},{2,18},{10... | collective-permute-start | bytes 6152 | tf_op jit(solution)/shard_map/ppermute | solution.py:570
  14.8 1.4 %collective-permute-start.5 = (f32[4,128]{1,0:T(4,128)S(1)}, f32[4,128]{1,0:T(4,128)S(1)}, u32[]{:S(2)}, u32[]{:S(2)}) collective-permute-start(f32[4,128]{1,0:T(4,128)S(1)} %get-tuple-element.38), channel_id=1, source_target_pairs={{0,24},{8,16},{16,8},{24,0},{1,25},{9,17},{17,9},{25,1},{2,26},{10... | collective-permute-start | bytes 6152 | tf_op jit(solution)/shard_map/ppermute | solution.py:570
  16.2 6.0 %shard_map.115 = (f32[7,20,2,72,128]{4,3,2,1,0:T(8,128)S(1)}, f32[2,22,2,64,128]{4,3,2,1,0:T(8,128)S(1)}, f32[2,22,2,64,128]{4,3,2,1,0:T(8,128)S(1)}) custom-call(s32[8]{0:T(128)S(1)} %copy-done, f32[2,8,2,64,128]{4,3,2,1,0:T(8,128)S(1)} %get-tuple-element.26.refs_1_.refs_4_, f32[2,8,2,64,128]{4,3,2,1,0:T(8,128)S(1)} %get-tuple-element.27.refs_2_, ...), custom_call_target="tpu_custom_call" | custom-call | flops 1 | bytes 1 | tf_op jit(solution)/shard_map/pallas_call | solution.py:490
  22.2 1.2 %shard_map.116.refs_11_.two_in = f32[2,22,2,64,128]{4,3,2,1,0:T(8,128)S(1)} custom-call(f32[7,20,2,72,128]{4,3,2,1,0:T(8,128)S(1)} %get-tuple-element.30.coef.refs_3_, f32[2,8,2,64,128]{4,3,2,1,0:T(8,128)S(1)} %get-tuple-element.31.own, f32[14,2,64,128]{3,2,1,0:T(8,128)S(1)} %collective-permute-done.1.refs_4_.near), custom_call_target="tpu_custom_call" | custom-call | flops 1 | bytes 1 | tf_op jit(solution)/shard_map/pallas_call | solution.py:490
  23.4 3.9 %collective-permute-done.2.refs_5_ = f32[27,2,64,128]{3,2,1,0:T(8,128)S(1)} collective-permute-done((f32[27,2,64,128]{3,2,1,0:T(8,128)S(1)}, f32[27,2,64,128]{3,2,1,0:T(8,128)S(1)}, u32[]{:S(2)}, u32[]{:S(2)}) %collective-permute-start.2) | collective-permute-done | bytes 1769504 | tf_op jit(solution)/shard_map/ppermute | solution.py:508
  27.3 0.0 collective-permute-done.3.refs_7_
  27.3 0.0 collective-permute-done.5.refs_9_
  27.3 5.2 %shard_map.118 = (f32[2,22,2,64,128]{4,3,2,1,0:T(8,128)S(1)}, f32[2,22,2,64,128]{4,3,2,1,0:T(8,128)S(1)}, f32[7,20,2,72,128]{4,3,2,1,0:T(8,128)S(1)}, f32[2,9,2,64,128]{4,3,2,1,0:T(8,128)S(1)}, f32[3,128]{1,0:T(4,128)S(1)}) custom-call(s32[8]{0:T(128)S(1)} %copy-done, ...), custom_call_target="tpu_custom_call", output_to_operand_aliasing={{0}: (1, {}), {1}: (2, {}), {2}: (3, {})} | custom-call | flops 1 | bytes 1 | tf_op jit(solution)/shard_map/pallas_call | solution.py:490
  32.5 0.9 %collective-permute-start.6 = (f32[3,128]{1,0:T(4,128)S(1)}, f32[3,128]{1,0:T(4,128)S(1)}, u32[]{:S(2)}, u32[]{:S(2)}) collective-permute-start(f32[3,128]{1,0:T(4,128)S(1)} %get-tuple-element.40.source), channel_id=1, source_target_pairs={{0,1},{1,0},{2,3},{3,2},{4,5},{5,4},{6,7},{7,6},{8,9},{9,8},{10,11... | collective-permute-start | bytes 4616 | tf_op jit(solution)/shard_map/ppermute | solution.py:503
  33.4 1.9 %collective-permute-start.8 = (f32[3,128]{1,0:T(4,128)S(1)}, f32[3,128]{1,0:T(4,128)S(1)}, u32[]{:S(2)}, u32[]{:S(2)}) collective-permute-start(f32[3,128]{1,0:T(4,128)S(1)} %get-tuple-element.40.source), channel_id=1, source_target_pairs={{1,2},{3,4},{5,6},{2,1},{4,3},{6,5},{9,10},{11,12},{13,14},{10,9},... | collective-permute-start | bytes 4616 | tf_op jit(solution)/shard_map/ppermute | solution.py:508
  35.3 3.7 %shard_map.119 = (f32[2,22,2,64,128]{4,3,2,1,0:T(8,128)S(1)}, f32[2,22,2,64,128]{4,3,2,1,0:T(8,128)S(1)}, f32[2,20,2,64,128]{4,3,2,1,0:T(8,128)S(1)}) custom-call(f32[2,22,2,64,128]{4,3,2,1,0:T(8,128)S(1)} %shard_map.116.refs_11_.two_in, f32[7,20,2,72,128]{4,3,2,1,0:T(8,128)S(1)} %get-tuple-element.39.coef, ...), custom_call_target="tpu_custom_call", output_to_operand_aliasing={{0}: (0, {})} | custom-call | flops 1 | bytes 1 | tf_op jit(solution)/shard_map/pallas_call | solution.py:490
  39.0 0.0 collective-permute-done.8.far_source
  39.1 4.2 %shard_map.120 = (f32[2,22,2,64,128]{4,3,2,1,0:T(8,128)S(1)}, f32[2,22,2,64,128]{4,3,2,1,0:T(8,128)S(1)}, f32[2,20,2,64,128]{4,3,2,1,0:T(8,128)S(1)}, f32[2,8,2,...) custom-call(f32[2,22,2,64,128]{4,3,2,1,0:T(8,128)S(1)} %get-tuple-el, ...), custom_call_target="tpu_custom_call", output_to_operand_aliasing={{0}: (0, {}), {1}: (1, {}), {2}: (2, {})} | custom-call | flops 1 | bytes 1 | tf_op jit(solution)/shard_map/pallas_call | solution.py:490
  43.2 0.6 collective-permute-start.9
  43.8 1.5 %collective-permute-start.11 = (f32[2,8,2,16,128]{4,3,2,1,0:T(8,128)S(1)}, f32[2,8,2,16,128]{4,3,2,1,0:T(8,128)S(1)}, u32[]{:S(2)}, u32[]{:S(2)}) collective-permute-start(f32[2,8,2,16,128]{4,3,2,1,0:T(8,128)S(1)} %get-tuple-element.49), channel_id=1, source_target_pairs={{0,16},{8,24},{16,0},{24,8},{1,17},{9,25},{17,1},{25,9},{2,18},{10... | collective-permute-start | bytes 786440 | tf_op jit(solution)/shard_map/ppermute | solution.py:620
  45.3 6.8 %collective-permute-done.9 = f32[2,8,2,16,128]{4,3,2,1,0:T(8,128)S(1)} collective-permute-done((f32[2,8,2,16,128]{4,3,2,1,0:T(8,128)S(1)}, f32[2,8,2,16,128]{4,3,2,1,0:T(8,128)S(1)}, u32[]{:S(2)}, u32[]{:S(2)}) %collective-permute-start.9) | collective-permute-done | bytes 262176 | tf_op jit(solution)/shard_map/ppermute | solution.py:620
  52.2 1.6 %collective-permute-start.10 = (f32[1,8,2,16,128]{4,3,2,1,0:T(8,128)S(1)}, f32[1,8,2,16,128]{4,3,2,1,0:T(8,128)S(1)}, u32[]{:S(2)}, u32[]{:S(2)}) collective-permute-start(f32[1,8,2,16,128]{4,3,2,1,0:T(8,128)S(1)} %get-tuple-element.52), channel_id=1, source_target_pairs={{0,16},{8,24},{16,0},{24,8},{1,17},{9,25},{17,1},{25,9},{2,18},{10... | collective-permute-start | bytes 393224 | tf_op jit(solution)/shard_map/ppermute | solution.py:620
  53.8 0.0 collective-permute-done.11
  53.9 0.6 collective-permute-start.12
  54.5 3.6 %collective-permute-done.10 = f32[1,8,2,16,128]{4,3,2,1,0:T(8,128)S(1)} collective-permute-done((f32[1,8,2,16,128]{4,3,2,1,0:T(8,128)S(1)}, f32[1,8,2,16,128]{4,3,2,1,0:T(8,128)S(1)}, u32[]{:S(2)}, u32[]{:S(2)}) %collective-permute-start.10) | collective-permute-done | bytes 131104 | tf_op jit(solution)/shard_map/ppermute | solution.py:620
  58.1 1.4 %collective-permute-done.12 = f32[1,8,2,16,128]{4,3,2,1,0:T(8,128)S(1)} collective-permute-done((f32[1,8,2,16,128]{4,3,2,1,0:T(8,128)S(1)}, f32[1,8,2,16,128]{4,3,2,1,0:T(8,128)S(1)}, u32[]{:S(2)}, u32[]{:S(2)}) %collective-permute-start.12) | collective-permute-done | bytes 131104 | tf_op jit(solution)/shard_map/ppermute | solution.py:620
  59.5 1.0 %shard_map.121 = (f32[8,16,256]{2,1,0:T(8,128)}, f32[8,16,256]{2,1,0:T(8,128)}) custom-call(f32[8,2,16,128]{3,2,1,0:T(8,128)S(1)} %get-tuple-element.53.refs_0_, f32[8,2,16,128]{3,2,1,0:T(8,128)S(1)} %bitcast.11, f32[8,2,16,128]{3,2,1,0:T(8,128)S(1)} %get-tuple-element.51.refs_2_, f32[8,2,16,128]{3,2,1,0:T(8,128)S(1)} %bitcast.12), custom_call_target="tpu_custom_call" | custom-call | flops 1 | bytes 1 | tf_op jit(solution)/shard_map/pallas_call | solution.py:490
  (9 shorter events, 0.1 us)
Async XLA Ops:
  0.6 15.6 %copy-start = (s32[8]{0:T(128)S(1)}, s32[8]{0:T(128)}, u32[]{:S(2)}) copy-start(s32[8]{0:T(128)} %refs_0_.7) | copy-start | bytes 100
  3.4 3.8 %collective-permute-start = (f32[27,2,64,128]{3,2,1,0:T(8,128)S(1)}, f32[27,2,64,128]{3,2,1,0:T(8,128)S(1)}, u32[]{:S(2)}, u32[]{:S(2)}) collective-permute-start(f32[27,2,64,128]{3,2,1,0:T(8,128)S(1)} %get-tuple-element.28), channel_id=1, source_target_pairs={{0,1},{1,0},{2,3},{3,2},{4,5},{5,4},{6,7},{7,6},{8,9},{9,8},{10,11... | collective-permute-start | bytes 5308424 | tf_op jit(solution)/shard_map/ppermute | solution.py:503
  3.5 23.8 %collective-permute-start.2 = (f32[27,2,64,128]{3,2,1,0:T(8,128)S(1)}, f32[27,2,64,128]{3,2,1,0:T(8,128)S(1)}, u32[]{:S(2)}, u32[]{:S(2)}) collective-permute-start(f32[27,2,64,128]{3,2,1,0:T(8,128)S(1)} %get-tuple-element.34), channel_id=1, source_target_pairs={{1,2},{3,4},{5,6},{2,1},{4,3},{6,5},{9,10},{11,12},{13,14},{10,9},... | collective-permute-start | bytes 5308424 | tf_op jit(solution)/shard_map/ppermute | solution.py:508
  9.0 2.5 %collective-permute-start.1 = (f32[14,2,64,128]{3,2,1,0:T(8,128)S(1)}, f32[14,2,64,128]{3,2,1,0:T(8,128)S(1)}, u32[]{:S(2)}, u32[]{:S(2)}) collective-permute-start(f32[14,2,64,128]{3,2,1,0:T(8,128)S(1)} %get-tuple-element.29), channel_id=1, source_target_pairs={{0,1},{1,0},{2,3},{3,2},{4,5},{5,4},{6,7},{7,6},{8,9},{9,8},{10,11... | collective-permute-start | bytes 2752520 | tf_op jit(solution)/shard_map/ppermute | solution.py:503
  9.3 29.8 %collective-permute-start.7 = (f32[14,2,64,128]{3,2,1,0:T(8,128)S(1)}, f32[14,2,64,128]{3,2,1,0:T(8,128)S(1)}, u32[]{:S(2)}, u32[]{:S(2)}) collective-permute-start(f32[14,2,64,128]{3,2,1,0:T(8,128)S(1)} %get-tuple-element.44), channel_id=1, source_target_pairs={{1,2},{3,4},{5,6},{2,1},{4,3},{6,5},{9,10},{11,12},{13,14},{10,9},... | collective-permute-start | bytes 2752520 | tf_op jit(solution)/shard_map/ppermute | solution.py:508
  12.7 14.6 %collective-permute-start.3 = (f32[4,128]{1,0:T(4,128)S(1)}, f32[4,128]{1,0:T(4,128)S(1)}, u32[]{:S(2)}, u32[]{:S(2)}) collective-permute-start(f32[4,128]{1,0:T(4,128)S(1)} %get-tuple-element.36), channel_id=1, source_target_pairs={{0,8},{8,0},{16,24},{24,16},{1,9},{9,1},{17,25},{25,17},{2,10},{10... | collective-permute-start | bytes 6152 | tf_op jit(solution)/shard_map/ppermute | solution.py:570
  13.3 14.1 %collective-permute-start.4 = (f32[4,128]{1,0:T(4,128)S(1)}, f32[4,128]{1,0:T(4,128)S(1)}, u32[]{:S(2)}, u32[]{:S(2)}) collective-permute-start(f32[4,128]{1,0:T(4,128)S(1)} %get-tuple-element.37), channel_id=1, source_target_pairs={{0,16},{8,24},{16,0},{24,8},{1,17},{9,25},{17,1},{25,9},{2,18},{10... | collective-permute-start | bytes 6152 | tf_op jit(solution)/shard_map/ppermute | solution.py:570
  14.8 12.5 %collective-permute-start.5 = (f32[4,128]{1,0:T(4,128)S(1)}, f32[4,128]{1,0:T(4,128)S(1)}, u32[]{:S(2)}, u32[]{:S(2)}) collective-permute-start(f32[4,128]{1,0:T(4,128)S(1)} %get-tuple-element.38), channel_id=1, source_target_pairs={{0,24},{8,16},{16,8},{24,0},{1,25},{9,17},{17,9},{25,1},{2,26},{10... | collective-permute-start | bytes 6152 | tf_op jit(solution)/shard_map/ppermute | solution.py:570
  32.5 2.8 %collective-permute-start.6 = (f32[3,128]{1,0:T(4,128)S(1)}, f32[3,128]{1,0:T(4,128)S(1)}, u32[]{:S(2)}, u32[]{:S(2)}) collective-permute-start(f32[3,128]{1,0:T(4,128)S(1)} %get-tuple-element.40.source), channel_id=1, source_target_pairs={{0,1},{1,0},{2,3},{3,2},{4,5},{5,4},{6,7},{7,6},{8,9},{9,8},{10,11... | collective-permute-start | bytes 4616 | tf_op jit(solution)/shard_map/ppermute | solution.py:503
  33.4 5.7 %collective-permute-start.8 = (f32[3,128]{1,0:T(4,128)S(1)}, f32[3,128]{1,0:T(4,128)S(1)}, u32[]{:S(2)}, u32[]{:S(2)}) collective-permute-start(f32[3,128]{1,0:T(4,128)S(1)} %get-tuple-element.40.source), channel_id=1, source_target_pairs={{1,2},{3,4},{5,6},{2,1},{4,3},{6,5},{9,10},{11,12},{13,14},{10,9},... | collective-permute-start | bytes 4616 | tf_op jit(solution)/shard_map/ppermute | solution.py:508
  43.2 8.9 %collective-permute-start.9 = (f32[2,8,2,16,128]{4,3,2,1,0:T(8,128)S(1)}, f32[2,8,2,16,128]{4,3,2,1,0:T(8,128)S(1)}, u32[]{:S(2)}, u32[]{:S(2)}) collective-permute-start(f32[2,8,2,16,128]{4,3,2,1,0:T(8,128)S(1)} %get-tuple-element.47), channel_id=1, source_target_pairs={{0,8},{8,0},{16,24},{24,16},{1,9},{9,1},{17,25},{25,17},{2,10},{10... | collective-permute-start | bytes 786440 | tf_op jit(solution)/shard_map/ppermute | solution.py:620
  43.8 10.0 %collective-permute-start.11 = (f32[2,8,2,16,128]{4,3,2,1,0:T(8,128)S(1)}, f32[2,8,2,16,128]{4,3,2,1,0:T(8,128)S(1)}, u32[]{:S(2)}, u32[]{:S(2)}) collective-permute-start(f32[2,8,2,16,128]{4,3,2,1,0:T(8,128)S(1)} %get-tuple-element.49), channel_id=1, source_target_pairs={{0,16},{8,24},{16,0},{24,8},{1,17},{9,25},{17,1},{25,9},{2,18},{10... | collective-permute-start | bytes 786440 | tf_op jit(solution)/shard_map/ppermute | solution.py:620
  52.2 5.9 %collective-permute-start.10 = (f32[1,8,2,16,128]{4,3,2,1,0:T(8,128)S(1)}, f32[1,8,2,16,128]{4,3,2,1,0:T(8,128)S(1)}, u32[]{:S(2)}, u32[]{:S(2)}) collective-permute-start(f32[1,8,2,16,128]{4,3,2,1,0:T(8,128)S(1)} %get-tuple-element.52), channel_id=1, source_target_pairs={{0,16},{8,24},{16,0},{24,8},{1,17},{9,25},{17,1},{25,9},{2,18},{10... | collective-permute-start | bytes 393224 | tf_op jit(solution)/shard_map/ppermute | solution.py:620
  53.9 5.6 %collective-permute-start.12 = (f32[1,8,2,16,128]{4,3,2,1,0:T(8,128)S(1)}, f32[1,8,2,16,128]{4,3,2,1,0:T(8,128)S(1)}, u32[]{:S(2)}, u32[]{:S(2)}) collective-permute-start(f32[1,8,2,16,128]{4,3,2,1,0:T(8,128)S(1)} %get-tuple-element.50), channel_id=1, source_target_pairs={{0,8},{8,0},{16,24},{24,16},{1,9},{9,1},{17,25},{25,17},{2,10},{10... | collective-permute-start | bytes 393224 | tf_op jit(solution)/shard_map/ppermute | solution.py:620

commit v5 on v4

--- a/solution.py
+++ b/solution.py
@@ -52,9 +52,10 @@
         ref[(*lead, j, pl.ds(SUB * g, SUB), slice(None))] = value
 
 
-def copy_planes(src, src_lead, src_first, dst, dst_lead, dst_first, count):
+def copy_planes(src, src_lead, src_first, dst, dst_lead, dst_first, count, scale=None):
     for i in range(count):
-        dst[(*dst_lead, dst_first + i)] = src[(*src_lead, src_first + i)]
+        plane = src[(*src_lead, src_first + i)]
+        dst[(*dst_lead, dst_first + i)] = plane if scale is None else scale * plane
 
 
 def split(values):
@@ -77,13 +78,14 @@
 def pack_kernel(kinds, *refs):
     (near, far, buffers, arrived), refs = refs[-4:], refs[:-4]
     owns, fetched = refs[-len(kinds) :], refs[: -len(kinds)]
-    sources = []
-    for ref in fetched:
-        sources += [ref] if len(ref.shape) == 3 else [ref.at[b] for b in range(ref.shape[0])]
-    copies = [pltpu.make_async_copy(ref, buffers.at[b], arrived.at[b]) for b, ref in enumerate(sources)]
-    for copy in copies:
+    copies, first = [], 0
+    for n, ref in enumerate(fetched):
+        here = first if len(ref.shape) == 3 else pl.ds(first, ref.shape[0])
+        copies.append((first, pltpu.make_async_copy(ref, buffers.at[here], arrived.at[n])))
+        first += 1 if len(ref.shape) == 3 else ref.shape[0]
+    for unused, copy in copies:
         copy.start()
-    blocks = [buffers.at[b] for b in range(len(sources))]
+    blocks = list(range(buffers.shape[0]))
     depth, width_y, width_z = buffers.shape[1:]
     chunks, groups = width_z // LANES, width_y // SUB
     parity = lax.axis_index("vox") % 2
@@ -92,9 +94,9 @@
     at = 0
     for own, widths in zip(owns, kinds):
         for b, width in enumerate(widths):
-            block = blocks.pop(0)
-            copies[0].wait()
-            copies.pop(0)
+            if copies and copies[0][0] == blocks[0]:
+                copies.pop(0)[1].wait()
+            block = buffers.at[blocks.pop(0)]
             for first in range(0, depth, together):
                 values = block[pl.ds(first, together)].reshape(together * width_y, width_z)
                 packed = exact_dot(values, order, 0)
@@ -154,7 +156,7 @@
             right[-1] = jnp.where(lane == LANES - 1, 0.0, right[-1])
             absorb = load_rows(mu, (i,), g, chunks)
             for j in range(chunks):
-                face = [0.5 * (mid[j] + other[j]) for other in (low, high, before, after, left, right)]
+                face = [mid[j] + other[j] for other in (low, high, before, after, left, right)]
                 diagonal = absorb[j] + face[0] + face[1] + face[2] + face[3] + face[4] + face[5]
                 inverse = jnp.where(inside, 1.0 / diagonal, 0.0)
                 if g == 0:
@@ -267,8 +269,8 @@
     count, depth = own.shape[:2]
     slab = lax.axis_index("vox")
     parity = slab % 2
-    copy_planes(coef_own, (0,), 0, kap, (), HALO, depth)
-    copy_planes(near, (), 0, kap, (), halo_place(parity, True, depth, HALO), HALO)
+    copy_planes(coef_own, (0,), 0, kap, (), HALO, depth, 0.5)
+    copy_planes(near, (), 0, kap, (), halo_place(parity, True, depth, HALO), HALO, 0.5)
     copy_planes(coef_own, (1,), 0, mu, (), SWEEPS, depth)
     copy_planes(near, (), HALO, mu, (), halo_place(parity, True, depth, SWEEPS), SWEEPS)
     coefficient_planes(slab, kap, mu, coef, *early_part(0, depth, parity), depth)
@@ -291,8 +293,8 @@
     slab = lax.axis_index("vox")
     parity = slab % 2
     edge = jnp.where(parity == 0, 0, depth - 2)
-    copy_planes(coef_own, (0,), edge, kap, (), edge + HALO, 2)
-    copy_planes(far, (), 0, kap, (), halo_place(parity, False, depth, HALO), HALO)
+    copy_planes(coef_own, (0,), edge, kap, (), edge + HALO, 2, 0.5)
+    copy_planes(far, (), 0, kap, (), halo_place(parity, False, depth, HALO), HALO, 0.5)
     copy_planes(coef_own, (1,), edge, mu, (), edge + SWEEPS, 2)
     copy_planes(far, (), HALO, mu, (), halo_place(parity, False, depth, SWEEPS), SWEEPS)
     coefficient_planes(slab, kap, mu, coef, *late_part(0, depth, parity), depth)
@@ -326,7 +328,7 @@
     sweep_planes(coef, one, two, *early_part(0, depth, parity), None)
 
 
-def add_sources(coef, source, bias, at, planes, moved):
+def add_sources(coef, source, bias, at, planes, moved, swept=None):
     count, unused, chunks, width_y, lanes = bias.shape
     width_z = chunks * LANES
     cells = source[pl.ds(count, 1), :].astype(jnp.int32) + moved * (width_y * width_z)
@@ -338,7 +340,11 @@
             for spread in spreads:
                 placed = placed + lax.dot_general(spread, z_hot[j], (((1,), (1,)), ((), ())), preferred_element_type=jnp.float32)
             placed = placed.reshape(planes, width_y, LANES)
-            bias[s, pl.ds(at, planes), j, pl.ds(0, width_y)] = placed * coef[6, pl.ds(at, planes), j, pl.ds(0, width_y)]
+            placed = placed * coef[6, pl.ds(at, planes), j, pl.ds(0, width_y)]
+            bias[s, pl.ds(at, planes), j] = placed
+            if swept is not None:
+                place = pl.ds(at + (HALO - SWEEPS), planes)
+                swept[s, place, j] = swept[s, place, j] + placed
 
 
 def adjoint_early_kernel(two_in, coef, source, near_source, two, one, bias):
@@ -346,17 +352,8 @@
     depth = planes - 2 * HALO
     parity = lax.axis_index("vox") % 2
     moved = SWEEPS + jnp.where(parity == 0, depth, -depth)
-    add_sources(coef, near_source, bias, halo_place(parity, True, depth, SWEEPS), SWEEPS, moved)
-    add_sources(coef, source, bias, SWEEPS, depth, SWEEPS)
-    first, count_first = early_part(0, depth, parity)
-
-    def add(n, carry):
-        at = first + n
-        for s in range(count):
-            two[s, at] = two[s, at] + bias[s, at - (HALO - SWEEPS)]
-        return carry
-
-    lax.fori_loop(0, count_first, add, 0)
+    add_sources(coef, near_source, bias, halo_place(parity, True, depth, SWEEPS), SWEEPS, moved, two)
+    add_sources(coef, source, bias, SWEEPS, depth, SWEEPS, two)
 
     def sweep(part, src, dst, t, together):
         sweep_planes(coef, src, dst, *part(t, depth, parity), bias, together)

time: 60.7 us -> 60.2 us (level)
  transfers between devices with their start and end apart: 13 -> 13, of which waited for: 5 -> 5; matrix products, arithmetic and copies ran while one was open for 0% -> 0% of each run, Pallas kernels for 32% -> 31%
where the time goes in v5:
time: 60.2 us; the launch traced here: 60 us
  Pallas kernels  26.4 us (44%)
  waiting for transfers between devices  17.1 us (28%)
  starting transfers between devices  15.7 us (26%)
  between operations  0.79 us (1%)
    pallas_call x9, Pallas kernels, call(): pl.pallas_call(kernel, out_shape=outs, in_specs=specs, out_specs=[VMEM] *...  26.4 us
    ppermute x4, waiting for transfers between devices, swap(): lax.ppermute(block, 'src', [(i, i ^ 1 << bit) for i in range(groups)])  11.8 us
    ppermute x3, starting transfers between devices, far_swap(): return lax.ppermute(block, 'vox', pairs + [(b, a) for a, b in pairs])  6.67 us
    ppermute x4, starting transfers between devices, swap(): lax.ppermute(block, 'src', [(i, i ^ 1 << bit) for i in range(groups)])  4.34 us
    ppermute x3, waiting for transfers between devices, far_swap(): return lax.ppermute(block, 'vox', pairs + [(b, a) for a, b in pairs])  4.03 us
    ppermute x3, starting transfers between devices, body(): lax.ppermute(sums[d], 'src', [(i, i ^ d) for i in range(groups)])  3.51 us
    ppermute x3, waiting for transfers between devices, near_swap(): lax.ppermute(block, 'vox', [(i, i ^ 1) for i in range(count) if i ^ 1 < c...  1.23 us
  transfers between devices with their start and end apart: 13, of which 5 were waited for; matrix products, arithmetic and copies ran while one was open for 0% of the time, Pallas kernels for 31%

profile of v5, /device:TPU:10, one launch (start us, length us, event | category | flops | bytes accessed | tf_op | source)
XLA Modules:
  0.0 60.0 jit_solution(14031997634435250292)
XLA Ops:
  0.6 2.5 %shard_map.113 = (f32[2,8,2,64,128]{4,3,2,1,0:T(8,128)S(1)}, f32[2,8,2,64,128]{4,3,2,1,0:T(8,128)S(1)}, f32[27,2,64,128]{3,2,1,0:T(8,128)S(1)}, f32[27,2,64,128]{3,2,1,0:T(8,128)S(1)}) custom-call(f32[8,64,256]{2,1,0:T(8,128)} %refs_0_.4, f32[8,64,256]{2,1,0:T(8,128)} %refs_1_.1, f32[2,8,64,256]{3,2,1,0:T(8,128)} %refs_2_.1), custom_call_target="tpu_custom_call" | custom-call | flops 1 | bytes 1 | tf_op jit(solution)/shard_map/pallas_call | solution.py:487
  3.2 0.1 collective-permute-start
  3.3 2.4 %collective-permute-start.2 = (f32[27,2,64,128]{3,2,1,0:T(8,128)S(1)}, f32[27,2,64,128]{3,2,1,0:T(8,128)S(1)}, u32[]{:S(2)}, u32[]{:S(2)}) collective-permute-start(f32[27,2,64,128]{3,2,1,0:T(8,128)S(1)} %get-tuple-element.34), channel_id=1, source_target_pairs={{1,2},{3,4},{5,6},{2,1},{4,3},{6,5},{9,10},{11,12},{13,14},{10,9},... | collective-permute-start | bytes 5308424 | tf_op jit(solution)/shard_map/ppermute | solution.py:505
  5.7 1.2 %collective-permute-done.refs_1_.refs_3_ = f32[27,2,64,128]{3,2,1,0:T(8,128)S(1)} collective-permute-done((f32[27,2,64,128]{3,2,1,0:T(8,128)S(1)}, f32[27,2,64,128]{3,2,1,0:T(8,128)S(1)}, u32[]{:S(2)}, u32[]{:S(2)}) %collective-permute-start) | collective-permute-done | bytes 1769504 | tf_op jit(solution)/shard_map/ppermute | solution.py:500
  6.9 1.9 %shard_map.114 = (f32[2,8,2,64,128]{4,3,2,1,0:T(8,128)S(1)}, f32[14,2,64,128]{3,2,1,0:T(8,128)S(1)}, f32[14,2,64,128]{3,2,1,0:T(8,128)S(1)}) custom-call(f32[2,8,64,256]{3,2,1,0:T(8,128)} %refs_0_.5, f32[27,2,64,128]{3,2,1,0:T(8,128)S(1)} %collective-permute-done.refs_1_.refs_3_), custom_call_target="tpu_custom_call" | custom-call | flops 1 | bytes 1 | tf_op jit(solution)/shard_map/pallas_call | solution.py:487
  8.8 0.2 collective-permute-start.1
  9.0 2.3 %collective-permute-start.7 = (f32[14,2,64,128]{3,2,1,0:T(8,128)S(1)}, f32[14,2,64,128]{3,2,1,0:T(8,128)S(1)}, u32[]{:S(2)}, u32[]{:S(2)}) collective-permute-start(f32[14,2,64,128]{3,2,1,0:T(8,128)S(1)} %get-tuple-element.44), channel_id=1, source_target_pairs={{1,2},{3,4},{5,6},{2,1},{4,3},{6,5},{9,10},{11,12},{13,14},{10,9},... | collective-permute-start | bytes 2752520 | tf_op jit(solution)/shard_map/ppermute | solution.py:505
  11.3 0.0 collective-permute-done.1.refs_4_.near
  11.4 1.1 %shard_map.117 = (f32[4,128]{1,0:T(4,128)S(1)}, f32[4,128]{1,0:T(4,128)S(1)}, f32[4,128]{1,0:T(4,128)S(1)}, f32[4,128]{1,0:T(4,128)S(1)}) custom-call(s32[8,128]{1,0:T(8,128)} %bitcast.13, s32[8,128]{1,0:T(8,128)} %bitcast.14, f32[8,128]{1,0:T(8,128)} %bitcast.15, f32[8,128]{1,0:T(8,128)} %bitcast.16, f32[14,2,64,128]{3,2,1,0:T(8,128)S(1)} %collective-permute-done.1.refs_4_.near), custom_call_target="tpu_custom_call" | custom-call | flops 1 | bytes 1 | tf_op jit(solution)/shard_map/pallas_call | solution.py:487
  12.5 0.5 collective-permute-start.3
  13.0 1.5 %collective-permute-start.4 = (f32[4,128]{1,0:T(4,128)S(1)}, f32[4,128]{1,0:T(4,128)S(1)}, u32[]{:S(2)}, u32[]{:S(2)}) collective-permute-start(f32[4,128]{1,0:T(4,128)S(1)} %get-tuple-element.37), channel_id=1, source_target_pairs={{0,16},{8,24},{16,0},{24,8},{1,17},{9,25},{17,1},{25,9},{2,18},{10... | collective-permute-start | bytes 6152 | tf_op jit(solution)/shard_map/ppermute | solution.py:567
  14.5 1.4 %collective-permute-start.5 = (f32[4,128]{1,0:T(4,128)S(1)}, f32[4,128]{1,0:T(4,128)S(1)}, u32[]{:S(2)}, u32[]{:S(2)}) collective-permute-start(f32[4,128]{1,0:T(4,128)S(1)} %get-tuple-element.38), channel_id=1, source_target_pairs={{0,24},{8,16},{16,8},{24,0},{1,25},{9,17},{17,9},{25,1},{2,26},{10... | collective-permute-start | bytes 6152 | tf_op jit(solution)/shard_map/ppermute | solution.py:567
  16.0 5.9 %shard_map.115 = (f32[7,20,2,72,128]{4,3,2,1,0:T(8,128)S(1)}, f32[2,22,2,64,128]{4,3,2,1,0:T(8,128)S(1)}, f32[2,22,2,64,128]{4,3,2,1,0:T(8,128)S(1)}) custom-call(s32[8]{0:T(128)S(1)} %copy-done, f32[2,8,2,64,128]{4,3,2,1,0:T(8,128)S(1)} %get-tuple-element.26.refs_1_.refs_4_, f32[2,8,2,64,128]{4,3,2,1,0:T(8,128)S(1)} %get-tuple-element.27.refs_2_, ...), custom_call_target="tpu_custom_call" | custom-call | flops 1 | bytes 1 | tf_op jit(solution)/shard_map/pallas_call | solution.py:487
  21.9 1.2 %shard_map.116.refs_11_.two_in = f32[2,22,2,64,128]{4,3,2,1,0:T(8,128)S(1)} custom-call(f32[7,20,2,72,128]{4,3,2,1,0:T(8,128)S(1)} %get-tuple-element.30.coef.refs_3_, f32[2,8,2,64,128]{4,3,2,1,0:T(8,128)S(1)} %get-tuple-element.31.own, f32[14,2,64,128]{3,2,1,0:T(8,128)S(1)} %collective-permute-done.1.refs_4_.near), custom_call_target="tpu_custom_call" | custom-call | flops 1 | bytes 1 | tf_op jit(solution)/shard_map/pallas_call | solution.py:487
  23.1 4.0 %collective-permute-done.2.refs_5_ = f32[27,2,64,128]{3,2,1,0:T(8,128)S(1)} collective-permute-done((f32[27,2,64,128]{3,2,1,0:T(8,128)S(1)}, f32[27,2,64,128]{3,2,1,0:T(8,128)S(1)}, u32[]{:S(2)}, u32[]{:S(2)}) %collective-permute-start.2) | collective-permute-done | bytes 1769504 | tf_op jit(solution)/shard_map/ppermute | solution.py:505
  27.1 0.0 collective-permute-done.3.refs_7_
  27.1 0.0 collective-permute-done.4.refs_8_
  27.1 0.0 collective-permute-done.5.refs_9_
  27.1 5.1 %shard_map.118 = (f32[2,22,2,64,128]{4,3,2,1,0:T(8,128)S(1)}, f32[2,22,2,64,128]{4,3,2,1,0:T(8,128)S(1)}, f32[7,20,2,72,128]{4,3,2,1,0:T(8,128)S(1)}, f32[2,9,2,64,128]{4,3,2,1,0:T(8,128)S(1)}, f32[3,128]{1,0:T(4,128)S(1)}) custom-call(s32[8]{0:T(128)S(1)} %copy-done, ...), custom_call_target="tpu_custom_call", output_to_operand_aliasing={{0}: (1, {}), {1}: (2, {}), {2}: (3, {})} | custom-call | flops 1 | bytes 1 | tf_op jit(solution)/shard_map/pallas_call | solution.py:487
  32.3 0.9 %collective-permute-start.6 = (f32[3,128]{1,0:T(4,128)S(1)}, f32[3,128]{1,0:T(4,128)S(1)}, u32[]{:S(2)}, u32[]{:S(2)}) collective-permute-start(f32[3,128]{1,0:T(4,128)S(1)} %get-tuple-element.40.source), channel_id=1, source_target_pairs={{0,1},{1,0},{2,3},{3,2},{4,5},{5,4},{6,7},{7,6},{8,9},{9,8},{10,11... | collective-permute-start | bytes 4616 | tf_op jit(solution)/shard_map/ppermute | solution.py:500
  33.1 1.9 %collective-permute-start.8 = (f32[3,128]{1,0:T(4,128)S(1)}, f32[3,128]{1,0:T(4,128)S(1)}, u32[]{:S(2)}, u32[]{:S(2)}) collective-permute-start(f32[3,128]{1,0:T(4,128)S(1)} %get-tuple-element.40.source), channel_id=1, source_target_pairs={{1,2},{3,4},{5,6},{2,1},{4,3},{6,5},{9,10},{11,12},{13,14},{10,9},... | collective-permute-start | bytes 4616 | tf_op jit(solution)/shard_map/ppermute | solution.py:505
  35.0 0.0 collective-permute-done.6.near_source
  35.1 3.5 %shard_map.119 = (f32[2,22,2,64,128]{4,3,2,1,0:T(8,128)S(1)}, f32[2,22,2,64,128]{4,3,2,1,0:T(8,128)S(1)}, f32[2,20,2,64,128]{4,3,2,1,0:T(8,128)S(1)}) custom-call(f32[2,22,2,64,128]{4,3,2,1,0:T(8,128)S(1)} %shard_map.116.refs_11_.two_in, f32[7,20,2,72,128]{4,3,2,1,0:T(8,128)S(1)} %get-tuple-element.39.coef, ...), custom_call_target="tpu_custom_call", output_to_operand_aliasing={{0}: (0, {})} | custom-call | flops 1 | bytes 1 | tf_op jit(solution)/shard_map/pallas_call | solution.py:487
  38.6 4.2 %shard_map.120 = (f32[2,22,2,64,128]{4,3,2,1,0:T(8,128)S(1)}, f32[2,22,2,64,128]{4,3,2,1,0:T(8,128)S(1)}, f32[2,20,2,64,128]{4,3,2,1,0:T(8,128)S(1)}, f32[2,8,2,...) custom-call(f32[2,22,2,64,128]{4,3,2,1,0:T(8,128)S(1)} %get-tuple-el, ...), custom_call_target="tpu_custom_call", output_to_operand_aliasing={{0}: (0, {}), {1}: (1, {}), {2}: (2, {})} | custom-call | flops 1 | bytes 1 | tf_op jit(solution)/shard_map/pallas_call | solution.py:487
  42.8 0.6 collective-permute-start.9
  43.4 1.5 %collective-permute-start.11 = (f32[2,8,2,16,128]{4,3,2,1,0:T(8,128)S(1)}, f32[2,8,2,16,128]{4,3,2,1,0:T(8,128)S(1)}, u32[]{:S(2)}, u32[]{:S(2)}) collective-permute-start(f32[2,8,2,16,128]{4,3,2,1,0:T(8,128)S(1)} %get-tuple-element.49), channel_id=1, source_target_pairs={{0,16},{8,24},{16,0},{24,8},{1,17},{9,25},{17,1},{25,9},{2,18},{10... | collective-permute-start | bytes 786440 | tf_op jit(solution)/shard_map/ppermute | solution.py:617
  44.9 6.8 %collective-permute-done.9 = f32[2,8,2,16,128]{4,3,2,1,0:T(8,128)S(1)} collective-permute-done((f32[2,8,2,16,128]{4,3,2,1,0:T(8,128)S(1)}, f32[2,8,2,16,128]{4,3,2,1,0:T(8,128)S(1)}, u32[]{:S(2)}, u32[]{:S(2)}) %collective-permute-start.9) | collective-permute-done | bytes 262176 | tf_op jit(solution)/shard_map/ppermute | solution.py:617
  51.7 1.6 %collective-permute-start.10 = (f32[1,8,2,16,128]{4,3,2,1,0:T(8,128)S(1)}, f32[1,8,2,16,128]{4,3,2,1,0:T(8,128)S(1)}, u32[]{:S(2)}, u32[]{:S(2)}) collective-permute-start(f32[1,8,2,16,128]{4,3,2,1,0:T(8,128)S(1)} %get-tuple-element.52), channel_id=1, source_target_pairs={{0,16},{8,24},{16,0},{24,8},{1,17},{9,25},{17,1},{25,9},{2,18},{10... | collective-permute-start | bytes 393224 | tf_op jit(solution)/shard_map/ppermute | solution.py:617
  53.4 0.6 %collective-permute-start.12 = (f32[1,8,2,16,128]{4,3,2,1,0:T(8,128)S(1)}, f32[1,8,2,16,128]{4,3,2,1,0:T(8,128)S(1)}, u32[]{:S(2)}, u32[]{:S(2)}) collective-permute-start(f32[1,8,2,16,128]{4,3,2,1,0:T(8,128)S(1)} %get-tuple-element.50), channel_id=1, source_target_pairs={{0,8},{8,0},{16,24},{24,16},{1,9},{9,1},{17,25},{25,17},{2,10},{10... | collective-permute-start | bytes 393224 | tf_op jit(solution)/shard_map/ppermute | solution.py:617
  54.0 3.6 %collective-permute-done.10 = f32[1,8,2,16,128]{4,3,2,1,0:T(8,128)S(1)} collective-permute-done((f32[1,8,2,16,128]{4,3,2,1,0:T(8,128)S(1)}, f32[1,8,2,16,128]{4,3,2,1,0:T(8,128)S(1)}, u32[]{:S(2)}, u32[]{:S(2)}) %collective-permute-start.10) | collective-permute-done | bytes 131104 | tf_op jit(solution)/shard_map/ppermute | solution.py:617
  57.7 1.4 %collective-permute-done.12 = f32[1,8,2,16,128]{4,3,2,1,0:T(8,128)S(1)} collective-permute-done((f32[1,8,2,16,128]{4,3,2,1,0:T(8,128)S(1)}, f32[1,8,2,16,128]{4,3,2,1,0:T(8,128)S(1)}, u32[]{:S(2)}, u32[]{:S(2)}) %collective-permute-start.12) | collective-permute-done | bytes 131104 | tf_op jit(solution)/shard_map/ppermute | solution.py:617
  59.0 1.0 %shard_map.121 = (f32[8,16,256]{2,1,0:T(8,128)}, f32[8,16,256]{2,1,0:T(8,128)}) custom-call(f32[8,2,16,128]{3,2,1,0:T(8,128)S(1)} %get-tuple-element.53.refs_0_, f32[8,2,16,128]{3,2,1,0:T(8,128)S(1)} %bitcast.11, f32[8,2,16,128]{3,2,1,0:T(8,128)S(1)} %get-tuple-element.51.refs_2_, f32[8,2,16,128]{3,2,1,0:T(8,128)S(1)} %bitcast.12), custom_call_target="tpu_custom_call" | custom-call | flops 1 | bytes 1 | tf_op jit(solution)/shard_map/pallas_call | solution.py:487
  (9 shorter events, 0.1 us)
Async XLA Ops:
  0.6 15.3 %copy-start = (s32[8]{0:T(128)S(1)}, s32[8]{0:T(128)}, u32[]{:S(2)}) copy-start(s32[8]{0:T(128)} %refs_0_.7) | copy-start | bytes 100
  3.2 3.8 %collective-permute-start = (f32[27,2,64,128]{3,2,1,0:T(8,128)S(1)}, f32[27,2,64,128]{3,2,1,0:T(8,128)S(1)}, u32[]{:S(2)}, u32[]{:S(2)}) collective-permute-start(f32[27,2,64,128]{3,2,1,0:T(8,128)S(1)} %get-tuple-element.28), channel_id=1, source_target_pairs={{0,1},{1,0},{2,3},{3,2},{4,5},{5,4},{6,7},{7,6},{8,9},{9,8},{10,11... | collective-permute-start | bytes 5308424 | tf_op jit(solution)/shard_map/ppermute | solution.py:500
  3.3 23.8 %collective-permute-start.2 = (f32[27,2,64,128]{3,2,1,0:T(8,128)S(1)}, f32[27,2,64,128]{3,2,1,0:T(8,128)S(1)}, u32[]{:S(2)}, u32[]{:S(2)}) collective-permute-start(f32[27,2,64,128]{3,2,1,0:T(8,128)S(1)} %get-tuple-element.34), channel_id=1, source_target_pairs={{1,2},{3,4},{5,6},{2,1},{4,3},{6,5},{9,10},{11,12},{13,14},{10,9},... | collective-permute-start | bytes 5308424 | tf_op jit(solution)/shard_map/ppermute | solution.py:505
  8.8 2.5 %collective-permute-start.1 = (f32[14,2,64,128]{3,2,1,0:T(8,128)S(1)}, f32[14,2,64,128]{3,2,1,0:T(8,128)S(1)}, u32[]{:S(2)}, u32[]{:S(2)}) collective-permute-start(f32[14,2,64,128]{3,2,1,0:T(8,128)S(1)} %get-tuple-element.29), channel_id=1, source_target_pairs={{0,1},{1,0},{2,3},{3,2},{4,5},{5,4},{6,7},{7,6},{8,9},{9,8},{10,11... | collective-permute-start | bytes 2752520 | tf_op jit(solution)/shard_map/ppermute | solution.py:500
  9.0 29.6 %collective-permute-start.7 = (f32[14,2,64,128]{3,2,1,0:T(8,128)S(1)}, f32[14,2,64,128]{3,2,1,0:T(8,128)S(1)}, u32[]{:S(2)}, u32[]{:S(2)}) collective-permute-start(f32[14,2,64,128]{3,2,1,0:T(8,128)S(1)} %get-tuple-element.44), channel_id=1, source_target_pairs={{1,2},{3,4},{5,6},{2,1},{4,3},{6,5},{9,10},{11,12},{13,14},{10,9},... | collective-permute-start | bytes 2752520 | tf_op jit(solution)/shard_map/ppermute | solution.py:505
  12.5 14.6 %collective-permute-start.3 = (f32[4,128]{1,0:T(4,128)S(1)}, f32[4,128]{1,0:T(4,128)S(1)}, u32[]{:S(2)}, u32[]{:S(2)}) collective-permute-start(f32[4,128]{1,0:T(4,128)S(1)} %get-tuple-element.36), channel_id=1, source_target_pairs={{0,8},{8,0},{16,24},{24,16},{1,9},{9,1},{17,25},{25,17},{2,10},{10... | collective-permute-start | bytes 6152 | tf_op jit(solution)/shard_map/ppermute | solution.py:567
  13.0 14.1 %collective-permute-start.4 = (f32[4,128]{1,0:T(4,128)S(1)}, f32[4,128]{1,0:T(4,128)S(1)}, u32[]{:S(2)}, u32[]{:S(2)}) collective-permute-start(f32[4,128]{1,0:T(4,128)S(1)} %get-tuple-element.37), channel_id=1, source_target_pairs={{0,16},{8,24},{16,0},{24,8},{1,17},{9,25},{17,1},{25,9},{2,18},{10... | collective-permute-start | bytes 6152 | tf_op jit(solution)/shard_map/ppermute | solution.py:567
  14.5 12.6 %collective-permute-start.5 = (f32[4,128]{1,0:T(4,128)S(1)}, f32[4,128]{1,0:T(4,128)S(1)}, u32[]{:S(2)}, u32[]{:S(2)}) collective-permute-start(f32[4,128]{1,0:T(4,128)S(1)} %get-tuple-element.38), channel_id=1, source_target_pairs={{0,24},{8,16},{16,8},{24,0},{1,25},{9,17},{17,9},{25,1},{2,26},{10... | collective-permute-start | bytes 6152 | tf_op jit(solution)/shard_map/ppermute | solution.py:567
  32.3 2.8 %collective-permute-start.6 = (f32[3,128]{1,0:T(4,128)S(1)}, f32[3,128]{1,0:T(4,128)S(1)}, u32[]{:S(2)}, u32[]{:S(2)}) collective-permute-start(f32[3,128]{1,0:T(4,128)S(1)} %get-tuple-element.40.source), channel_id=1, source_target_pairs={{0,1},{1,0},{2,3},{3,2},{4,5},{5,4},{6,7},{7,6},{8,9},{9,8},{10,11... | collective-permute-start | bytes 4616 | tf_op jit(solution)/shard_map/ppermute | solution.py:500
  33.1 5.5 %collective-permute-start.8 = (f32[3,128]{1,0:T(4,128)S(1)}, f32[3,128]{1,0:T(4,128)S(1)}, u32[]{:S(2)}, u32[]{:S(2)}) collective-permute-start(f32[3,128]{1,0:T(4,128)S(1)} %get-tuple-element.40.source), channel_id=1, source_target_pairs={{1,2},{3,4},{5,6},{2,1},{4,3},{6,5},{9,10},{11,12},{13,14},{10,9},... | collective-permute-start | bytes 4616 | tf_op jit(solution)/shard_map/ppermute | solution.py:505
  42.8 8.9 %collective-permute-start.9 = (f32[2,8,2,16,128]{4,3,2,1,0:T(8,128)S(1)}, f32[2,8,2,16,128]{4,3,2,1,0:T(8,128)S(1)}, u32[]{:S(2)}, u32[]{:S(2)}) collective-permute-start(f32[2,8,2,16,128]{4,3,2,1,0:T(8,128)S(1)} %get-tuple-element.47), channel_id=1, source_target_pairs={{0,8},{8,0},{16,24},{24,16},{1,9},{9,1},{17,25},{25,17},{2,10},{10... | collective-permute-start | bytes 786440 | tf_op jit(solution)/shard_map/ppermute | solution.py:617
  43.4 9.9 %collective-permute-start.11 = (f32[2,8,2,16,128]{4,3,2,1,0:T(8,128)S(1)}, f32[2,8,2,16,128]{4,3,2,1,0:T(8,128)S(1)}, u32[]{:S(2)}, u32[]{:S(2)}) collective-permute-start(f32[2,8,2,16,128]{4,3,2,1,0:T(8,128)S(1)} %get-tuple-element.49), channel_id=1, source_target_pairs={{0,16},{8,24},{16,0},{24,8},{1,17},{9,25},{17,1},{25,9},{2,18},{10... | collective-permute-start | bytes 786440 | tf_op jit(solution)/shard_map/ppermute | solution.py:617
  51.7 5.9 %collective-permute-start.10 = (f32[1,8,2,16,128]{4,3,2,1,0:T(8,128)S(1)}, f32[1,8,2,16,128]{4,3,2,1,0:T(8,128)S(1)}, u32[]{:S(2)}, u32[]{:S(2)}) collective-permute-start(f32[1,8,2,16,128]{4,3,2,1,0:T(8,128)S(1)} %get-tuple-element.52), channel_id=1, source_target_pairs={{0,16},{8,24},{16,0},{24,8},{1,17},{9,25},{17,1},{25,9},{2,18},{10... | collective-permute-start | bytes 393224 | tf_op jit(solution)/shard_map/ppermute | solution.py:617
  53.4 5.7 %collective-permute-start.12 = (f32[1,8,2,16,128]{4,3,2,1,0:T(8,128)S(1)}, f32[1,8,2,16,128]{4,3,2,1,0:T(8,128)S(1)}, u32[]{:S(2)}, u32[]{:S(2)}) collective-permute-start(f32[1,8,2,16,128]{4,3,2,1,0:T(8,128)S(1)} %get-tuple-element.50), channel_id=1, source_target_pairs={{0,8},{8,0},{16,24},{24,16},{1,9},{9,1},{17,25},{25,17},{2,10},{10... | collective-permute-start | bytes 393224 | tf_op jit(solution)/shard_map/ppermute | solution.py:617

commit v6 on v5

--- a/solution.py
+++ b/solution.py
@@ -76,7 +76,7 @@
 
 
 def pack_kernel(kinds, *refs):
-    (near, far, buffers, arrived), refs = refs[-4:], refs[:-4]
+    (far, buffers, arrived), refs = refs[-3:], refs[:-3]
     owns, fetched = refs[-len(kinds) :], refs[: -len(kinds)]
     copies, first = [], 0
     for n, ref in enumerate(fetched):
@@ -112,8 +112,12 @@
                                     own[b, first + i, j, pl.ds(row, 1), :] = part[k : k + 1]
             low, high = 0, depth - width
             copy_planes(own, (b,), jnp.where(parity == 0, low, high), far, (), at, width)
-            copy_planes(own, (b,), jnp.where(parity == 0, high, low), near, (), at, width)
             at += width
+
+
+def near_planes(near, lead, width, dst, dst_lead, dst_first, parity, scale=None):
+    first = jnp.where(parity == 0, 0, near.shape[1] - width)
+    copy_planes(near, lead, first, dst, dst_lead, dst_first, width, scale)
 
 
 def early_part(t, depth, parity):
@@ -265,18 +269,18 @@
     lax.fori_loop(0, SWEEPS // 2, step, 0)
 
 
-def early_kernel(positions, coef_own, own, near, coef, one, two, kap, mu, spots):
+def early_kernel(positions, coef_own, own, near_coef, near, coef, one, two, kap, mu, spots):
     count, depth = own.shape[:2]
     slab = lax.axis_index("vox")
     parity = slab % 2
     copy_planes(coef_own, (0,), 0, kap, (), HALO, depth, 0.5)
-    copy_planes(near, (), 0, kap, (), halo_place(parity, True, depth, HALO), HALO, 0.5)
+    near_planes(near_coef, (0,), HALO, kap, (), halo_place(parity, True, depth, HALO), parity, 0.5)
     copy_planes(coef_own, (1,), 0, mu, (), SWEEPS, depth)
-    copy_planes(near, (), HALO, mu, (), halo_place(parity, True, depth, SWEEPS), SWEEPS)
+    near_planes(near_coef, (1,), SWEEPS, mu, (), halo_place(parity, True, depth, SWEEPS), parity)
     coefficient_planes(slab, kap, mu, coef, *early_part(0, depth, parity), depth)
     for s in range(count):
         copy_planes(own, (s,), 0, one, (s,), HALO, depth)
-        copy_planes(near, (), HALO + SWEEPS + s * HALO, one, (s,), halo_place(parity, True, depth, HALO), HALO)
+        near_planes(near, (s,), HALO, one, (s,), halo_place(parity, True, depth, HALO), parity)
     find_sources(positions, spots, count, depth, *own.shape[2:4])
 
     def sweep(part, src, dst, t, together):
@@ -324,7 +328,7 @@
     parity = lax.axis_index("vox") % 2
     for s in range(count):
         copy_planes(own, (s,), 0, one, (s,), HALO, depth)
-        copy_planes(near, (), s * HALO, one, (s,), halo_place(parity, True, depth, HALO), HALO)
+        near_planes(near, (s,), HALO, one, (s,), halo_place(parity, True, depth, HALO), parity)
     sweep_planes(coef, one, two, *early_part(0, depth, parity), None)
 
 
@@ -525,10 +529,11 @@
 
     def pack(kinds, *blocks, after=()):
         rim = held(sum(sum(widths) for widths in kinds), *plane)
-        outs = [held(len(widths), depth, *plane) for widths in kinds] + [rim, rim]
+        outs = [held(len(widths), depth, *plane) for widths in kinds] + [rim]
         blocks_held = sum(len(widths) for widths in kinds)
         scratch = [held(blocks_held, depth, width_y, width_z), pltpu.SemaphoreType.DMA((blocks_held,))]
-        return call(functools.partial(pack_kernel, kinds), outs, scratch, 6, fetched=blocks, after=after)
+        *owns, far = call(functools.partial(pack_kernel, kinds), outs, scratch, 6, fetched=blocks, after=after)
+        return *owns, *[near_swap(own, slabs) for own in owns], far_swap(far, slabs)
 
     def sides(near, far):
         return near_swap(near, slabs), far_swap(far, slabs)
@@ -540,10 +545,8 @@
     coef_work = [held(planes, *plane), held(planes - 2, *plane)]
 
     field_rims = (HALO,) * count
-    coef_own, fwd_own, near, far = pack([(HALO, SWEEPS), field_rims], kappa, mua, prior_forward_fields)
-    near, far = sides(near, far)
-    adj_own, adj_near, adj_far = pack([field_rims], prior_adjoint_fields, after=[near])
-    adj_near, adj_far = sides(adj_near, adj_far)
+    coef_own, fwd_own, coef_near, near, far = pack([(HALO, SWEEPS), field_rims], kappa, mua, prior_forward_fields)
+    adj_own, adj_near, adj_far = pack([field_rims], prior_adjoint_fields, after=[coef_near, near])
     coef, one, two = call(
         early_kernel,
         [coef_held, field, field],
@@ -551,6 +554,7 @@
         6,
         coef_own,
         fwd_own,
+        coef_near,
         near,
         positions=source_position,
         after=[adj_near],

time: 60.2 us -> 60.2 us (level)
    ppermute x3 -> x4, waiting for transfers between devices: 1.23 us -> 1.79 us  [near_swap(): lax.ppermute(block, 'vox', [(i, i ^ 1) for i in range(count) if i ^ 1 < c...]
    ppermute x3 -> x4, starting transfers between devices: 1.15 us -> 1.22 us  [near_swap(): lax.ppermute(block, 'vox', [(i, i ^ 1) for i in range(count) if i ^ 1 < c...]
  transfers between devices with their start and end apart: 13 -> 14, of which waited for: 5 -> 7; matrix products, arithmetic and copies ran while one was open for 0% -> 0% of each run, Pallas kernels for 31% -> 31%
where the time goes in v6:
time: 60.2 us; the launch traced here: 59.9 us
  Pallas kernels  26.2 us (44%)
  waiting for transfers between devices  17.5 us (29%)
  starting transfers between devices  15.3 us (25%)
  between operations  0.78 us (1%)
    pallas_call x9, Pallas kernels, call(): pl.pallas_call(kernel, out_shape=outs, in_specs=specs, out_specs=[VMEM] *...  26.2 us
    ppermute x4, waiting for transfers between devices, swap(): lax.ppermute(block, 'src', [(i, i ^ 1 << bit) for i in range(groups)])  11.8 us
    ppermute x3, starting transfers between devices, far_swap(): return lax.ppermute(block, 'vox', pairs + [(b, a) for a, b in pairs])  6.27 us
    ppermute x4, starting transfers between devices, swap(): lax.ppermute(block, 'src', [(i, i ^ 1 << bit) for i in range(groups)])  4.34 us
    ppermute x3, waiting for transfers between devices, far_swap(): return lax.ppermute(block, 'vox', pairs + [(b, a) for a, b in pairs])  3.93 us
    ppermute x3, starting transfers between devices, body(): lax.ppermute(sums[d], 'src', [(i, i ^ d) for i in range(groups)])  3.51 us
    ppermute x4, waiting for transfers between devices, near_swap(): lax.ppermute(block, 'vox', [(i, i ^ 1) for i in range(count) if i ^ 1 < c...  1.79 us
    ppermute x4, starting transfers between devices, near_swap(): lax.ppermute(block, 'vox', [(i, i ^ 1) for i in range(count) if i ^ 1 < c...  1.22 us
  transfers between devices with their start and end apart: 14, of which 7 were waited for; matrix products, arithmetic and copies ran while one was open for 0% of the time, Pallas kernels for 31%

profile of v6, /device:TPU:10, one launch (start us, length us, event | category | flops | bytes accessed | tf_op | source)
XLA Modules:
  0.0 59.9 jit_solution(4886695336172200687)
XLA Ops:
  0.6 2.4 %shard_map.113 = (f32[2,8,2,64,128]{4,3,2,1,0:T(8,128)S(1)}, f32[2,8,2,64,128]{4,3,2,1,0:T(8,128)S(1)}, f32[27,2,64,128]{3,2,1,0:T(8,128)S(1)}) custom-call(f32[8,64,256]{2,1,0:T(8,128)} %refs_0_.4, f32[8,64,256]{2,1,0:T(8,128)} %refs_1_.1, f32[2,8,64,256]{3,2,1,0:T(8,128)} %refs_2_.1), custom_call_target="tpu_custom_call" | custom-call | flops 1 | bytes 1 | tf_op jit(solution)/shard_map/pallas_call | solution.py:491
  3.0 0.1 collective-permute-start.1
  3.1 0.5 collective-permute-start
  3.6 2.0 %collective-permute-start.3 = (f32[27,2,64,128]{3,2,1,0:T(8,128)S(1)}, f32[27,2,64,128]{3,2,1,0:T(8,128)S(1)}, u32[]{:S(2)}, u32[]{:S(2)}) collective-permute-start(f32[27,2,64,128]{3,2,1,0:T(8,128)S(1)} %get-tuple-element.30), channel_id=1, source_target_pairs={{1,2},{3,4},{5,6},{2,1},{4,3},{6,5},{9,10},{11,12},{13,14},{10,9},... | collective-permute-start | bytes 5308424 | tf_op jit(solution)/shard_map/ppermute | solution.py:509
  5.7 0.1 collective-permute-done.1.refs_2_.refs_4_
  5.8 1.5 %collective-permute-done.refs_1_.refs_3_ = f32[2,8,2,64,128]{4,3,2,1,0:T(8,128)S(1)} collective-permute-done((f32[2,8,2,64,128]{4,3,2,1,0:T(8,128)S(1)}, f32[2,8,2,64,128]{4,3,2,1,0:T(8,128)S(1)}, u32[]{:S(2)}, u32[]{:S(2)}) %collective-permute-start) | collective-permute-done | bytes 1048608 | tf_op jit(solution)/shard_map/ppermute | solution.py:504
  7.3 1.8 %shard_map.114 = (f32[2,8,2,64,128]{4,3,2,1,0:T(8,128)S(1)}, f32[14,2,64,128]{3,2,1,0:T(8,128)S(1)}) custom-call(f32[2,8,64,256]{3,2,1,0:T(8,128)} %refs_0_.5, f32[2,8,2,64,128]{4,3,2,1,0:T(8,128)S(1)} %collective-permute-done.refs_1_.refs_3_, f32[2,8,2,64,128]{4,3,2,1,0:T(8,128)S(1)} %collective-permute-done.1.refs_2_.refs_4_), custom_call_target="tpu_custom_call" | custom-call | flops 1 | bytes 1 | tf_op jit(solution)/shard_map/pallas_call | solution.py:491
  9.1 0.2 collective-permute-start.2
  9.3 2.3 %collective-permute-start.8 = (f32[14,2,64,128]{3,2,1,0:T(8,128)S(1)}, f32[14,2,64,128]{3,2,1,0:T(8,128)S(1)}, u32[]{:S(2)}, u32[]{:S(2)}) collective-permute-start(f32[14,2,64,128]{3,2,1,0:T(8,128)S(1)} %get-tuple-element.40), channel_id=1, source_target_pairs={{1,2},{3,4},{5,6},{2,1},{4,3},{6,5},{9,10},{11,12},{13,14},{10,9},... | collective-permute-start | bytes 2752520 | tf_op jit(solution)/shard_map/ppermute | solution.py:509
  11.6 0.2 collective-permute-done.2.refs_5_.near.refs_4_
  11.8 1.1 %shard_map.117 = (f32[4,128]{1,0:T(4,128)S(1)}, f32[4,128]{1,0:T(4,128)S(1)}, f32[4,128]{1,0:T(4,128)S(1)}, f32[4,128]{1,0:T(4,128)S(1)}) custom-call(s32[8,128]{1,0:T(8,128)} %bitcast.13, s32[8,128]{1,0:T(8,128)} %bitcast.14, f32[8,128]{1,0:T(8,128)} %bitcast.15, f32[8,128]{1,0:T(8,128)} %bitcast.16, ...), custom_call_target="tpu_custom_call" | custom-call | flops 1 | bytes 1 | tf_op jit(solution)/shard_map/pallas_call | solution.py:491
  12.9 0.6 collective-permute-start.4
  13.5 1.5 %collective-permute-start.5 = (f32[4,128]{1,0:T(4,128)S(1)}, f32[4,128]{1,0:T(4,128)S(1)}, u32[]{:S(2)}, u32[]{:S(2)}) collective-permute-start(f32[4,128]{1,0:T(4,128)S(1)} %get-tuple-element.33), channel_id=1, source_target_pairs={{0,16},{8,24},{16,0},{24,8},{1,17},{9,25},{17,1},{25,9},{2,18},{10... | collective-permute-start | bytes 6152 | tf_op jit(solution)/shard_map/ppermute | solution.py:571
  15.0 1.4 %collective-permute-start.6 = (f32[4,128]{1,0:T(4,128)S(1)}, f32[4,128]{1,0:T(4,128)S(1)}, u32[]{:S(2)}, u32[]{:S(2)}) collective-permute-start(f32[4,128]{1,0:T(4,128)S(1)} %get-tuple-element.34), channel_id=1, source_target_pairs={{0,24},{8,16},{16,8},{24,0},{1,25},{9,17},{17,9},{25,1},{2,26},{10... | collective-permute-start | bytes 6152 | tf_op jit(solution)/shard_map/ppermute | solution.py:571
  16.4 5.9 %shard_map.115 = (f32[7,20,2,72,128]{4,3,2,1,0:T(8,128)S(1)}, f32[2,22,2,64,128]{4,3,2,1,0:T(8,128)S(1)}, f32[2,22,2,64,128]{4,3,2,1,0:T(8,128)S(1)}) custom-call(s32[8]{0:T(128)S(1)} %copy-done, f32[2,8,2,64,128]{4,3,2,1,0:T(8,128)S(1)} %get-tuple-element.24.refs_1_.refs_4_, f32[2,8,2,64,128]{4,3,2,1,0:T(8,128)S(1)} %get-tuple-element.25.refs_2_, ...), custom_call_target="tpu_custom_call" | custom-call | flops 1 | bytes 1 | tf_op jit(solution)/shard_map/pallas_call | solution.py:491
  22.3 1.2 %shard_map.116.refs_11_.two_in = f32[2,22,2,64,128]{4,3,2,1,0:T(8,128)S(1)} custom-call(f32[7,20,2,72,128]{4,3,2,1,0:T(8,128)S(1)} %get-tuple-element.27.coef.refs_3_, f32[2,8,2,64,128]{4,3,2,1,0:T(8,128)S(1)} %get-tuple-element.26.own, f32[2,8,2,64,128]{4,3,2,1,0:T(8,128)S(1)} %collective-permute-done.2.refs_5_.near.refs_4_), custom_call_target="tpu_custom_call" | custom-call | flops 1 | bytes 1 | tf_op jit(solution)/shard_map/pallas_call | solution.py:491
  23.5 3.9 %collective-permute-done.3.refs_5_ = f32[27,2,64,128]{3,2,1,0:T(8,128)S(1)} collective-permute-done((f32[27,2,64,128]{3,2,1,0:T(8,128)S(1)}, f32[27,2,64,128]{3,2,1,0:T(8,128)S(1)}, u32[]{:S(2)}, u32[]{:S(2)}) %collective-permute-start.3) | collective-permute-done | bytes 1769504 | tf_op jit(solution)/shard_map/ppermute | solution.py:509
  27.4 0.0 collective-permute-done.4.refs_7_
  27.5 5.2 %shard_map.118 = (f32[2,22,2,64,128]{4,3,2,1,0:T(8,128)S(1)}, f32[2,22,2,64,128]{4,3,2,1,0:T(8,128)S(1)}, f32[7,20,2,72,128]{4,3,2,1,0:T(8,128)S(1)}, f32[2,9,2,64,128]{4,3,2,1,0:T(8,128)S(1)}, f32[3,128]{1,0:T(4,128)S(1)}) custom-call(s32[8]{0:T(128)S(1)} %copy-done, ...), custom_call_target="tpu_custom_call", output_to_operand_aliasing={{0}: (1, {}), {1}: (2, {}), {2}: (3, {})} | custom-call | flops 1 | bytes 1 | tf_op jit(solution)/shard_map/pallas_call | solution.py:491
  32.6 0.4 collective-permute-start.7
  33.1 1.9 %collective-permute-start.9 = (f32[3,128]{1,0:T(4,128)S(1)}, f32[3,128]{1,0:T(4,128)S(1)}, u32[]{:S(2)}, u32[]{:S(2)}) collective-permute-start(f32[3,128]{1,0:T(4,128)S(1)} %get-tuple-element.36.source), channel_id=1, source_target_pairs={{1,2},{3,4},{5,6},{2,1},{4,3},{6,5},{9,10},{11,12},{13,14},{10,9},... | collective-permute-start | bytes 4616 | tf_op jit(solution)/shard_map/ppermute | solution.py:509
  35.0 3.5 %shard_map.119 = (f32[2,22,2,64,128]{4,3,2,1,0:T(8,128)S(1)}, f32[2,22,2,64,128]{4,3,2,1,0:T(8,128)S(1)}, f32[2,20,2,64,128]{4,3,2,1,0:T(8,128)S(1)}) custom-call(f32[2,22,2,64,128]{4,3,2,1,0:T(8,128)S(1)} %shard_map.116.refs_11_.two_in, f32[7,20,2,72,128]{4,3,2,1,0:T(8,128)S(1)} %get-tuple-element.35.coef, ...), custom_call_target="tpu_custom_call", output_to_operand_aliasing={{0}: (0, {})} | custom-call | flops 1 | bytes 1 | tf_op jit(solution)/shard_map/pallas_call | solution.py:491
  38.5 0.0 collective-permute-done.9.far_source
  38.5 4.2 %shard_map.120 = (f32[2,22,2,64,128]{4,3,2,1,0:T(8,128)S(1)}, f32[2,22,2,64,128]{4,3,2,1,0:T(8,128)S(1)}, f32[2,20,2,64,128]{4,3,2,1,0:T(8,128)S(1)}, f32[2,8,2,...) custom-call(f32[2,22,2,64,128]{4,3,2,1,0:T(8,128)S(1)} %get-tuple-el, ...), custom_call_target="tpu_custom_call", output_to_operand_aliasing={{0}: (0, {}), {1}: (1, {}), {2}: (2, {})} | custom-call | flops 1 | bytes 1 | tf_op jit(solution)/shard_map/pallas_call | solution.py:491
  42.7 0.6 %collective-permute-start.10 = (f32[2,8,2,16,128]{4,3,2,1,0:T(8,128)S(1)}, f32[2,8,2,16,128]{4,3,2,1,0:T(8,128)S(1)}, u32[]{:S(2)}, u32[]{:S(2)}) collective-permute-start(f32[2,8,2,16,128]{4,3,2,1,0:T(8,128)S(1)} %get-tuple-element.43), channel_id=1, source_target_pairs={{0,8},{8,0},{16,24},{24,16},{1,9},{9,1},{17,25},{25,17},{2,10},{10... | collective-permute-start | bytes 786440 | tf_op jit(solution)/shard_map/ppermute | solution.py:621
  43.3 1.5 %collective-permute-start.12 = (f32[2,8,2,16,128]{4,3,2,1,0:T(8,128)S(1)}, f32[2,8,2,16,128]{4,3,2,1,0:T(8,128)S(1)}, u32[]{:S(2)}, u32[]{:S(2)}) collective-permute-start(f32[2,8,2,16,128]{4,3,2,1,0:T(8,128)S(1)} %get-tuple-element.45), channel_id=1, source_target_pairs={{0,16},{8,24},{16,0},{24,8},{1,17},{9,25},{17,1},{25,9},{2,18},{10... | collective-permute-start | bytes 786440 | tf_op jit(solution)/shard_map/ppermute | solution.py:621
  44.8 6.8 %collective-permute-done.10 = f32[2,8,2,16,128]{4,3,2,1,0:T(8,128)S(1)} collective-permute-done((f32[2,8,2,16,128]{4,3,2,1,0:T(8,128)S(1)}, f32[2,8,2,16,128]{4,3,2,1,0:T(8,128)S(1)}, u32[]{:S(2)}, u32[]{:S(2)}) %collective-permute-start.10) | collective-permute-done | bytes 262176 | tf_op jit(solution)/shard_map/ppermute | solution.py:621
  51.7 1.6 %collective-permute-start.11 = (f32[1,8,2,16,128]{4,3,2,1,0:T(8,128)S(1)}, f32[1,8,2,16,128]{4,3,2,1,0:T(8,128)S(1)}, u32[]{:S(2)}, u32[]{:S(2)}) collective-permute-start(f32[1,8,2,16,128]{4,3,2,1,0:T(8,128)S(1)} %get-tuple-element.48), channel_id=1, source_target_pairs={{0,16},{8,24},{16,0},{24,8},{1,17},{9,25},{17,1},{25,9},{2,18},{10... | collective-permute-start | bytes 393224 | tf_op jit(solution)/shard_map/ppermute | solution.py:621
  53.3 0.6 %collective-permute-start.13 = (f32[1,8,2,16,128]{4,3,2,1,0:T(8,128)S(1)}, f32[1,8,2,16,128]{4,3,2,1,0:T(8,128)S(1)}, u32[]{:S(2)}, u32[]{:S(2)}) collective-permute-start(f32[1,8,2,16,128]{4,3,2,1,0:T(8,128)S(1)} %get-tuple-element.46), channel_id=1, source_target_pairs={{0,8},{8,0},{16,24},{24,16},{1,9},{9,1},{17,25},{25,17},{2,10},{10... | collective-permute-start | bytes 393224 | tf_op jit(solution)/shard_map/ppermute | solution.py:621
  54.0 3.6 %collective-permute-done.11 = f32[1,8,2,16,128]{4,3,2,1,0:T(8,128)S(1)} collective-permute-done((f32[1,8,2,16,128]{4,3,2,1,0:T(8,128)S(1)}, f32[1,8,2,16,128]{4,3,2,1,0:T(8,128)S(1)}, u32[]{:S(2)}, u32[]{:S(2)}) %collective-permute-start.11) | collective-permute-done | bytes 131104 | tf_op jit(solution)/shard_map/ppermute | solution.py:621
  57.6 1.4 %collective-permute-done.13 = f32[1,8,2,16,128]{4,3,2,1,0:T(8,128)S(1)} collective-permute-done((f32[1,8,2,16,128]{4,3,2,1,0:T(8,128)S(1)}, f32[1,8,2,16,128]{4,3,2,1,0:T(8,128)S(1)}, u32[]{:S(2)}, u32[]{:S(2)}) %collective-permute-start.13) | collective-permute-done | bytes 131104 | tf_op jit(solution)/shard_map/ppermute | solution.py:621
  59.0 1.0 %shard_map.121 = (f32[8,16,256]{2,1,0:T(8,128)}, f32[8,16,256]{2,1,0:T(8,128)}) custom-call(f32[8,2,16,128]{3,2,1,0:T(8,128)S(1)} %get-tuple-element.49.refs_0_, f32[8,2,16,128]{3,2,1,0:T(8,128)S(1)} %bitcast.11, f32[8,2,16,128]{3,2,1,0:T(8,128)S(1)} %get-tuple-element.47.refs_2_, f32[8,2,16,128]{3,2,1,0:T(8,128)S(1)} %bitcast.12), custom_call_target="tpu_custom_call" | custom-call | flops 1 | bytes 1 | tf_op jit(solution)/shard_map/pallas_call | solution.py:491
  (11 shorter events, 0.1 us)
Async XLA Ops:
  0.6 15.8 %copy-start = (s32[8]{0:T(128)S(1)}, s32[8]{0:T(128)}, u32[]{:S(2)}) copy-start(s32[8]{0:T(128)} %refs_0_.7) | copy-start | bytes 100
  3.0 2.7 %collective-permute-start.1 = (f32[2,8,2,64,128]{4,3,2,1,0:T(8,128)S(1)}, f32[2,8,2,64,128]{4,3,2,1,0:T(8,128)S(1)}, u32[]{:S(2)}, u32[]{:S(2)}) collective-permute-start(f32[2,8,2,64,128]{4,3,2,1,0:T(8,128)S(1)} %get-tuple-element.25.refs_2_), channel_id=1, source_target_pairs={{0,1},{1,0},{2,3},{3,2},{4,5},{5,4},{6,7},{7,6},{8,9},{9,8},{10,11... | collective-permute-start | bytes 3145736 | tf_op jit(solution)/shard_map/ppermute | solution.py:504
  3.1 4.1 %collective-permute-start = (f32[2,8,2,64,128]{4,3,2,1,0:T(8,128)S(1)}, f32[2,8,2,64,128]{4,3,2,1,0:T(8,128)S(1)}, u32[]{:S(2)}, u32[]{:S(2)}) collective-permute-start(f32[2,8,2,64,128]{4,3,2,1,0:T(8,128)S(1)} %get-tuple-element.24.refs_1_.refs_4_), channel_id=1, source_target_pairs={{0,1},{1,0},{2,3},{3,2},{4,5},{5,4},{6,7},{7,6},{8,9},{9,8},{10,11... | collective-permute-start | bytes 3145736 | tf_op jit(solution)/shard_map/ppermute | solution.py:504
  3.6 23.8 %collective-permute-start.3 = (f32[27,2,64,128]{3,2,1,0:T(8,128)S(1)}, f32[27,2,64,128]{3,2,1,0:T(8,128)S(1)}, u32[]{:S(2)}, u32[]{:S(2)}) collective-permute-start(f32[27,2,64,128]{3,2,1,0:T(8,128)S(1)} %get-tuple-element.30), channel_id=1, source_target_pairs={{1,2},{3,4},{5,6},{2,1},{4,3},{6,5},{9,10},{11,12},{13,14},{10,9},... | collective-permute-start | bytes 5308424 | tf_op jit(solution)/shard_map/ppermute | solution.py:509
  9.1 2.7 %collective-permute-start.2 = (f32[2,8,2,64,128]{4,3,2,1,0:T(8,128)S(1)}, f32[2,8,2,64,128]{4,3,2,1,0:T(8,128)S(1)}, u32[]{:S(2)}, u32[]{:S(2)}) collective-permute-start(f32[2,8,2,64,128]{4,3,2,1,0:T(8,128)S(1)} %get-tuple-element.26.own), channel_id=1, source_target_pairs={{0,1},{1,0},{2,3},{3,2},{4,5},{5,4},{6,7},{7,6},{8,9},{9,8},{10,11... | collective-permute-start | bytes 3145736 | tf_op jit(solution)/shard_map/ppermute | solution.py:504
  9.3 29.2 %collective-permute-start.8 = (f32[14,2,64,128]{3,2,1,0:T(8,128)S(1)}, f32[14,2,64,128]{3,2,1,0:T(8,128)S(1)}, u32[]{:S(2)}, u32[]{:S(2)}) collective-permute-start(f32[14,2,64,128]{3,2,1,0:T(8,128)S(1)} %get-tuple-element.40), channel_id=1, source_target_pairs={{1,2},{3,4},{5,6},{2,1},{4,3},{6,5},{9,10},{11,12},{13,14},{10,9},... | collective-permute-start | bytes 2752520 | tf_op jit(solution)/shard_map/ppermute | solution.py:509
  12.9 14.5 %collective-permute-start.4 = (f32[4,128]{1,0:T(4,128)S(1)}, f32[4,128]{1,0:T(4,128)S(1)}, u32[]{:S(2)}, u32[]{:S(2)}) collective-permute-start(f32[4,128]{1,0:T(4,128)S(1)} %get-tuple-element.32), channel_id=1, source_target_pairs={{0,8},{8,0},{16,24},{24,16},{1,9},{9,1},{17,25},{25,17},{2,10},{10... | collective-permute-start | bytes 6152 | tf_op jit(solution)/shard_map/ppermute | solution.py:571
  13.5 14.0 %collective-permute-start.5 = (f32[4,128]{1,0:T(4,128)S(1)}, f32[4,128]{1,0:T(4,128)S(1)}, u32[]{:S(2)}, u32[]{:S(2)}) collective-permute-start(f32[4,128]{1,0:T(4,128)S(1)} %get-tuple-element.33), channel_id=1, source_target_pairs={{0,16},{8,24},{16,0},{24,8},{1,17},{9,25},{17,1},{25,9},{2,18},{10... | collective-permute-start | bytes 6152 | tf_op jit(solution)/shard_map/ppermute | solution.py:571
  15.0 12.5 %collective-permute-start.6 = (f32[4,128]{1,0:T(4,128)S(1)}, f32[4,128]{1,0:T(4,128)S(1)}, u32[]{:S(2)}, u32[]{:S(2)}) collective-permute-start(f32[4,128]{1,0:T(4,128)S(1)} %get-tuple-element.34), channel_id=1, source_target_pairs={{0,24},{8,16},{16,8},{24,0},{1,25},{9,17},{17,9},{25,1},{2,26},{10... | collective-permute-start | bytes 6152 | tf_op jit(solution)/shard_map/ppermute | solution.py:571
  32.6 2.4 %collective-permute-start.7 = (f32[3,128]{1,0:T(4,128)S(1)}, f32[3,128]{1,0:T(4,128)S(1)}, u32[]{:S(2)}, u32[]{:S(2)}) collective-permute-start(f32[3,128]{1,0:T(4,128)S(1)} %get-tuple-element.36.source), channel_id=1, source_target_pairs={{0,1},{1,0},{2,3},{3,2},{4,5},{5,4},{6,7},{7,6},{8,9},{9,8},{10,11... | collective-permute-start | bytes 4616 | tf_op jit(solution)/shard_map/ppermute | solution.py:504
  33.1 5.5 %collective-permute-start.9 = (f32[3,128]{1,0:T(4,128)S(1)}, f32[3,128]{1,0:T(4,128)S(1)}, u32[]{:S(2)}, u32[]{:S(2)}) collective-permute-start(f32[3,128]{1,0:T(4,128)S(1)} %get-tuple-element.36.source), channel_id=1, source_target_pairs={{1,2},{3,4},{5,6},{2,1},{4,3},{6,5},{9,10},{11,12},{13,14},{10,9},... | collective-permute-start | bytes 4616 | tf_op jit(solution)/shard_map/ppermute | solution.py:509
  42.7 8.9 %collective-permute-start.10 = (f32[2,8,2,16,128]{4,3,2,1,0:T(8,128)S(1)}, f32[2,8,2,16,128]{4,3,2,1,0:T(8,128)S(1)}, u32[]{:S(2)}, u32[]{:S(2)}) collective-permute-start(f32[2,8,2,16,128]{4,3,2,1,0:T(8,128)S(1)} %get-tuple-element.43), channel_id=1, source_target_pairs={{0,8},{8,0},{16,24},{24,16},{1,9},{9,1},{17,25},{25,17},{2,10},{10... | collective-permute-start | bytes 786440 | tf_op jit(solution)/shard_map/ppermute | solution.py:621
  43.3 10.0 %collective-permute-start.12 = (f32[2,8,2,16,128]{4,3,2,1,0:T(8,128)S(1)}, f32[2,8,2,16,128]{4,3,2,1,0:T(8,128)S(1)}, u32[]{:S(2)}, u32[]{:S(2)}) collective-permute-start(f32[2,8,2,16,128]{4,3,2,1,0:T(8,128)S(1)} %get-tuple-element.45), channel_id=1, source_target_pairs={{0,16},{8,24},{16,0},{24,8},{1,17},{9,25},{17,1},{25,9},{2,18},{10... | collective-permute-start | bytes 786440 | tf_op jit(solution)/shard_map/ppermute | solution.py:621
  51.7 5.9 %collective-permute-start.11 = (f32[1,8,2,16,128]{4,3,2,1,0:T(8,128)S(1)}, f32[1,8,2,16,128]{4,3,2,1,0:T(8,128)S(1)}, u32[]{:S(2)}, u32[]{:S(2)}) collective-permute-start(f32[1,8,2,16,128]{4,3,2,1,0:T(8,128)S(1)} %get-tuple-element.48), channel_id=1, source_target_pairs={{0,16},{8,24},{16,0},{24,8},{1,17},{9,25},{17,1},{25,9},{2,18},{10... | collective-permute-start | bytes 393224 | tf_op jit(solution)/shard_map/ppermute | solution.py:621
  53.3 5.6 %collective-permute-start.13 = (f32[1,8,2,16,128]{4,3,2,1,0:T(8,128)S(1)}, f32[1,8,2,16,128]{4,3,2,1,0:T(8,128)S(1)}, u32[]{:S(2)}, u32[]{:S(2)}) collective-permute-start(f32[1,8,2,16,128]{4,3,2,1,0:T(8,128)S(1)} %get-tuple-element.46), channel_id=1, source_target_pairs={{0,8},{8,0},{16,24},{24,16},{1,9},{9,1},{17,25},{25,17},{2,10},{10... | collective-permute-start | bytes 393224 | tf_op jit(solution)/shard_map/ppermute | solution.py:621
